TPU v7x, 32 devices: a whole 2x2x4 slice. The times are simulated.
32 devices in a mesh: gx: 4 (over z), gy: 4 (over y, x), gz: 2 (over core).
Axes of the slice: x: 2, y: 2, z: 4, core: 2. Of those that a mesh axis runs over, the one named last changes fastest.
Arguments:
- e_field: float32 [3, 64, 32, 1024], P(None, 'gx', 'gz', 'gy'), may hold values from -6 to 6
- h_field: float32 [3, 64, 32, 1024], P(None, 'gx', 'gz', 'gy'), may hold values from -6 to 6
- polar: float32 [3, 64, 32, 1024], P(None, 'gx', 'gz', 'gy'), may hold values from -4 to 4
- permittivity: float32 [64, 32, 1024], P('gx', 'gz', 'gy'), may hold values from 1 to 4
- resonance: float32 [64, 32, 1024], P('gx', 'gz', 'gy'), may hold values from 0.3 to 1.2
- dispersive: int32 [64, 32, 8], P('gx', 'gz', 'gy'), may hold values 0 or 1
Outputs:
- e_final: float32 [3, 64, 32, 1024], P(None, 'gx', 'gz', 'gy')
- h_final: float32 [3, 64, 32, 1024], P(None, 'gx', 'gz', 'gy')
All inputs are finite; a program needn't handle non-finite values. No bound on the sum of `dispersive` on one device may be relied on, other than what follows from the above.
Results may differ from a plain program's by a relative error of at most 0.00002.
Values sent between devices are 32-bit elements; how exact they have to be, the bound alone decides.
No kernel may reach another device: no remote copies, remote signals or barrier semaphores. Data moves between devices by JAX's collectives and lax.ppermute only.
A program may use at most 64 MiB of HBM per device.

v0:
```python
import jax
import jax.numpy as jnp
from jax import lax
from jax.sharding import PartitionSpec as P

STEPS = 5
NPML = 8


DT = 0.5
DAMPING = 0.1
STRENGTH = 3.0
SMAX = 0.8


def from_behind(value, axis, steps):
    count = lax.axis_size(axis)
    initial, last = (max(0, -steps), min(count, count - steps))
    return lax.ppermute(value, axis, [(source, source + steps) for source in range(initial, last)])


def move_x(face, by):
    return from_behind(face, "gx", by)


def move_y(face, by):
    return from_behind(face, "gy", by)


def move_z(face, by):
    return from_behind(face, "gz", by)


def ahead(f, axis, mover):
    size = f.shape[axis]
    arrived = mover(lax.slice_in_dim(f, 0, 1, axis=axis), -1)
    return jnp.concatenate([lax.slice_in_dim(f, 1, size, axis=axis), arrived], axis=axis)


def behind(f, axis, mover):
    size = f.shape[axis]
    arrived = mover(lax.slice_in_dim(f, size - 1, size, axis=axis), 1)
    return jnp.concatenate([arrived, lax.slice_in_dim(f, 0, size - 1, axis=axis)], axis=axis)


def curl_forward(f, movers):
    xpair = ahead(f[1:3], 1, movers[0])
    ypair = ahead(jnp.stack([f[0], f[2]]), 3, movers[1])
    zpair = ahead(f[0:2], 2, movers[2])
    dxy = xpair[0] - f[1]
    dxz = xpair[1] - f[2]
    dyx = ypair[0] - f[0]
    dyz = ypair[1] - f[2]
    dzx = zpair[0] - f[0]
    dzy = zpair[1] - f[1]
    return jnp.stack([dyz - dzy, dzx - dxz, dxy - dyx])


def curl_backward(f, movers):
    xpair = behind(f[1:3], 1, movers[0])
    ypair = behind(jnp.stack([f[0], f[2]]), 3, movers[1])
    zpair = behind(f[0:2], 2, movers[2])
    dxy = f[1] - xpair[0]
    dxz = f[2] - xpair[1]
    dyx = f[0] - ypair[0]
    dyz = f[2] - ypair[1]
    dzx = f[0] - zpair[0]
    dzy = f[1] - zpair[1]
    return jnp.stack([dyz - dzy, dzx - dxz, dxy - dyx])


def profile(index, total):
    depth = jnp.maximum(NPML - index, 0.0) + jnp.maximum(index - (total - 1 - NPML), 0.0)
    return SMAX * (depth / NPML) ** 3


def body(e_field, h_field, polar, permittivity, resonance, dispersive):
    xcount, zcount, ycount = permittivity.shape
    marks_block = dispersive.astype(jnp.float32)
    efield, hfield, pnow, eps, freq = (e_field, h_field, polar, permittivity, resonance)
    marks = jnp.repeat(marks_block, 128, axis=2)
    total_x = xcount * lax.axis_size("gx")
    total_y = ycount * lax.axis_size("gy")
    width = 0
    movers = (move_x, move_y, move_z)
    xlength = xcount + 2 * width
    ylength = ycount + 2 * width
    xpos = (lax.axis_index("gx") * xcount - width + jnp.arange(xlength)).astype(jnp.float32)
    ypos = (lax.axis_index("gy") * ycount - width + jnp.arange(ylength)).astype(jnp.float32)
    xinside = ((xpos >= 0.0) & (xpos < total_x)).astype(jnp.float32)
    yinside = ((ypos >= 0.0) & (ypos < total_y)).astype(jnp.float32)
    inside = xinside[:, None, None] * yinside[None, None, :]
    eps = jnp.where(inside > 0.0, eps, 1.0)
    sigma = profile(xpos, total_x)[:, None, None] + profile(ypos, total_y)[None, None, :]
    half = sigma * DT / 2.0
    h_keep = (1.0 - half) / (1.0 + half)
    h_gain = DT / (1.0 + half)
    e_keep = (eps - half) / (eps + half)
    e_gain = DT / (eps + half)
    wsq = (freq * DT) ** 2
    denom = 1.0 + DAMPING * DT / 2.0
    coef_one = (2.0 - wsq) / denom
    coef_two = (1.0 - DAMPING * DT / 2.0) / denom
    coef_three = STRENGTH * wsq / denom
    pold = pnow
    for step in range(STEPS):
        hfield = h_keep * hfield - h_gain * curl_forward(efield, movers)
        pnext = marks * (coef_one * pnow - coef_two * pold + coef_three * efield)
        efield = (
            e_keep * efield
            + e_gain * curl_backward(hfield, movers)
            - e_gain / DT * (pnext - marks * pnow)
        )
        pold = pnow
        pnow = pnext
    return (efield, hfield)


def solution(mesh):
    return jax.shard_map(
        body,
        mesh=mesh,
        in_specs=(
            P(None, "gx", "gz", "gy"),
            P(None, "gx", "gz", "gy"),
            P(None, "gx", "gz", "gy"),
            P("gx", "gz", "gy"),
            P("gx", "gz", "gy"),
            P("gx", "gz", "gy"),
        ),
        out_specs=(P(None, "gx", "gz", "gy"), P(None, "gx", "gz", "gy")),
        check_vma=False,
    )
```

profile of v0, /device:TPU:24, one launch (start us, length us, event | category | flops | bytes accessed | tf_op | source)
XLA Modules:
  0.0 152.9 jit_solution(10490481802502108007)
XLA Ops:
  0.6 0.8 slice.571
  1.4 2.3 %collective-permute-start.2 = (f32[2,1,16,256]{3,2,1,0:T(8,128)S(1)}, f32[2,1,16,256]{3,2,1,0:T(8,128)S(1)}, u32[]{:S(2)}, u32[]{:S(2)}) collective-permute-start(f32[2,1,16,256]{3,2,1,0:T(8,128)S(1)} %slice.571), channel_id=1, source_target_pairs={{8,0},{16,8},{24,16},{9,1},{17,9},{25,17},{10,2},{18,10},{26,18},{... | collective-permute-start | bytes 98312 | tf_op jit(solution)/shard_map/ppermute | solution.py:19
  3.7 1.0 slice.566
  4.7 1.3 collective-permute-start.1
  6.0 1.1 fusion.142
  7.1 1.4 collective-permute-start
  9.1 9.1 %collective-permute-done = f32[2,16,16,1]{3,2,1,0:T(8,128)S(1)} collective-permute-done((f32[2,16,16,1]{3,2,1,0:T(8,128)S(1)}, f32[2,16,16,1]{3,2,1,0:T(8,128)S(1)}, u32[]{:S(2)}, u32[]{:S(2)}) %collective-permute-start) | collective-permute-done | bytes 2080 | tf_op jit(solution)/shard_map/ppermute | solution.py:19
  18.8 0.5 copy-done.6
  19.5 0.8 fusion.86
  20.4 5.0 %collective-permute-start.3 = (f32[2,16,16,1]{3,2,1,0:T(8,128)}, f32[2,16,16,1]{3,2,1,0:T(8,128)}, u32[]{:S(2)}, u32[]{:S(2)}) collective-permute-start(f32[2,16,16,1]{3,2,1,0:T(8,128)} %fusion.86), channel_id=1, source_target_pairs={{0,2},{2,4},{4,6},{1,3},{3,5},{5,7},{8,10},{10,12},{12,14},{9,11},... | collective-permute-start | bytes 6152 | tf_op jit(solution)/shard_map/ppermute | solution.py:19
  25.4 0.9 subtract_multiply_fusion
  26.3 0.8 copy.8
  27.1 2.0 %broadcast_in_dim.16 = f32[16,16,2,128]{3,2,1,0:T(2,128)} broadcast(f32[16,16,2]{2,1,0:T(8,128)} %copy.8), dimensions={0,1,2} | broadcast | bytes 264192 | tf_op jit(solution)/shard_map/broadcast_in_dim | solution.py:81
  29.1 1.9 %mul.164 = f32[16,16,256]{2,1,0:T(8,128)} reshape(f32[16,16,2,128]{3,2,1,0:T(2,128)} %broadcast_in_dim.16) | data formatting | bytes 524288 | tf_op jit(solution)/shard_map/mul | solution.py:108
  31.1 1.9 %collective-permute-start.4 = (f32[2,16,1,256]{3,2,1,0:T(1,128)S(1)}, f32[2,16,1,256]{3,2,1,0:T(1,128)S(1)}, u32[]{:S(2)}, u32[]{:S(2)}) collective-permute-start(f32[2,16,1,256]{3,2,1,0:T(1,128)S(1)} %slice.724), channel_id=1, source_target_pairs={{0,1},{2,3},{4,5},{6,7},{8,9},{10,11},{12,13},{14,15},{16,17},{18,... | collective-permute-start | bytes 98312 | tf_op jit(solution)/shard_map/ppermute | solution.py:19
  33.0 1.3 collective-permute-start.5
  34.3 1.2 fusion.19
  35.5 3.3 %collective-permute-done.5 = f32[2,1,16,256]{3,2,1,0:T(8,128)S(1)} collective-permute-done((f32[2,1,16,256]{3,2,1,0:T(8,128)S(1)}, f32[2,1,16,256]{3,2,1,0:T(8,128)S(1)}, u32[]{:S(2)}, u32[]{:S(2)}) %collective-permute-start.5) | collective-permute-done | bytes 32800 | tf_op jit(solution)/shard_map/ppermute | solution.py:19
  39.1 0.5 fusion.2
  39.7 2.4 %collective-permute-start.8 = (f32[2,1,16,256]{3,2,1,0:T(8,128)S(1)}, f32[2,1,16,256]{3,2,1,0:T(8,128)S(1)}, u32[]{:S(2)}, u32[]{:S(2)}) collective-permute-start(f32[2,1,16,256]{3,2,1,0:T(8,128)S(1)} %slice.745), channel_id=1, source_target_pairs={{8,0},{16,8},{24,16},{9,1},{17,9},{25,17},{10,2},{18,10},{26,18},{... | collective-permute-start | bytes 98312 | tf_op jit(solution)/shard_map/ppermute | solution.py:19
  42.1 1.3 collective-permute-start.7
  43.4 1.3 collective-permute-start.6
  45.0 9.3 %collective-permute-done.6 = f32[2,16,16,1]{3,2,1,0:T(8,128)S(1)} collective-permute-done((f32[2,16,16,1]{3,2,1,0:T(8,128)S(1)}, f32[2,16,16,1]{3,2,1,0:T(8,128)S(1)}, u32[]{:S(2)}, u32[]{:S(2)}) %collective-permute-start.6) | collective-permute-done | bytes 2080 | tf_op jit(solution)/shard_map/ppermute | solution.py:19
  54.3 0.4 fusion.77
  55.2 2.7 %collective-permute-start.9 = (f32[2,16,16,1]{3,2,1,0:T(8,128)S(1)}, f32[2,16,16,1]{3,2,1,0:T(8,128)S(1)}, u32[]{:S(2)}, u32[]{:S(2)}) collective-permute-start(f32[2,16,16,1]{3,2,1,0:T(8,128)S(1)} %fusion.71), channel_id=1, source_target_pairs={{0,2},{2,4},{4,6},{1,3},{3,5},{5,7},{8,10},{10,12},{12,14},{9,11},... | collective-permute-start | bytes 6152 | tf_op jit(solution)/shard_map/ppermute | solution.py:19
  58.1 1.7 %collective-permute-start.10 = (f32[2,16,1,256]{3,2,1,0:T(1,128)S(1)}, f32[2,16,1,256]{3,2,1,0:T(1,128)S(1)}, u32[]{:S(2)}, u32[]{:S(2)}) collective-permute-start(f32[2,16,1,256]{3,2,1,0:T(1,128)S(1)} %slice.754), channel_id=1, source_target_pairs={{0,1},{2,3},{4,5},{6,7},{8,9},{10,11},{12,13},{14,15},{16,17},{18,... | collective-permute-start | bytes 98312 | tf_op jit(solution)/shard_map/ppermute | solution.py:19
  59.8 1.3 collective-permute-start.11
  61.1 2.6 %collective-permute-done.9 = f32[2,16,16,1]{3,2,1,0:T(8,128)S(1)} collective-permute-done((f32[2,16,16,1]{3,2,1,0:T(8,128)S(1)}, f32[2,16,16,1]{3,2,1,0:T(8,128)S(1)}, u32[]{:S(2)}, u32[]{:S(2)}) %collective-permute-start.9) | collective-permute-done | bytes 2080 | tf_op jit(solution)/shard_map/ppermute | solution.py:19
  63.9 1.7 %collective-permute-done.11 = f32[2,1,16,256]{3,2,1,0:T(8,128)S(1)} collective-permute-done((f32[2,1,16,256]{3,2,1,0:T(8,128)S(1)}, f32[2,1,16,256]{3,2,1,0:T(8,128)S(1)}, u32[]{:S(2)}, u32[]{:S(2)}) %collective-permute-start.11) | collective-permute-done | bytes 32800 | tf_op jit(solution)/shard_map/ppermute | solution.py:19
  65.9 0.7 fusion.5
  66.6 2.4 %collective-permute-start.14 = (f32[2,1,16,256]{3,2,1,0:T(8,128)S(1)}, f32[2,1,16,256]{3,2,1,0:T(8,128)S(1)}, u32[]{:S(2)}, u32[]{:S(2)}) collective-permute-start(f32[2,1,16,256]{3,2,1,0:T(8,128)S(1)} %slice.775), channel_id=1, source_target_pairs={{8,0},{16,8},{24,16},{9,1},{17,9},{25,17},{10,2},{18,10},{26,18},{... | collective-permute-start | bytes 98312 | tf_op jit(solution)/shard_map/ppermute | solution.py:19
  69.0 1.3 collective-permute-start.13
  70.3 1.3 collective-permute-start.12
  71.9 9.3 %collective-permute-done.12 = f32[2,16,16,1]{3,2,1,0:T(8,128)S(1)} collective-permute-done((f32[2,16,16,1]{3,2,1,0:T(8,128)S(1)}, f32[2,16,16,1]{3,2,1,0:T(8,128)S(1)}, u32[]{:S(2)}, u32[]{:S(2)}) %collective-permute-start.12) | collective-permute-done | bytes 2080 | tf_op jit(solution)/shard_map/ppermute | solution.py:19
  81.3 0.4 fusion.62
  81.6 0.4 fusion.6
  82.2 3.6 %collective-permute-start.15 = (f32[2,16,16,1]{3,2,1,0:T(8,128)S(1)}, f32[2,16,16,1]{3,2,1,0:T(8,128)S(1)}, u32[]{:S(2)}, u32[]{:S(2)}) collective-permute-start(f32[2,16,16,1]{3,2,1,0:T(8,128)S(1)} %fusion.56), channel_id=1, source_target_pairs={{0,2},{2,4},{4,6},{1,3},{3,5},{5,7},{8,10},{10,12},{12,14},{9,11},... | collective-permute-start | bytes 6152 | tf_op jit(solution)/shard_map/ppermute | solution.py:19
  86.0 1.7 %collective-permute-start.16 = (f32[2,16,1,256]{3,2,1,0:T(1,128)S(1)}, f32[2,16,1,256]{3,2,1,0:T(1,128)S(1)}, u32[]{:S(2)}, u32[]{:S(2)}) collective-permute-start(f32[2,16,1,256]{3,2,1,0:T(1,128)S(1)} %slice.784), channel_id=1, source_target_pairs={{0,1},{2,3},{4,5},{6,7},{8,9},{10,11},{12,13},{14,15},{16,17},{18,... | collective-permute-start | bytes 98312 | tf_op jit(solution)/shard_map/ppermute | solution.py:19
  87.7 1.3 collective-permute-start.17
  89.0 2.6 %collective-permute-done.15 = f32[2,16,16,1]{3,2,1,0:T(8,128)S(1)} collective-permute-done((f32[2,16,16,1]{3,2,1,0:T(8,128)S(1)}, f32[2,16,16,1]{3,2,1,0:T(8,128)S(1)}, u32[]{:S(2)}, u32[]{:S(2)}) %collective-permute-start.15) | collective-permute-done | bytes 2080 | tf_op jit(solution)/shard_map/ppermute | solution.py:19
  91.9 1.7 %collective-permute-done.17 = f32[2,1,16,256]{3,2,1,0:T(8,128)S(1)} collective-permute-done((f32[2,1,16,256]{3,2,1,0:T(8,128)S(1)}, f32[2,1,16,256]{3,2,1,0:T(8,128)S(1)}, u32[]{:S(2)}, u32[]{:S(2)}) %collective-permute-start.17) | collective-permute-done | bytes 32800 | tf_op jit(solution)/shard_map/ppermute | solution.py:19
  93.8 1.0 fusion.8
  94.9 2.2 %collective-permute-start.20 = (f32[2,1,16,256]{3,2,1,0:T(8,128)S(1)}, f32[2,1,16,256]{3,2,1,0:T(8,128)S(1)}, u32[]{:S(2)}, u32[]{:S(2)}) collective-permute-start(f32[2,1,16,256]{3,2,1,0:T(8,128)S(1)} %slice.805), channel_id=1, source_target_pairs={{8,0},{16,8},{24,16},{9,1},{17,9},{25,17},{10,2},{18,10},{26,18},{... | collective-permute-start | bytes 98312 | tf_op jit(solution)/shard_map/ppermute | solution.py:19
  97.1 1.3 collective-permute-start.19
  98.4 1.3 collective-permute-start.18
  100.0 9.3 %collective-permute-done.18 = f32[2,16,16,1]{3,2,1,0:T(8,128)S(1)} collective-permute-done((f32[2,16,16,1]{3,2,1,0:T(8,128)S(1)}, f32[2,16,16,1]{3,2,1,0:T(8,128)S(1)}, u32[]{:S(2)}, u32[]{:S(2)}) %collective-permute-start.18) | collective-permute-done | bytes 2080 | tf_op jit(solution)/shard_map/ppermute | solution.py:19
  109.7 0.5 fusion.9
  110.4 3.6 %collective-permute-start.21 = (f32[2,16,16,1]{3,2,1,0:T(8,128)S(1)}, f32[2,16,16,1]{3,2,1,0:T(8,128)S(1)}, u32[]{:S(2)}, u32[]{:S(2)}) collective-permute-start(f32[2,16,16,1]{3,2,1,0:T(8,128)S(1)} %fusion.41), channel_id=1, source_target_pairs={{0,2},{2,4},{4,6},{1,3},{3,5},{5,7},{8,10},{10,12},{12,14},{9,11},... | collective-permute-start | bytes 6152 | tf_op jit(solution)/shard_map/ppermute | solution.py:19
  114.2 1.7 %collective-permute-start.22 = (f32[2,16,1,256]{3,2,1,0:T(1,128)S(1)}, f32[2,16,1,256]{3,2,1,0:T(1,128)S(1)}, u32[]{:S(2)}, u32[]{:S(2)}) collective-permute-start(f32[2,16,1,256]{3,2,1,0:T(1,128)S(1)} %slice.814), channel_id=1, source_target_pairs={{0,1},{2,3},{4,5},{6,7},{8,9},{10,11},{12,13},{14,15},{16,17},{18,... | collective-permute-start | bytes 98312 | tf_op jit(solution)/shard_map/ppermute | solution.py:19
  115.9 1.5 collective-permute-start.23
  117.4 2.4 %collective-permute-done.21 = f32[2,16,16,1]{3,2,1,0:T(8,128)S(1)} collective-permute-done((f32[2,16,16,1]{3,2,1,0:T(8,128)S(1)}, f32[2,16,16,1]{3,2,1,0:T(8,128)S(1)}, u32[]{:S(2)}, u32[]{:S(2)}) %collective-permute-start.21) | collective-permute-done | bytes 2080 | tf_op jit(solution)/shard_map/ppermute | solution.py:19
  120.0 1.7 %collective-permute-done.23 = f32[2,1,16,256]{3,2,1,0:T(8,128)S(1)} collective-permute-done((f32[2,1,16,256]{3,2,1,0:T(8,128)S(1)}, f32[2,1,16,256]{3,2,1,0:T(8,128)S(1)}, u32[]{:S(2)}, u32[]{:S(2)}) %collective-permute-start.23) | collective-permute-done | bytes 32800 | tf_op jit(solution)/shard_map/ppermute | solution.py:19
  122.0 1.4 fusion.11
  123.5 1.9 %collective-permute-start.26 = (f32[2,1,16,256]{3,2,1,0:T(8,128)S(1)}, f32[2,1,16,256]{3,2,1,0:T(8,128)S(1)}, u32[]{:S(2)}, u32[]{:S(2)}) collective-permute-start(f32[2,1,16,256]{3,2,1,0:T(8,128)S(1)} %slice.835), channel_id=1, source_target_pairs={{8,0},{16,8},{24,16},{9,1},{17,9},{25,17},{10,2},{18,10},{26,18},{... | collective-permute-start | bytes 98312 | tf_op jit(solution)/shard_map/ppermute | solution.py:19
  125.4 1.3 collective-permute-start.25
  126.7 1.3 collective-permute-start.24
  128.3 9.3 %collective-permute-done.24 = f32[2,16,16,1]{3,2,1,0:T(8,128)S(1)} collective-permute-done((f32[2,16,16,1]{3,2,1,0:T(8,128)S(1)}, f32[2,16,16,1]{3,2,1,0:T(8,128)S(1)}, u32[]{:S(2)}, u32[]{:S(2)}) %collective-permute-start.24) | collective-permute-done | bytes 2080 | tf_op jit(solution)/shard_map/ppermute | solution.py:19
  138.0 0.6 fusion.12
  138.8 3.6 %collective-permute-start.27 = (f32[2,16,16,1]{3,2,1,0:T(8,128)S(1)}, f32[2,16,16,1]{3,2,1,0:T(8,128)S(1)}, u32[]{:S(2)}, u32[]{:S(2)}) collective-permute-start(f32[2,16,16,1]{3,2,1,0:T(8,128)S(1)} %fusion.26), channel_id=1, source_target_pairs={{0,2},{2,4},{4,6},{1,3},{3,5},{5,7},{8,10},{10,12},{12,14},{9,11},... | collective-permute-start | bytes 6152 | tf_op jit(solution)/shard_map/ppermute | solution.py:19
  142.6 1.7 %collective-permute-start.28 = (f32[2,16,1,256]{3,2,1,0:T(1,128)S(1)}, f32[2,16,1,256]{3,2,1,0:T(1,128)S(1)}, u32[]{:S(2)}, u32[]{:S(2)}) collective-permute-start(f32[2,16,1,256]{3,2,1,0:T(1,128)S(1)} %slice.844), channel_id=1, source_target_pairs={{0,1},{2,3},{4,5},{6,7},{8,9},{10,11},{12,13},{14,15},{16,17},{18,... | collective-permute-start | bytes 98312 | tf_op jit(solution)/shard_map/ppermute | solution.py:19
  144.3 1.3 collective-permute-start.29
  145.6 2.6 %collective-permute-done.27 = f32[2,16,16,1]{3,2,1,0:T(8,128)S(1)} collective-permute-done((f32[2,16,16,1]{3,2,1,0:T(8,128)S(1)}, f32[2,16,16,1]{3,2,1,0:T(8,128)S(1)}, u32[]{:S(2)}, u32[]{:S(2)}) %collective-permute-start.27) | collective-permute-done | bytes 2080 | tf_op jit(solution)/shard_map/ppermute | solution.py:19
  148.5 1.7 %collective-permute-done.29 = f32[2,1,16,256]{3,2,1,0:T(8,128)S(1)} collective-permute-done((f32[2,1,16,256]{3,2,1,0:T(8,128)S(1)}, f32[2,1,16,256]{3,2,1,0:T(8,128)S(1)}, u32[]{:S(2)}, u32[]{:S(2)}) %collective-permute-start.29) | collective-permute-done | bytes 32800 | tf_op jit(solution)/shard_map/ppermute | solution.py:19
  150.5 2.5 %fusion.14 = f32[3,16,16,256]{3,2,1,0:T(8,128)} fusion(f32[1,16,16,256]{3,2,1,0:T(8,128)S(1)} %get-tuple-element.21, f32[1,16,16,256]{3,2,1,0:T(8,128)S(1)} %get-tuple-element.20, f32[1,16,16,256]{3,2,1,0:T(8,128)S(1)} %get-tuple-element.19, f32[16,16,256]{2,1,0:T(8,128)S(1)} %get-tuple-element.56, f32[16,16,256]{2,1,0:T(8,128)S(1)} %get-tuple-element.55, ...), kind=kLoop, calls=%fused_computation.24 | loop fusion | flops 14548992 | bytes 7864320 | tf_op jit(solution)/shard_map/sub | solution.py:110
  (135 shorter events, 7.3 us)
Async XLA Ops:
  1.4 16.8 %collective-permute-start.2 = (f32[2,1,16,256]{3,2,1,0:T(8,128)S(1)}, f32[2,1,16,256]{3,2,1,0:T(8,128)S(1)}, u32[]{:S(2)}, u32[]{:S(2)}) collective-permute-start(f32[2,1,16,256]{3,2,1,0:T(8,128)S(1)} %slice.571), channel_id=1, source_target_pairs={{8,0},{16,8},{24,16},{9,1},{17,9},{25,17},{10,2},{18,10},{26,18},{... | collective-permute-start | bytes 98312 | tf_op jit(solution)/shard_map/ppermute | solution.py:19
  4.7 13.5 %collective-permute-start.1 = (f32[2,16,1,256]{3,2,1,0:T(1,128)S(1)}, f32[2,16,1,256]{3,2,1,0:T(1,128)S(1)}, u32[]{:S(2)}, u32[]{:S(2)}) collective-permute-start(f32[2,16,1,256]{3,2,1,0:T(1,128)S(1)} %slice.566), channel_id=1, source_target_pairs={{1,0},{3,2},{5,4},{7,6},{9,8},{11,10},{13,12},{15,14},{17,16},{19,... | collective-permute-start | bytes 98312 | tf_op jit(solution)/shard_map/ppermute | solution.py:19
  7.1 1.9 %copy-start = (f32[3,16,16,256]{3,2,1,0:T(8,128)S(1)}, f32[3,16,16,256]{3,2,1,0:T(8,128)}, u32[]{:S(2)}) copy-start(f32[3,16,16,256]{3,2,1,0:T(8,128)} %param.6) | copy-start | bytes 2359300
  7.1 11.0 %collective-permute-start = (f32[2,16,16,1]{3,2,1,0:T(8,128)S(1)}, f32[2,16,16,1]{3,2,1,0:T(8,128)S(1)}, u32[]{:S(2)}, u32[]{:S(2)}) collective-permute-start(f32[2,16,16,1]{3,2,1,0:T(8,128)S(1)} %pad_maximum_fusion.34), channel_id=1, source_target_pairs={{2,0},{4,2},{6,4},{3,1},{5,3},{7,5},{10,8},{12,10},{14,12},{11,9},... | collective-permute-start | bytes 6152 | tf_op jit(solution)/shard_map/ppermute | solution.py:19
  9.1 9.5 %copy-start.1 = (f32[3,16,16,256]{3,2,1,0:T(8,128)S(1)}, f32[3,16,16,256]{3,2,1,0:T(8,128)}, u32[]{:S(2)}) copy-start(f32[3,16,16,256]{3,2,1,0:T(8,128)} %param.7) | copy-start | bytes 2359300
  18.5 0.7 copy-start.6
  18.5 0.8 copy-start.8
  18.6 0.9 copy-start.10
  19.5 0.9 copy-start.12
  19.5 0.9 copy-start.14
  19.5 5.9 %copy-start.16 = (f32[16,16,256]{2,1,0:T(8,128)S(1)}, f32[16,16,256]{2,1,0:T(8,128)}, u32[]{:S(2)}) copy-start(f32[16,16,256]{2,1,0:T(8,128)} %param.10) | copy-start | bytes 786436
  19.5 5.9 %copy-start.17 = (f32[16,16,256]{2,1,0:T(8,128)S(1)}, f32[16,16,256]{2,1,0:T(8,128)}, u32[]{:S(2)}) copy-start(f32[16,16,256]{2,1,0:T(8,128)} %param.9) | copy-start | bytes 786436
  20.4 13.9 %collective-permute-start.3 = (f32[2,16,16,1]{3,2,1,0:T(8,128)}, f32[2,16,16,1]{3,2,1,0:T(8,128)}, u32[]{:S(2)}, u32[]{:S(2)}) collective-permute-start(f32[2,16,16,1]{3,2,1,0:T(8,128)} %fusion.86), channel_id=1, source_target_pairs={{0,2},{2,4},{4,6},{1,3},{3,5},{5,7},{8,10},{10,12},{12,14},{9,11},... | collective-permute-start | bytes 6152 | tf_op jit(solution)/shard_map/ppermute | solution.py:19
  25.4 0.9 copy-start.18
  31.0 3.3 %copy-start.13 = (f32[1,16,16,256]{3,2,1,0:T(8,128)S(1)}, f32[1,16,16,256]{3,2,1,0:T(8,128)}, u32[]{:S(2)}) copy-start(f32[1,16,16,256]{3,2,1,0:T(8,128)} %copy-done.12) | copy-start | bytes 786436
  31.0 3.3 %copy-start.15 = (f32[1,16,16,256]{3,2,1,0:T(8,128)S(1)}, f32[1,16,16,256]{3,2,1,0:T(8,128)}, u32[]{:S(2)}) copy-start(f32[1,16,16,256]{3,2,1,0:T(8,128)} %copy-done.14) | copy-start | bytes 786436
  31.1 4.4 %collective-permute-start.4 = (f32[2,16,1,256]{3,2,1,0:T(1,128)S(1)}, f32[2,16,1,256]{3,2,1,0:T(1,128)S(1)}, u32[]{:S(2)}, u32[]{:S(2)}) collective-permute-start(f32[2,16,1,256]{3,2,1,0:T(1,128)S(1)} %slice.724), channel_id=1, source_target_pairs={{0,1},{2,3},{4,5},{6,7},{8,9},{10,11},{12,13},{14,15},{16,17},{18,... | collective-permute-start | bytes 98312 | tf_op jit(solution)/shard_map/ppermute | solution.py:19
  33.0 5.8 %collective-permute-start.5 = (f32[2,1,16,256]{3,2,1,0:T(8,128)S(1)}, f32[2,1,16,256]{3,2,1,0:T(8,128)S(1)}, u32[]{:S(2)}, u32[]{:S(2)}) collective-permute-start(f32[2,1,16,256]{3,2,1,0:T(8,128)S(1)} %slice.728), channel_id=1, source_target_pairs={{0,8},{8,16},{16,24},{1,9},{9,17},{17,25},{2,10},{10,18},{18,26},{... | collective-permute-start | bytes 98312 | tf_op jit(solution)/shard_map/ppermute | solution.py:19
  35.5 3.6 %copy-start.2 = (f32[3,16,16,256]{3,2,1,0:T(8,128)S(1)}, f32[3,16,16,256]{3,2,1,0:T(8,128)}, u32[]{:S(2)}) copy-start(f32[3,16,16,256]{3,2,1,0:T(8,128)} %param.8) | copy-start | bytes 2359300
  35.5 3.6 %copy-start.4 = (f32[16,16,256]{2,1,0:T(8,128)S(1)}, f32[16,16,256]{2,1,0:T(8,128)}, u32[]{:S(2)}) copy-start(f32[16,16,256]{2,1,0:T(8,128)} %get-tuple-element.62) | copy-start | bytes 786436
  35.5 3.6 %copy-start.5 = (f32[16,16,256]{2,1,0:T(8,128)S(1)}, f32[16,16,256]{2,1,0:T(8,128)}, u32[]{:S(2)}) copy-start(f32[16,16,256]{2,1,0:T(8,128)} %mul.164) | copy-start | bytes 786436
  39.7 14.6 %collective-permute-start.8 = (f32[2,1,16,256]{3,2,1,0:T(8,128)S(1)}, f32[2,1,16,256]{3,2,1,0:T(8,128)S(1)}, u32[]{:S(2)}, u32[]{:S(2)}) collective-permute-start(f32[2,1,16,256]{3,2,1,0:T(8,128)S(1)} %slice.745), channel_id=1, source_target_pairs={{8,0},{16,8},{24,16},{9,1},{17,9},{25,17},{10,2},{18,10},{26,18},{... | collective-permute-start | bytes 98312 | tf_op jit(solution)/shard_map/ppermute | solution.py:19
  42.1 12.2 %collective-permute-start.7 = (f32[2,16,1,256]{3,2,1,0:T(1,128)S(1)}, f32[2,16,1,256]{3,2,1,0:T(1,128)S(1)}, u32[]{:S(2)}, u32[]{:S(2)}) collective-permute-start(f32[2,16,1,256]{3,2,1,0:T(1,128)S(1)} %slice.740), channel_id=1, source_target_pairs={{1,0},{3,2},{5,4},{7,6},{9,8},{11,10},{13,12},{15,14},{17,16},{19,... | collective-permute-start | bytes 98312 | tf_op jit(solution)/shard_map/ppermute | solution.py:19
  43.4 10.9 %collective-permute-start.6 = (f32[2,16,16,1]{3,2,1,0:T(8,128)S(1)}, f32[2,16,16,1]{3,2,1,0:T(8,128)S(1)}, u32[]{:S(2)}, u32[]{:S(2)}) collective-permute-start(f32[2,16,16,1]{3,2,1,0:T(8,128)S(1)} %pad_maximum_fusion.28), channel_id=1, source_target_pairs={{2,0},{4,2},{6,4},{3,1},{5,3},{7,5},{10,8},{12,10},{14,12},{11,9},... | collective-permute-start | bytes 6152 | tf_op jit(solution)/shard_map/ppermute | solution.py:19
  45.0 9.7 %copy-start.7 = (f32[1,16,16,256]{3,2,1,0:T(8,128)S(1)}, f32[1,16,16,256]{3,2,1,0:T(8,128)}, u32[]{:S(2)}) copy-start(f32[1,16,16,256]{3,2,1,0:T(8,128)} %copy-done.6) | copy-start | bytes 786436
  45.0 9.7 %copy-start.9 = (f32[1,16,16,256]{3,2,1,0:T(8,128)S(1)}, f32[1,16,16,256]{3,2,1,0:T(8,128)}, u32[]{:S(2)}) copy-start(f32[1,16,16,256]{3,2,1,0:T(8,128)} %copy-done.8) | copy-start | bytes 786436
  45.0 9.7 %copy-start.11 = (f32[1,16,16,256]{3,2,1,0:T(8,128)S(1)}, f32[1,16,16,256]{3,2,1,0:T(8,128)}, u32[]{:S(2)}) copy-start(f32[1,16,16,256]{3,2,1,0:T(8,128)} %copy-done.10) | copy-start | bytes 786436
  55.2 8.6 %collective-permute-start.9 = (f32[2,16,16,1]{3,2,1,0:T(8,128)S(1)}, f32[2,16,16,1]{3,2,1,0:T(8,128)S(1)}, u32[]{:S(2)}, u32[]{:S(2)}) collective-permute-start(f32[2,16,16,1]{3,2,1,0:T(8,128)S(1)} %fusion.71), channel_id=1, source_target_pairs={{0,2},{2,4},{4,6},{1,3},{3,5},{5,7},{8,10},{10,12},{12,14},{9,11},... | collective-permute-start | bytes 6152 | tf_op jit(solution)/shard_map/ppermute | solution.py:19
  58.1 5.9 %collective-permute-start.10 = (f32[2,16,1,256]{3,2,1,0:T(1,128)S(1)}, f32[2,16,1,256]{3,2,1,0:T(1,128)S(1)}, u32[]{:S(2)}, u32[]{:S(2)}) collective-permute-start(f32[2,16,1,256]{3,2,1,0:T(1,128)S(1)} %slice.754), channel_id=1, source_target_pairs={{0,1},{2,3},{4,5},{6,7},{8,9},{10,11},{12,13},{14,15},{16,17},{18,... | collective-permute-start | bytes 98312 | tf_op jit(solution)/shard_map/ppermute | solution.py:19
  59.8 5.8 %collective-permute-start.11 = (f32[2,1,16,256]{3,2,1,0:T(8,128)S(1)}, f32[2,1,16,256]{3,2,1,0:T(8,128)S(1)}, u32[]{:S(2)}, u32[]{:S(2)}) collective-permute-start(f32[2,1,16,256]{3,2,1,0:T(8,128)S(1)} %slice.758), channel_id=1, source_target_pairs={{0,8},{8,16},{16,24},{1,9},{9,17},{17,25},{2,10},{10,18},{18,26},{... | collective-permute-start | bytes 98312 | tf_op jit(solution)/shard_map/ppermute | solution.py:19
  66.6 14.6 %collective-permute-start.14 = (f32[2,1,16,256]{3,2,1,0:T(8,128)S(1)}, f32[2,1,16,256]{3,2,1,0:T(8,128)S(1)}, u32[]{:S(2)}, u32[]{:S(2)}) collective-permute-start(f32[2,1,16,256]{3,2,1,0:T(8,128)S(1)} %slice.775), channel_id=1, source_target_pairs={{8,0},{16,8},{24,16},{9,1},{17,9},{25,17},{10,2},{18,10},{26,18},{... | collective-permute-start | bytes 98312 | tf_op jit(solution)/shard_map/ppermute | solution.py:19
  69.0 12.2 %collective-permute-start.13 = (f32[2,16,1,256]{3,2,1,0:T(1,128)S(1)}, f32[2,16,1,256]{3,2,1,0:T(1,128)S(1)}, u32[]{:S(2)}, u32[]{:S(2)}) collective-permute-start(f32[2,16,1,256]{3,2,1,0:T(1,128)S(1)} %slice.770), channel_id=1, source_target_pairs={{1,0},{3,2},{5,4},{7,6},{9,8},{11,10},{13,12},{15,14},{17,16},{19,... | collective-permute-start | bytes 98312 | tf_op jit(solution)/shard_map/ppermute | solution.py:19
  70.3 10.9 %collective-permute-start.12 = (f32[2,16,16,1]{3,2,1,0:T(8,128)S(1)}, f32[2,16,16,1]{3,2,1,0:T(8,128)S(1)}, u32[]{:S(2)}, u32[]{:S(2)}) collective-permute-start(f32[2,16,16,1]{3,2,1,0:T(8,128)S(1)} %pad_maximum_fusion.22), channel_id=1, source_target_pairs={{2,0},{4,2},{6,4},{3,1},{5,3},{7,5},{10,8},{12,10},{14,12},{11,9},... | collective-permute-start | bytes 6152 | tf_op jit(solution)/shard_map/ppermute | solution.py:19
  82.2 9.5 %collective-permute-start.15 = (f32[2,16,16,1]{3,2,1,0:T(8,128)S(1)}, f32[2,16,16,1]{3,2,1,0:T(8,128)S(1)}, u32[]{:S(2)}, u32[]{:S(2)}) collective-permute-start(f32[2,16,16,1]{3,2,1,0:T(8,128)S(1)} %fusion.56), channel_id=1, source_target_pairs={{0,2},{2,4},{4,6},{1,3},{3,5},{5,7},{8,10},{10,12},{12,14},{9,11},... | collective-permute-start | bytes 6152 | tf_op jit(solution)/shard_map/ppermute | solution.py:19
  86.0 5.9 %collective-permute-start.16 = (f32[2,16,1,256]{3,2,1,0:T(1,128)S(1)}, f32[2,16,1,256]{3,2,1,0:T(1,128)S(1)}, u32[]{:S(2)}, u32[]{:S(2)}) collective-permute-start(f32[2,16,1,256]{3,2,1,0:T(1,128)S(1)} %slice.784), channel_id=1, source_target_pairs={{0,1},{2,3},{4,5},{6,7},{8,9},{10,11},{12,13},{14,15},{16,17},{18,... | collective-permute-start | bytes 98312 | tf_op jit(solution)/shard_map/ppermute | solution.py:19
  87.7 5.8 %collective-permute-start.17 = (f32[2,1,16,256]{3,2,1,0:T(8,128)S(1)}, f32[2,1,16,256]{3,2,1,0:T(8,128)S(1)}, u32[]{:S(2)}, u32[]{:S(2)}) collective-permute-start(f32[2,1,16,256]{3,2,1,0:T(8,128)S(1)} %slice.788), channel_id=1, source_target_pairs={{0,8},{8,16},{16,24},{1,9},{9,17},{17,25},{2,10},{10,18},{18,26},{... | collective-permute-start | bytes 98312 | tf_op jit(solution)/shard_map/ppermute | solution.py:19
  94.9 14.4 %collective-permute-start.20 = (f32[2,1,16,256]{3,2,1,0:T(8,128)S(1)}, f32[2,1,16,256]{3,2,1,0:T(8,128)S(1)}, u32[]{:S(2)}, u32[]{:S(2)}) collective-permute-start(f32[2,1,16,256]{3,2,1,0:T(8,128)S(1)} %slice.805), channel_id=1, source_target_pairs={{8,0},{16,8},{24,16},{9,1},{17,9},{25,17},{10,2},{18,10},{26,18},{... | collective-permute-start | bytes 98312 | tf_op jit(solution)/shard_map/ppermute | solution.py:19
  97.1 12.2 %collective-permute-start.19 = (f32[2,16,1,256]{3,2,1,0:T(1,128)S(1)}, f32[2,16,1,256]{3,2,1,0:T(1,128)S(1)}, u32[]{:S(2)}, u32[]{:S(2)}) collective-permute-start(f32[2,16,1,256]{3,2,1,0:T(1,128)S(1)} %slice.800), channel_id=1, source_target_pairs={{1,0},{3,2},{5,4},{7,6},{9,8},{11,10},{13,12},{15,14},{17,16},{19,... | collective-permute-start | bytes 98312 | tf_op jit(solution)/shard_map/ppermute | solution.py:19
  98.4 10.9 %collective-permute-start.18 = (f32[2,16,16,1]{3,2,1,0:T(8,128)S(1)}, f32[2,16,16,1]{3,2,1,0:T(8,128)S(1)}, u32[]{:S(2)}, u32[]{:S(2)}) collective-permute-start(f32[2,16,16,1]{3,2,1,0:T(8,128)S(1)} %pad_maximum_fusion.16), channel_id=1, source_target_pairs={{2,0},{4,2},{6,4},{3,1},{5,3},{7,5},{10,8},{12,10},{14,12},{11,9},... | collective-permute-start | bytes 6152 | tf_op jit(solution)/shard_map/ppermute | solution.py:19
  110.4 9.5 %collective-permute-start.21 = (f32[2,16,16,1]{3,2,1,0:T(8,128)S(1)}, f32[2,16,16,1]{3,2,1,0:T(8,128)S(1)}, u32[]{:S(2)}, u32[]{:S(2)}) collective-permute-start(f32[2,16,16,1]{3,2,1,0:T(8,128)S(1)} %fusion.41), channel_id=1, source_target_pairs={{0,2},{2,4},{4,6},{1,3},{3,5},{5,7},{8,10},{10,12},{12,14},{9,11},... | collective-permute-start | bytes 6152 | tf_op jit(solution)/shard_map/ppermute | solution.py:19
  114.2 5.9 %collective-permute-start.22 = (f32[2,16,1,256]{3,2,1,0:T(1,128)S(1)}, f32[2,16,1,256]{3,2,1,0:T(1,128)S(1)}, u32[]{:S(2)}, u32[]{:S(2)}) collective-permute-start(f32[2,16,1,256]{3,2,1,0:T(1,128)S(1)} %slice.814), channel_id=1, source_target_pairs={{0,1},{2,3},{4,5},{6,7},{8,9},{10,11},{12,13},{14,15},{16,17},{18,... | collective-permute-start | bytes 98312 | tf_op jit(solution)/shard_map/ppermute | solution.py:19
  115.9 5.8 %collective-permute-start.23 = (f32[2,1,16,256]{3,2,1,0:T(8,128)S(1)}, f32[2,1,16,256]{3,2,1,0:T(8,128)S(1)}, u32[]{:S(2)}, u32[]{:S(2)}) collective-permute-start(f32[2,1,16,256]{3,2,1,0:T(8,128)S(1)} %slice.818), channel_id=1, source_target_pairs={{0,8},{8,16},{16,24},{1,9},{9,17},{17,25},{2,10},{10,18},{18,26},{... | collective-permute-start | bytes 98312 | tf_op jit(solution)/shard_map/ppermute | solution.py:19
  123.5 14.2 %collective-permute-start.26 = (f32[2,1,16,256]{3,2,1,0:T(8,128)S(1)}, f32[2,1,16,256]{3,2,1,0:T(8,128)S(1)}, u32[]{:S(2)}, u32[]{:S(2)}) collective-permute-start(f32[2,1,16,256]{3,2,1,0:T(8,128)S(1)} %slice.835), channel_id=1, source_target_pairs={{8,0},{16,8},{24,16},{9,1},{17,9},{25,17},{10,2},{18,10},{26,18},{... | collective-permute-start | bytes 98312 | tf_op jit(solution)/shard_map/ppermute | solution.py:19
  125.4 12.2 %collective-permute-start.25 = (f32[2,16,1,256]{3,2,1,0:T(1,128)S(1)}, f32[2,16,1,256]{3,2,1,0:T(1,128)S(1)}, u32[]{:S(2)}, u32[]{:S(2)}) collective-permute-start(f32[2,16,1,256]{3,2,1,0:T(1,128)S(1)} %slice.830), channel_id=1, source_target_pairs={{1,0},{3,2},{5,4},{7,6},{9,8},{11,10},{13,12},{15,14},{17,16},{19,... | collective-permute-start | bytes 98312 | tf_op jit(solution)/shard_map/ppermute | solution.py:19
  126.7 10.9 %collective-permute-start.24 = (f32[2,16,16,1]{3,2,1,0:T(8,128)S(1)}, f32[2,16,16,1]{3,2,1,0:T(8,128)S(1)}, u32[]{:S(2)}, u32[]{:S(2)}) collective-permute-start(f32[2,16,16,1]{3,2,1,0:T(8,128)S(1)} %pad_maximum_fusion.10), channel_id=1, source_target_pairs={{2,0},{4,2},{6,4},{3,1},{5,3},{7,5},{10,8},{12,10},{14,12},{11,9},... | collective-permute-start | bytes 6152 | tf_op jit(solution)/shard_map/ppermute | solution.py:19
  138.6 11.5 %copy-start.3 = (f32[3,16,16,256]{3,2,1,0:T(8,128)}, f32[3,16,16,256]{3,2,1,0:T(8,128)S(1)}, u32[]{:S(2)}) copy-start(f32[3,16,16,256]{3,2,1,0:T(8,128)S(1)} %fusion.12) | copy-start | bytes 2359300
  138.8 9.5 %collective-permute-start.27 = (f32[2,16,16,1]{3,2,1,0:T(8,128)S(1)}, f32[2,16,16,1]{3,2,1,0:T(8,128)S(1)}, u32[]{:S(2)}, u32[]{:S(2)}) collective-permute-start(f32[2,16,16,1]{3,2,1,0:T(8,128)S(1)} %fusion.26), channel_id=1, source_target_pairs={{0,2},{2,4},{4,6},{1,3},{3,5},{5,7},{8,10},{10,12},{12,14},{9,11},... | collective-permute-start | bytes 6152 | tf_op jit(solution)/shard_map/ppermute | solution.py:19
  142.6 5.9 %collective-permute-start.28 = (f32[2,16,1,256]{3,2,1,0:T(1,128)S(1)}, f32[2,16,1,256]{3,2,1,0:T(1,128)S(1)}, u32[]{:S(2)}, u32[]{:S(2)}) collective-permute-start(f32[2,16,1,256]{3,2,1,0:T(1,128)S(1)} %slice.844), channel_id=1, source_target_pairs={{0,1},{2,3},{4,5},{6,7},{8,9},{10,11},{12,13},{14,15},{16,17},{18,... | collective-permute-start | bytes 98312 | tf_op jit(solution)/shard_map/ppermute | solution.py:19
  144.3 5.8 %collective-permute-start.29 = (f32[2,1,16,256]{3,2,1,0:T(8,128)S(1)}, f32[2,1,16,256]{3,2,1,0:T(8,128)S(1)}, u32[]{:S(2)}, u32[]{:S(2)}) collective-permute-start(f32[2,1,16,256]{3,2,1,0:T(8,128)S(1)} %slice.848), channel_id=1, source_target_pairs={{0,8},{8,16},{16,24},{1,9},{9,17},{17,25},{2,10},{10,18},{18,26},{... | collective-permute-start | bytes 98312 | tf_op jit(solution)/shard_map/ppermute | solution.py:19
where the time goes:
time: 154 us; the launch traced here: 153 us
  waiting for transfers between devices  66.7 us (43%)
  starting transfers between devices  58.3 us (38%)
  other arithmetic  16.6 us (11%)
  local copies, waits for them, and re-layouts  9.58 us (6%)
  between operations  1.72 us (1%)
    ppermute x30, waiting for transfers between devices, from_behind(): lax.ppermute(value, axis, [(source, source + steps) for source in range(i...  66.7 us
    ppermute x30, starting transfers between devices, from_behind(): lax.ppermute(value, axis, [(source, source + steps) for source in range(i...  58.3 us
    sub x5, other arithmetic, body(): e_keep * efield + e_gain * curl_backward(hfield, movers)  5.98 us
  transfers between devices with their start and end apart: 30, of which 14 were waited for; matrix products, arithmetic and copies ran while one was open for 8% of the time, Pallas kernels for 0%

commit v1 on v0

v1 whole, which is shorter than its diff:
```python
import functools
import jax
import jax.numpy as jnp
from jax import lax
from jax.experimental import pallas as pl
from jax.experimental.pallas import tpu as pltpu
from jax.sharding import PartitionSpec as P

STEPS = 5
NPML = 8
DT = 0.5
DAMPING = 0.1
STRENGTH = 3.0
SMAX = 0.8
DENOM = 1.0 + DAMPING * DT / 2.0
KEEP = (1.0 - DAMPING * DT / 2.0) / DENOM

LANES = 128
ROWS = 8
SLOT = 8
GUARD = 8
VMEM_LIMIT = 56 * 1024 * 1024

EX, HX, PX, EPS, RES = 0, 3, 6, 9, 10
ARRAYS = 11


def faces(count):
    up, down = [], []
    last = count - STEPS
    for c in range(3):
        up.append((EX + c, last, STEPS))
        down.append((EX + c, 0, STEPS if c > 0 else STEPS - 1))
    for c in range(3):
        up.append((HX + c, last if c > 0 else last + 1, STEPS if c > 0 else STEPS - 1))
        down.append((HX + c, 0, STEPS - 1))
    for c in range(3):
        up.append((PX + c, last + 1, STEPS - 1))
        down.append((PX + c, 0, STEPS - 1 if c > 0 else STEPS - 2))
    for a in (EPS, RES):
        up.append((a, last + 1, STEPS - 1))
        down.append((a, 0, STEPS - 1))
    return up, down


def planes_of(parts):
    return sum(count for _, _, count in parts)


def pick(refs, array):
    e_ref, h_ref, p_ref, eps_ref, res_ref = refs
    if array < HX:
        return e_ref.at[array]
    if array < PX:
        return h_ref.at[array - HX]
    if array < EPS:
        return p_ref.at[array - PX]
    return eps_ref if array == EPS else res_ref


def pack_faces(e_ref, h_ref, p_ref, eps_ref, freq_ref, mark_ref, up_ref, down_ref, side_ref, res_ref):
    xcount, zcount, ycount = eps_ref.shape
    core = lax.axis_index("gz")
    for z in range(0, zcount, ROWS):
        for j in range(ycount // LANES):
            lanes = slice(j * LANES, (j + 1) * LANES)
            mark = mark_ref[:, z : z + ROWS, j : j + 1].astype(jnp.float32)
            freq = freq_ref[:, z : z + ROWS, lanes] * DT
            res_ref[:, z : z + ROWS, lanes] = mark * (freq * freq / DENOM)
    refs = (e_ref, h_ref, p_ref, eps_ref, res_ref)
    for parts, out_ref in zip(faces(xcount), (up_ref, down_ref)):
        at = 0
        for array, first, count in parts:
            out_ref[at : at + count] = pick(refs, array)[first : first + count]
            at += count
    begin = pl.multiple_of((1 - core) * (zcount - ROWS), ROWS)
    for array in range(ARRAYS):
        side_ref[array] = pick(refs, array)[:, pl.ds(begin, ROWS), :]


def pack_strips(e_ref, h_ref, p_ref, eps_ref, res_ref, side_ref, low_ref, high_ref):
    xcount, zcount, ycount = eps_ref.shape
    core = lax.axis_index("gz")
    refs = (e_ref, h_ref, p_ref, eps_ref, res_ref)
    own = pl.multiple_of(core * ROWS, ROWS)
    halo = pl.multiple_of((1 - core) * zcount, ROWS)
    slot = lax.broadcasted_iota(jnp.int32, (ROWS, LANES), 1) // SLOT
    for array in range(ARRAYS):
        src = pick(refs, array)
        for z in range(0, zcount + ROWS, ROWS):
            low = high = jnp.zeros((ROWS, LANES), jnp.float32)
            for x in range(xcount):
                if z < zcount:
                    first, last = src[x, z : z + ROWS, 0:LANES], src[x, z : z + ROWS, ycount - LANES : ycount]
                else:
                    first, last = side_ref[array, x, :, 0:LANES], side_ref[array, x, :, ycount - LANES : ycount]
                here = slot == x
                low = jnp.where(here, pltpu.roll(first, SLOT * x, 1) if x else first, low)
                shift = (SLOT * x + SLOT) % LANES
                high = jnp.where(here, pltpu.roll(last, shift, 1) if shift else last, high)
            rows = pl.ds(own + z, ROWS) if z < zcount else pl.ds(halo, ROWS)
            low_ref[array, rows, :] = low
            high_ref[array, rows, :] = high


def pack_corners(ahead_ref, behind_ref, up_ref, down_ref):
    wide = STEPS * SLOT
    lane = lax.broadcasted_iota(jnp.int32, (1, 1, LANES), 2)
    ahead, behind = ahead_ref[...], behind_ref[...]
    up_ref[...] = jnp.where(lane >= LANES - wide, ahead, pltpu.roll(behind, wide, 2))
    down_ref[...] = jnp.where(lane < wide, ahead, pltpu.roll(behind, LANES - wide, 2))


def profile(index, total):
    depth = jnp.maximum(NPML - index, 0.0) + jnp.maximum(index - (total - 1 - NPML), 0.0)
    return SMAX * (depth / NPML) ** 3


def turn(value, shift):
    shift = shift % LANES
    return pltpu.roll(value, shift, 1) if shift else value


def advance(
    e_ref, h_ref, p_ref, eps_ref, res_ref, side_ref, low_ref, low_side_ref, high_ref, high_side_ref,
    ahead_ref, behind_ref, corner_low_ref, corner_high_ref, e_out, h_out,
    E, H, R, U, EC, EB, BM, HC, HB,
):
    xcount, zcount, ycount = eps_ref.shape
    tiles = ycount // LANES
    core = lax.axis_index("gz")
    xplace = lax.axis_index("gx") * xcount
    yplace = lax.axis_index("gy") * ycount
    xtotal = xcount * lax.axis_size("gx")
    ytotal = ycount * lax.axis_size("gy")
    own = pl.multiple_of(GUARD + core * ROWS, ROWS)
    halo = pl.multiple_of(GUARD + (1 - core) * zcount, ROWS)
    near = pl.multiple_of(core * (zcount - ROWS), ROWS)
    zsteps = (zcount + ROWS) // ROWS
    lane = lax.broadcasted_iota(jnp.int32, (ROWS, LANES), 1)
    is_ahead, is_behind = lane < SLOT, lane >= LANES - SLOT
    wide = STEPS * SLOT

    def put(array, plane, row, j, value):
        if array < HX:
            E[array, plane, j, pl.ds(row, ROWS), :] = value
        elif array < PX:
            H[array - HX, plane, j, pl.ds(row, ROWS), :] = value * (1.0 / 6.0)
        elif array < EPS:
            R[array - PX, plane, j, pl.ds(row, ROWS), :] = value * (1.0 / 3.0)
        elif array == EPS:
            EC[plane, j, pl.ds(row, ROWS), :] = value
        else:
            BM[plane, j, pl.ds(row, ROWS), :] = value

    refs = (e_ref, h_ref, p_ref, eps_ref, res_ref)
    for array in range(ARRAYS):
        src = pick(refs, array)

        def own_plane(x, _, array=array, src=src):
            for j in range(tiles):
                lanes = slice(j * LANES, (j + 1) * LANES)
                for z in range(0, zcount, ROWS):
                    put(array, x + STEPS, own + z, j, src[x, z : z + ROWS, lanes])
                put(array, x + STEPS, halo, j, side_ref[array, x, :, lanes])
            return _

        lax.fori_loop(0, xcount, own_plane, 0, unroll=4)
        for x in range(xcount):
            for t in range(zsteps):
                rows = slice(t * ROWS, (t + 1) * ROWS)
                a = turn(ahead_ref[array, rows, :], -SLOT * x)
                b = turn(behind_ref[array, rows, :], LANES - SLOT - SLOT * x)
                put(array, x + STEPS, GUARD + t * ROWS, tiles, jnp.where(is_ahead, a, jnp.where(is_behind, b, 0.0)))
    ups, downs = faces(xcount)
    for parts, face, face_side, corner, above in (
        (ups, low_ref, low_side_ref, corner_low_ref, False),
        (downs, high_ref, high_side_ref, corner_high_ref, True),
    ):
        at = 0
        for array, first, count in parts:
            base = xcount + STEPS if above else first + STEPS - xcount
            for i in range(count):
                plane = base + i
                for j in range(tiles):
                    lanes = slice(j * LANES, (j + 1) * LANES)
                    for z in range(0, zcount, ROWS):
                        put(array, plane, own + z, j, face[at + i, z : z + ROWS, lanes])
                    put(array, plane, halo, j, face_side[at + i, pl.ds(near, ROWS), lanes])
                slot = plane - (xcount + STEPS) if above else plane
                for t in range(zsteps):
                    rows = slice(t * ROWS, (t + 1) * ROWS)
                    c = corner[array, rows, :]
                    if above:
                        a, b = turn(c, -SLOT * slot), turn(c, (LANES - SLOT) - (LANES - wide + SLOT * slot))
                    else:
                        a, b = turn(c, -(LANES - wide + SLOT * slot)), turn(c, (LANES - SLOT) - SLOT * slot)
                    put(array, plane, GUARD + t * ROWS, tiles, jnp.where(is_ahead, a, jnp.where(is_behind, b, 0.0)))
            at += count
    extent = xcount + 2 * STEPS
    for j in range(tiles + 1):
        for t in range(zsteps):
            rows = pl.ds(GUARD + t * ROWS, ROWS)
            H[0, 0, j, rows, :] = jnp.zeros((ROWS, LANES), jnp.float32)
            E[0, extent - 1, j, rows, :] = jnp.zeros((ROWS, LANES), jnp.float32)
            R[0, extent - 2, j, rows, :] = jnp.zeros((ROWS, LANES), jnp.float32)

    def guards(x, _):
        for j in range(tiles + 1):
            for c in range(3):
                H[c, x, j, 0:GUARD, :] = jnp.zeros((ROWS, LANES), jnp.float32)
                E[c, x, j, GUARD + zcount + ROWS : GUARD + zcount + 2 * ROWS, :] = jnp.zeros((ROWS, LANES), jnp.float32)
        return _

    lax.fori_loop(0, extent, guards, 0)

    def coefficients(x, _):
        xpos = xplace + x - STEPS
        xin = (xpos >= 0) & (xpos < xtotal)
        xsigma = profile(jnp.full((ROWS, LANES), xpos, jnp.int32).astype(jnp.float32), xtotal)
        for j in range(tiles + 1):
            if j < tiles:
                ypos = yplace + j * LANES + lane
                inside = jnp.full((ROWS, LANES), xin)
            else:
                ypos = yplace + jnp.where(lane < SLOT, ycount + lane, lane - LANES)
                inside = (is_ahead | is_behind) & (ypos >= 0) & (ypos < ytotal) & xin
            half = (xsigma + profile(ypos.astype(jnp.float32), ytotal)) * (DT / 2.0)
            over = 1.0 / (1.0 + half)
            HC[x, j] = jnp.where(inside, (1.0 - half) * over, 0.0)
            HB[x, j] = jnp.where(inside, (DT / 6.0) * over, 0.0)
            for t in range(zsteps):
                rows = pl.ds(GUARD + t * ROWS, ROWS)
                eps = EC[x, j, rows, :]
                over = 1.0 / jnp.where(inside, eps + half, 1.0)
                EC[x, j, rows, :] = jnp.where(inside, (eps - half) * over, 0.0)
                EB[x, j, rows, :] = jnp.where(inside, (6.0 * DT) * over, 0.0)
        return _

    lax.fori_loop(1, extent - 1, coefficients, 0)
    xpos = xplace - STEPS
    xsigma = profile(jnp.full((ROWS, LANES), xpos, jnp.int32).astype(jnp.float32), xtotal)
    for j in range(tiles + 1):
        if j < tiles:
            ypos = yplace + j * LANES + lane
            inside = jnp.full((ROWS, LANES), xpos >= 0)
        else:
            ypos = yplace + jnp.where(lane < SLOT, ycount + lane, lane - LANES)
            inside = (is_ahead | is_behind) & (ypos >= 0) & (ypos < ytotal) & (xpos >= 0)
        half = (xsigma + profile(ypos.astype(jnp.float32), ytotal)) * (DT / 2.0)
        over = 1.0 / (1.0 + half)
        HC[0, j] = jnp.where(inside, (1.0 - half) * over, 0.0)
        HB[0, j] = jnp.where(inside, (DT / 6.0) * over, 0.0)

    last_lane, first_lane = lane == LANES - 1, lane == 0

    def next_lane(v):
        r = [pltpu.roll(t, LANES - 1, 1) for t in v]
        return [jnp.where(last_lane, r[(j + 1) % len(v)], r[j]) for j in range(len(v))]

    def previous_lane(v):
        r = [pltpu.roll(t, 1, 1) for t in v]
        return [jnp.where(first_lane, r[j - 1], r[j]) for j in range(len(v))]

    def load(ref, c, x, row):
        return [ref[c, x, j, pl.ds(row, ROWS), :] for j in range(tiles + 1)]

    def magnetic(x):
        for t in range(zsteps):
            row = GUARD + t * ROWS
            ex, ey, ez = (load(E, c, x, row) for c in range(3))
            ex_z, ey_z = (load(E, c, x, row + 1) for c in (0, 1))
            ey_x, ez_x = (load(E, c, x + 1, row) for c in (1, 2))
            ex_y, ez_y = next_lane(ex), next_lane(ez)
            for j in range(tiles + 1):
                hc, hb = HC[x, j], HB[x, j]
                rows = pl.ds(row, ROWS)
                H[0, x, j, rows, :] = hc * H[0, x, j, rows, :] - hb * ((ez_y[j] - ez[j]) - (ey_z[j] - ey[j]))
                H[1, x, j, rows, :] = hc * H[1, x, j, rows, :] - hb * ((ex_z[j] - ex[j]) - (ez_x[j] - ez[j]))
                H[2, x, j, rows, :] = hc * H[2, x, j, rows, :] - hb * ((ey_x[j] - ey[j]) - (ex_y[j] - ex[j]))

    def electric(x, first):
        for t in range(zsteps):
            row = GUARD + t * ROWS
            hx, hy, hz = (load(H, c, x, row) for c in range(3))
            hx_z, hy_z = (load(H, c, x, row - 1) for c in (0, 1))
            hy_x, hz_x = (load(H, c, x - 1, row) for c in (1, 2))
            hx_y, hz_y = previous_lane(hx), previous_lane(hz)
            for j in range(tiles + 1):
                rows = pl.ds(row, ROWS)
                ec, eb, bm = EC[x, j, rows, :], EB[x, j, rows, :], BM[x, j, rows, :]
                curls = (
                    (hz[j] - hz_y[j]) - (hy[j] - hy_z[j]),
                    (hx[j] - hx_z[j]) - (hz[j] - hz_x[j]),
                    (hy[j] - hy_x[j]) - (hx[j] - hx_y[j]),
                )
                for c in range(3):
                    e, r = E[c, x, j, rows, :], R[c, x, j, rows, :]
                    u = bm * (e - r)
                    if not first:
                        u = KEEP * U[c, x, j, rows, :] + u
                    U[c, x, j, rows, :] = u
                    R[c, x, j, rows, :] = r + u
                    E[c, x, j, rows, :] = ec * e + eb * (curls[c] - u)

    for step in range(1, STEPS + 1):
        reach = STEPS - step

        def sweep_h(x, _):
            magnetic(x)
            return _

        def sweep_e(x, _, first=step == 1):
            electric(x, first)
            return _

        lax.fori_loop(step - 1, STEPS + xcount + reach, sweep_h, 0)
        lax.fori_loop(step, STEPS + xcount + reach, sweep_e, 0)

    def finish(x, _):
        for c in range(3):
            for j in range(tiles):
                lanes = slice(j * LANES, (j + 1) * LANES)
                for z in range(0, zcount, ROWS):
                    e_out[c, x, z : z + ROWS, lanes] = E[c, x + STEPS, j, pl.ds(own + z, ROWS), :]
                    h_out[c, x, z : z + ROWS, lanes] = H[c, x + STEPS, j, pl.ds(own + z, ROWS), :] * 6.0
        return _

    lax.fori_loop(0, xcount, finish, 0)


def call(kernel, outs, args, scratch=()):
    return pl.pallas_call(
        kernel,
        out_shape=[jax.ShapeDtypeStruct(s, jnp.float32) for s in outs],
        in_specs=[pl.BlockSpec(memory_space=pltpu.VMEM)] * len(args),
        out_specs=[pl.BlockSpec(memory_space=pltpu.VMEM)] * len(outs),
        scratch_shapes=[pltpu.VMEM(s, jnp.float32) for s in scratch],
        compiler_params=pltpu.CompilerParams(vmem_limit_bytes=VMEM_LIMIT),
    )(*args)


def shift(value, axis, by):
    count = lax.axis_size(axis)
    return lax.ppermute(value, axis, [(i, i + by) for i in range(count) if 0 <= i + by < count])


def swap(value):
    return lax.ppermute(value, "gz", [(0, 1), (1, 0)])


def body(e_field, h_field, polar, permittivity, resonance, dispersive):
    xcount, zcount, ycount = permittivity.shape
    ups, downs = faces(xcount)
    up, down, side, res = call(
        pack_faces,
        [
            (planes_of(ups), zcount, ycount),
            (planes_of(downs), zcount, ycount),
            (ARRAYS, xcount, ROWS, ycount),
            (xcount, zcount, ycount),
        ],
        (e_field, h_field, polar, permittivity, resonance, dispersive),
    )
    low, high = shift(up, "gx", 1), shift(down, "gx", -1)
    side = swap(side)
    strip = (ARRAYS, zcount + ROWS, LANES)
    first, last = call(pack_strips, [strip, strip], (e_field, h_field, polar, permittivity, res, side))
    ahead, behind = shift(first, "gy", -1), shift(last, "gy", 1)
    corner_up, corner_down = call(pack_corners, [strip, strip], (ahead, behind))
    corner_low, corner_high = shift(corner_up, "gx", 1), shift(corner_down, "gx", -1)
    low_side, high_side = swap(low), swap(high)
    extent, tiles = xcount + 2 * STEPS, ycount // LANES + 1
    rows = zcount + ROWS + 2 * GUARD
    field, plane = (3, extent, tiles, rows, LANES), (extent, tiles, rows, LANES)
    flat = (extent, tiles, ROWS, LANES)
    return tuple(
        call(
            advance,
            [e_field.shape, h_field.shape],
            (
                e_field, h_field, polar, permittivity, res, side, low, low_side, high, high_side,
                ahead, behind, corner_low, corner_high,
            ),
            [field] * 4 + [plane] * 3 + [flat] * 2,
        )
    )


def solution(mesh):
    field, cell = P(None, "gx", "gz", "gy"), P("gx", "gz", "gy")
    return jax.shard_map(
        body,
        mesh=mesh,
        in_specs=(field, field, field, cell, cell, cell),
        out_specs=(field, field),
        check_vma=False,
    )
```

time: 154 us -> 89.7 us (0.58)
  the two profiles are of different devices: /device:TPU:24 before, /device:TPU:4 now
where the time goes in v1:
time: 89.7 us; the launch traced here: 89.3 us
  Pallas kernels  37.8 us (42%)
  waiting for transfers between devices  31.4 us (35%)
  starting transfers between devices  15.4 us (17%)
  local copies, waits for them, and re-layouts  4.01 us (4%)
    pallas_call x4, Pallas kernels, call(): pl.pallas_call(kernel, out_shape=[jax.ShapeDtypeStruct(s, jnp.float32) fo...  37.8 us
    ppermute x6, waiting for transfers between devices, shift(): lax.ppermute(value, axis, [(i, i + by) for i in range(count) if 0 <= i +...  31.4 us
    ppermute x6, starting transfers between devices, shift(): lax.ppermute(value, axis, [(i, i + by) for i in range(count) if 0 <= i +...  15.4 us
    unnamed x19, local copies, waits for them, and re-layouts  4.01 us
  transfers between devices with their start and end apart: 9, of which 6 were waited for; matrix products, arithmetic and copies ran while one was open for 0% of the time, Pallas kernels for 7%

profile of v1, /device:TPU:4, one launch (start us, length us, event | category | flops | bytes accessed | tf_op | source)
XLA Modules:
  0.0 89.3 jit_solution(6592712700238802724)
XLA Ops:
  0.6 1.5 %copy.8.mark_ref = s32[16,16,2]{2,1,0:T(8,128)} copy(s32[16,16,2]{1,2,0:T(2,128)} %param.11) | data formatting | bytes 4096 | tf_op args[5]
  2.2 3.6 %shard_map.77 = (f32[49,16,256]{2,1,0:T(8,128)}, f32[45,16,256]{2,1,0:T(8,128)}, f32[11,16,8,256]{3,2,1,0:T(8,128)}, f32[16,16,256]{2,1,0:T(8,128)}) custom-call(f32[3,16,16,256]{3,2,1,0:T(8,128)} %e_ref.5, f32[3,16,16,256]{3,2,1,0:T(8,128)} %h_ref.5, f32[3,16,16,256]{3,2,1,0:T(8,128)} %p_ref.5, f32[16,16,256]{2,1,0:T(8,128)} %eps_ref.5, ...), custom_call_target="tpu_custom_call" | custom-call | tf_op jit(solution)/shard_map/pallas_call | solution.py:333
  5.8 0.0 collective-permute-start
  5.8 3.5 %collective-permute-start.1 = (f32[49,16,256]{2,1,0:T(8,128)}, f32[49,16,256]{2,1,0:T(8,128)S(1)}, u32[]{:S(2)}, u32[]{:S(2)}) collective-permute-start(f32[49,16,256]{2,1,0:T(8,128)} %get-tuple-element.12), channel_id=1, source_target_pairs={{0,8},{8,16},{16,24},{1,9},{9,17},{17,25},{2,10},{10,18},{18,26},{... | collective-permute-start | bytes 2408456 | tf_op jit(solution)/shard_map/ppermute | solution.py:345
  9.3 1.3 %collective-permute-start.3 = (f32[45,16,256]{2,1,0:T(8,128)}, f32[45,16,256]{2,1,0:T(8,128)S(1)}, u32[]{:S(2)}, u32[]{:S(2)}) collective-permute-start(f32[45,16,256]{2,1,0:T(8,128)} %get-tuple-element.13), channel_id=1, source_target_pairs={{8,0},{16,8},{24,16},{9,1},{17,9},{25,17},{10,2},{18,10},{26,18},{... | collective-permute-start | bytes 2211848 | tf_op jit(solution)/shard_map/ppermute | solution.py:345
  10.6 16.8 %collective-permute-done.1.low_ref = f32[49,16,256]{2,1,0:T(8,128)S(1)} collective-permute-done((f32[49,16,256]{2,1,0:T(8,128)}, f32[49,16,256]{2,1,0:T(8,128)S(1)}, u32[]{:S(2)}, u32[]{:S(2)}) %collective-permute-start.1) | collective-permute-done | bytes 802848 | tf_op jit(solution)/shard_map/ppermute | solution.py:345
  27.4 0.0 copy-start.1
  27.4 0.0 collective-permute-start.2
  27.4 2.6 %collective-permute-done.3.high_ref = f32[45,16,256]{2,1,0:T(8,128)S(1)} collective-permute-done((f32[45,16,256]{2,1,0:T(8,128)}, f32[45,16,256]{2,1,0:T(8,128)S(1)}, u32[]{:S(2)}, u32[]{:S(2)}) %collective-permute-start.3) | collective-permute-done | bytes 737312 | tf_op jit(solution)/shard_map/ppermute | solution.py:345
  30.1 0.0 copy-start.3
  30.1 0.0 collective-permute-start.4
  30.1 0.0 collective-permute-done.side_ref
  30.1 0.0 copy-start
  30.1 1.1 %copy-done = f32[11,16,8,256]{3,2,1,0:T(8,128)} copy-done((f32[11,16,8,256]{3,2,1,0:T(8,128)}, f32[11,16,8,256]{3,2,1,0:T(8,128)S(1)}, u32[]{:S(2)}) %copy-start) | copy-done | bytes 1441816
  31.2 4.0 %shard_map.78 = (f32[11,24,128]{2,1,0:T(8,128)}, f32[11,24,128]{2,1,0:T(8,128)}) custom-call(f32[3,16,16,256]{3,2,1,0:T(8,128)} %e_ref.5, f32[3,16,16,256]{3,2,1,0:T(8,128)} %h_ref.5, f32[3,16,16,256]{3,2,1,0:T(8,128)} %p_ref.5, f32[16,16,256]{2,1,0:T(8,128)} %eps_ref.5, f32[16,16,256]{2,1,0:T(8,128)} %get-tuple-element.10.res_ref, f32[11,16,8,256]{3,2,1,0:T(8,128)} %copy-done), custom_call_target="tpu_custom_call" | custom-call | tf_op jit(solution)/shard_map/pallas_call | solution.py:333
  35.3 3.3 %collective-permute-start.5 = (f32[11,24,128]{2,1,0:T(8,128)}, f32[11,24,128]{2,1,0:T(8,128)S(1)}, u32[]{:S(2)}, u32[]{:S(2)}) collective-permute-start(f32[11,24,128]{2,1,0:T(8,128)} %get-tuple-element.14), channel_id=1, source_target_pairs={{2,0},{4,2},{6,4},{3,1},{5,3},{7,5},{10,8},{12,10},{14,12},{11,9},... | collective-permute-start | bytes 405512 | tf_op jit(solution)/shard_map/ppermute | solution.py:345
  38.6 2.5 %collective-permute-start.6 = (f32[11,24,128]{2,1,0:T(8,128)}, f32[11,24,128]{2,1,0:T(8,128)S(1)}, u32[]{:S(2)}, u32[]{:S(2)}) collective-permute-start(f32[11,24,128]{2,1,0:T(8,128)} %get-tuple-element.15), channel_id=1, source_target_pairs={{0,2},{2,4},{4,6},{1,3},{3,5},{5,7},{8,10},{10,12},{12,14},{9,11},... | collective-permute-start | bytes 405512 | tf_op jit(solution)/shard_map/ppermute | solution.py:345
  41.1 2.2 %collective-permute-done.5.ahead_ref = f32[11,24,128]{2,1,0:T(8,128)S(1)} collective-permute-done((f32[11,24,128]{2,1,0:T(8,128)}, f32[11,24,128]{2,1,0:T(8,128)S(1)}, u32[]{:S(2)}, u32[]{:S(2)}) %collective-permute-start.5) | collective-permute-done | bytes 135200 | tf_op jit(solution)/shard_map/ppermute | solution.py:345
  43.3 0.0 copy-start.5
  43.3 4.0 %collective-permute-done.6.behind_ref = f32[11,24,128]{2,1,0:T(8,128)S(1)} collective-permute-done((f32[11,24,128]{2,1,0:T(8,128)}, f32[11,24,128]{2,1,0:T(8,128)S(1)}, u32[]{:S(2)}, u32[]{:S(2)}) %collective-permute-start.6) | collective-permute-done | bytes 135200 | tf_op jit(solution)/shard_map/ppermute | solution.py:345
  47.3 0.0 copy-done.5
  47.3 0.0 copy-start.6
  47.3 0.7 copy-done.6
  47.9 1.8 %shard_map.79 = (f32[11,24,128]{2,1,0:T(8,128)}, f32[11,24,128]{2,1,0:T(8,128)}) custom-call(f32[11,24,128]{2,1,0:T(8,128)} %copy-done.5, f32[11,24,128]{2,1,0:T(8,128)} %copy-done.6), custom_call_target="tpu_custom_call" | custom-call | tf_op jit(solution)/shard_map/pallas_call | solution.py:333
  49.7 3.4 %collective-permute-start.7 = (f32[11,24,128]{2,1,0:T(8,128)}, f32[11,24,128]{2,1,0:T(8,128)S(1)}, u32[]{:S(2)}, u32[]{:S(2)}) collective-permute-start(f32[11,24,128]{2,1,0:T(8,128)} %get-tuple-element.16), channel_id=1, source_target_pairs={{0,8},{8,16},{16,24},{1,9},{9,17},{17,25},{2,10},{10,18},{18,26},{... | collective-permute-start | bytes 405512 | tf_op jit(solution)/shard_map/ppermute | solution.py:345
  53.2 1.3 %collective-permute-start.8 = (f32[11,24,128]{2,1,0:T(8,128)}, f32[11,24,128]{2,1,0:T(8,128)S(1)}, u32[]{:S(2)}, u32[]{:S(2)}) collective-permute-start(f32[11,24,128]{2,1,0:T(8,128)} %get-tuple-element.17), channel_id=1, source_target_pairs={{8,0},{16,8},{24,16},{9,1},{17,9},{25,17},{10,2},{18,10},{26,18},{... | collective-permute-start | bytes 405512 | tf_op jit(solution)/shard_map/ppermute | solution.py:345
  54.5 0.0 collective-permute-done.4.high_side_ref
  54.5 0.0 copy-start.4
  54.5 0.0 collective-permute-done.2.low_side_ref
  54.5 0.0 copy-start.2
  54.5 1.5 %collective-permute-done.7.corner_low_ref = f32[11,24,128]{2,1,0:T(8,128)S(1)} collective-permute-done((f32[11,24,128]{2,1,0:T(8,128)}, f32[11,24,128]{2,1,0:T(8,128)S(1)}, u32[]{:S(2)}, u32[]{:S(2)}) %collective-permute-start.7) | collective-permute-done | bytes 135200 | tf_op jit(solution)/shard_map/ppermute | solution.py:345
  56.0 0.0 copy-start.7
  56.0 4.3 %collective-permute-done.8.corner_high_ref = f32[11,24,128]{2,1,0:T(8,128)S(1)} collective-permute-done((f32[11,24,128]{2,1,0:T(8,128)}, f32[11,24,128]{2,1,0:T(8,128)S(1)}, u32[]{:S(2)}, u32[]{:S(2)}) %collective-permute-start.8) | collective-permute-done | bytes 135200 | tf_op jit(solution)/shard_map/ppermute | solution.py:345
  60.3 0.0 copy-done.1
  60.3 0.0 copy-done.3
  60.3 0.0 copy-done.4
  60.3 0.0 copy-done.2
  60.3 0.0 copy-done.7
  60.3 0.0 copy-start.8
  60.3 0.7 copy-done.8
  61.0 28.4 %shard_map.80 = (f32[3,16,16,256]{3,2,1,0:T(8,128)}, f32[3,16,16,256]{3,2,1,0:T(8,128)}) custom-call(f32[3,16,16,256]{3,2,1,0:T(8,128)} %e_ref.5, f32[3,16,16,256]{3,2,1,0:T(8,128)} %h_ref.5, f32[3,16,16,256]{3,2,1,0:T(8,128)} %p_ref.5, f32[16,16,256]{2,1,0:T(8,128)} %eps_ref.5, f32[16,16,256]{2,1,0:T(8,128)} %get-tuple-element.10.res_ref, ...), custom_call_target="tpu_custom_call" | custom-call | tf_op jit(solution)/shard_map/pallas_call | solution.py:333
Async XLA Ops:
  5.8 24.3 %collective-permute-start = (f32[11,16,8,256]{3,2,1,0:T(8,128)}, f32[11,16,8,256]{3,2,1,0:T(8,128)S(1)}, u32[]{:S(2)}, u32[]{:S(2)}) collective-permute-start(f32[11,16,8,256]{3,2,1,0:T(8,128)} %get-tuple-element.11), channel_id=1, source_target_pairs={{0,1},{1,0},{2,3},{3,2},{4,5},{5,4},{6,7},{7,6},{8,9},{9,8},{10,11... | collective-permute-start | bytes 4325384 | tf_op jit(solution)/shard_map/ppermute | solution.py:349
  5.8 21.6 %collective-permute-start.1 = (f32[49,16,256]{2,1,0:T(8,128)}, f32[49,16,256]{2,1,0:T(8,128)S(1)}, u32[]{:S(2)}, u32[]{:S(2)}) collective-permute-start(f32[49,16,256]{2,1,0:T(8,128)} %get-tuple-element.12), channel_id=1, source_target_pairs={{0,8},{8,16},{16,24},{1,9},{9,17},{17,25},{2,10},{10,18},{18,26},{... | collective-permute-start | bytes 2408456 | tf_op jit(solution)/shard_map/ppermute | solution.py:345
  9.3 20.7 %collective-permute-start.3 = (f32[45,16,256]{2,1,0:T(8,128)}, f32[45,16,256]{2,1,0:T(8,128)S(1)}, u32[]{:S(2)}, u32[]{:S(2)}) collective-permute-start(f32[45,16,256]{2,1,0:T(8,128)} %get-tuple-element.13), channel_id=1, source_target_pairs={{8,0},{16,8},{24,16},{9,1},{17,9},{25,17},{10,2},{18,10},{26,18},{... | collective-permute-start | bytes 2211848 | tf_op jit(solution)/shard_map/ppermute | solution.py:345
  27.4 32.9 %copy-start.1 = (f32[49,16,256]{2,1,0:T(8,128)}, f32[49,16,256]{2,1,0:T(8,128)S(1)}, u32[]{:S(2)}) copy-start(f32[49,16,256]{2,1,0:T(8,128)S(1)} %collective-permute-done.1.low_ref) | copy-start | bytes 2408452
  27.4 27.1 %collective-permute-start.2 = (f32[49,16,256]{2,1,0:T(8,128)S(1)}, f32[49,16,256]{2,1,0:T(8,128)S(1)}, u32[]{:S(2)}, u32[]{:S(2)}) collective-permute-start(f32[49,16,256]{2,1,0:T(8,128)S(1)} %collective-permute-done.1.low_ref), channel_id=1, source_target_pairs={{0,1},{1,0},{2,3},{3,2},{4,5},{5,4},{6,7},{7,6},{8,9},{9,8},{10,11... | collective-permute-start | bytes 2408456 | tf_op jit(solution)/shard_map/ppermute | solution.py:349
  30.1 30.2 %copy-start.3 = (f32[45,16,256]{2,1,0:T(8,128)}, f32[45,16,256]{2,1,0:T(8,128)S(1)}, u32[]{:S(2)}) copy-start(f32[45,16,256]{2,1,0:T(8,128)S(1)} %collective-permute-done.3.high_ref) | copy-start | bytes 2211844
  30.1 24.4 %collective-permute-start.4 = (f32[45,16,256]{2,1,0:T(8,128)S(1)}, f32[45,16,256]{2,1,0:T(8,128)S(1)}, u32[]{:S(2)}, u32[]{:S(2)}) collective-permute-start(f32[45,16,256]{2,1,0:T(8,128)S(1)} %collective-permute-done.3.high_ref), channel_id=1, source_target_pairs={{0,1},{1,0},{2,3},{3,2},{4,5},{5,4},{6,7},{7,6},{8,9},{9,8},{10,11... | collective-permute-start | bytes 2211848 | tf_op jit(solution)/shard_map/ppermute | solution.py:349
  30.1 1.2 %copy-start = (f32[11,16,8,256]{3,2,1,0:T(8,128)}, f32[11,16,8,256]{3,2,1,0:T(8,128)S(1)}, u32[]{:S(2)}) copy-start(f32[11,16,8,256]{3,2,1,0:T(8,128)S(1)} %collective-permute-done.side_ref) | copy-start | bytes 4325380
  35.3 8.0 %collective-permute-start.5 = (f32[11,24,128]{2,1,0:T(8,128)}, f32[11,24,128]{2,1,0:T(8,128)S(1)}, u32[]{:S(2)}, u32[]{:S(2)}) collective-permute-start(f32[11,24,128]{2,1,0:T(8,128)} %get-tuple-element.14), channel_id=1, source_target_pairs={{2,0},{4,2},{6,4},{3,1},{5,3},{7,5},{10,8},{12,10},{14,12},{11,9},... | collective-permute-start | bytes 405512 | tf_op jit(solution)/shard_map/ppermute | solution.py:345
  38.6 8.7 %collective-permute-start.6 = (f32[11,24,128]{2,1,0:T(8,128)}, f32[11,24,128]{2,1,0:T(8,128)S(1)}, u32[]{:S(2)}, u32[]{:S(2)}) collective-permute-start(f32[11,24,128]{2,1,0:T(8,128)} %get-tuple-element.15), channel_id=1, source_target_pairs={{0,2},{2,4},{4,6},{1,3},{3,5},{5,7},{8,10},{10,12},{12,14},{9,11},... | collective-permute-start | bytes 405512 | tf_op jit(solution)/shard_map/ppermute | solution.py:345
  43.3 4.0 %copy-start.5 = (f32[11,24,128]{2,1,0:T(8,128)}, f32[11,24,128]{2,1,0:T(8,128)S(1)}, u32[]{:S(2)}) copy-start(f32[11,24,128]{2,1,0:T(8,128)S(1)} %collective-permute-done.5.ahead_ref) | copy-start | bytes 405508
  47.3 0.7 copy-start.6
  49.7 6.3 %collective-permute-start.7 = (f32[11,24,128]{2,1,0:T(8,128)}, f32[11,24,128]{2,1,0:T(8,128)S(1)}, u32[]{:S(2)}, u32[]{:S(2)}) collective-permute-start(f32[11,24,128]{2,1,0:T(8,128)} %get-tuple-element.16), channel_id=1, source_target_pairs={{0,8},{8,16},{16,24},{1,9},{9,17},{17,25},{2,10},{10,18},{18,26},{... | collective-permute-start | bytes 405512 | tf_op jit(solution)/shard_map/ppermute | solution.py:345
  53.2 7.1 %collective-permute-start.8 = (f32[11,24,128]{2,1,0:T(8,128)}, f32[11,24,128]{2,1,0:T(8,128)S(1)}, u32[]{:S(2)}, u32[]{:S(2)}) collective-permute-start(f32[11,24,128]{2,1,0:T(8,128)} %get-tuple-element.17), channel_id=1, source_target_pairs={{8,0},{16,8},{24,16},{9,1},{17,9},{25,17},{10,2},{18,10},{26,18},{... | collective-permute-start | bytes 405512 | tf_op jit(solution)/shard_map/ppermute | solution.py:345
  54.5 5.8 %copy-start.4 = (f32[45,16,256]{2,1,0:T(8,128)}, f32[45,16,256]{2,1,0:T(8,128)S(1)}, u32[]{:S(2)}) copy-start(f32[45,16,256]{2,1,0:T(8,128)S(1)} %collective-permute-done.4.high_side_ref) | copy-start | bytes 2211844
  54.5 5.8 %copy-start.2 = (f32[49,16,256]{2,1,0:T(8,128)}, f32[49,16,256]{2,1,0:T(8,128)S(1)}, u32[]{:S(2)}) copy-start(f32[49,16,256]{2,1,0:T(8,128)S(1)} %collective-permute-done.2.low_side_ref) | copy-start | bytes 2408452
  56.0 4.3 %copy-start.7 = (f32[11,24,128]{2,1,0:T(8,128)}, f32[11,24,128]{2,1,0:T(8,128)S(1)}, u32[]{:S(2)}) copy-start(f32[11,24,128]{2,1,0:T(8,128)S(1)} %collective-permute-done.7.corner_low_ref) | copy-start | bytes 405508
  60.3 0.7 copy-start.8

commit v2 on v0

v2 whole, which is shorter than its diff:
```python
import functools
import jax
import jax.numpy as jnp
from jax import lax
from jax.experimental import pallas as pl
from jax.experimental.pallas import tpu as pltpu
from jax.sharding import PartitionSpec as P

STEPS = 5
NPML = 8
DT = 0.5
DAMPING = 0.1
STRENGTH = 3.0
SMAX = 0.8
DENOM = 1.0 + DAMPING * DT / 2.0
KEEP = (1.0 - DAMPING * DT / 2.0) / DENOM

LANES = 128
ROWS = 8
SIDE = 8
SLOT = 2 * SIDE
GUARD = 8
VMEM_LIMIT = 8 * 1024 * 1024

EX, HX, PX, EPS, RES = 0, 3, 6, 9, 10
ARRAYS = 11

COST = 3_000_000


def faces(count):
    up, down = [], []
    last = count - STEPS
    for c in range(3):
        up.append((EX + c, last, STEPS))
        down.append((EX + c, 0, STEPS if c > 0 else STEPS - 1))
    for c in range(3):
        up.append((HX + c, last if c > 0 else last + 1, STEPS if c > 0 else STEPS - 1))
        down.append((HX + c, 0, STEPS - 1))
    for c in range(3):
        up.append((PX + c, last + 1, STEPS - 1))
        down.append((PX + c, 0, STEPS - 1 if c > 0 else STEPS - 2))
    for a in (EPS, RES):
        up.append((a, last + 1, STEPS - 1))
        down.append((a, 0, STEPS - 1))
    return up, down


def planes_of(parts):
    return sum(count for _, _, count in parts)


def pick(refs, array):
    e_ref, h_ref, p_ref, eps_ref, res_ref = refs
    if array < HX:
        return e_ref.at[array]
    if array < PX:
        return h_ref.at[array - HX]
    if array < EPS:
        return p_ref.at[array - PX]
    return eps_ref if array == EPS else res_ref


def pack_faces(e_ref, h_ref, p_ref, eps_ref, freq_ref, mark_ref, up_ref, down_ref, side_ref, res_ref):
    xcount, zcount, ycount = eps_ref.shape
    core = lax.axis_index("gz")
    shape = (zcount, zcount)
    diagonal = lax.broadcasted_iota(jnp.int32, shape, 0) == lax.broadcasted_iota(jnp.int32, shape, 1)
    for x in range(xcount):
        for j in range(ycount // LANES):
            lanes = slice(j * LANES, (j + 1) * LANES)
            row = jnp.broadcast_to(mark_ref[x, j : j + 1, :].astype(jnp.float32), shape)
            mark = jnp.sum(jnp.where(diagonal, row, 0.0), axis=1, keepdims=True)
            freq = freq_ref[x, :, lanes] * DT
            res_ref[x, :, lanes] = mark * (freq * freq / DENOM)
    refs = (e_ref, h_ref, p_ref, eps_ref, res_ref)
    for parts, out_ref in zip(faces(xcount), (up_ref, down_ref)):
        at = 0
        for array, first, count in parts:
            out_ref[at : at + count] = pick(refs, array)[first : first + count]
            at += count
    begin = pl.multiple_of((1 - core) * (zcount - ROWS), ROWS)
    for array in range(ARRAYS):
        side_ref[array] = pick(refs, array)[:, pl.ds(begin, ROWS), :]


def slots():
    lane = lax.broadcasted_iota(jnp.int32, (ROWS, LANES), 1)
    return lane, lane // SLOT, lane % SLOT < SIDE


def turn(value, shift):
    shift = shift % LANES
    return pltpu.roll(value, shift, 1) if shift else value


def pack_strips(e_ref, h_ref, p_ref, eps_ref, res_ref, side_ref, low_ref, high_ref):
    xcount, zcount, ycount = eps_ref.shape
    core = lax.axis_index("gz")
    refs = (e_ref, h_ref, p_ref, eps_ref, res_ref)
    own = pl.multiple_of(core * ROWS, ROWS)
    halo = pl.multiple_of((1 - core) * zcount, ROWS)
    lane, slot, left = slots()
    per = LANES // SLOT
    assert per < xcount <= 2 * per and xcount - STEPS >= per >= STEPS
    for array in range(ARRAYS):
        src = pick(refs, array)
        for z in range(0, zcount + ROWS, ROWS):
            packed = [jnp.zeros((ROWS, LANES), jnp.float32)] * 2
            for x in range(xcount):
                if z < zcount:
                    first, last = src[x, z : z + ROWS, 0:LANES], src[x, z : z + ROWS, ycount - LANES : ycount]
                else:
                    first, last = side_ref[array, x, :, 0:LANES], side_ref[array, x, :, ycount - LANES : ycount]
                ends = turn(jnp.where(lane < SIDE, first, last), SLOT * (x % per) + SIDE)
                packed[x // per] = jnp.where(slot == x % per, ends, packed[x // per])
            rows = pl.ds(own + z, ROWS) if z < zcount else pl.ds(halo, ROWS)
            low_ref[array, rows, :] = jnp.where(left, turn(packed[1], -SIDE), packed[0])
            high_ref[array, rows, :] = jnp.where(left, packed[0], turn(packed[1], SIDE))


def merge_strips(ahead_ref, behind_ref, low_ref, high_ref):
    _, _, left = slots()
    for array in range(ARRAYS):
        for t in range(ahead_ref.shape[1] // ROWS):
            rows = slice(t * ROWS, (t + 1) * ROWS)
            ahead, behind = ahead_ref[array, rows, :], behind_ref[array, rows, :]
            low_ref[array, rows, :] = jnp.where(left, behind, ahead)
            high_ref[array, rows, :] = jnp.where(left, turn(behind, -SIDE), turn(ahead, SIDE))


def profile(index, total):
    depth = jnp.maximum(NPML - index, 0.0) + jnp.maximum(index - (total - 1 - NPML), 0.0)
    return SMAX * (depth / NPML) ** 3


class Block:
    def __init__(self, shape, state):
        self.xcount, self.zcount, self.ycount = shape
        self.E, self.H, self.R, self.U, self.EC, self.EB, self.BM, self.HC, self.HB = state
        self.tiles = self.ycount // LANES
        self.extent = self.xcount + 2 * STEPS
        self.zsteps = self.zcount // ROWS + 1
        core = lax.axis_index("gz")
        self.own = pl.multiple_of(GUARD + core * ROWS, ROWS)
        self.halo = pl.multiple_of(GUARD + (1 - core) * self.zcount, ROWS)
        self.near = pl.multiple_of(core * (self.zcount - ROWS), ROWS)
        self.lane = lax.broadcasted_iota(jnp.int32, (ROWS, LANES), 1)

    def put(self, array, plane, row, j, value):
        rows = pl.ds(row, ROWS)
        if array < HX:
            self.E[array, plane, j, rows, :] = value
        elif array < PX:
            self.H[array - HX, plane, j, rows, :] = value * (1.0 / 6.0)
        elif array < EPS:
            self.R[array - PX, plane, j, rows, :] = value * (1.0 / 3.0)
        elif array == EPS:
            self.EC[plane, j, rows, :] = value
        else:
            self.BM[plane, j, rows, :] = value

    def put_ends(self, array, plane, packed, slot):
        for t in range(self.zsteps):
            ends = turn(packed[array, t * ROWS : (t + 1) * ROWS, :], -(SLOT * slot + SIDE))
            self.put(array, plane, GUARD + t * ROWS, self.tiles, ends)

    def place(self, x, j):
        xtotal = self.xcount * lax.axis_size("gx")
        ytotal = self.ycount * lax.axis_size("gy")
        yplace = lax.axis_index("gy") * self.ycount
        xpos = lax.axis_index("gx") * self.xcount + x - STEPS
        lane = self.lane
        inside = jnp.full((ROWS, LANES), (xpos >= 0) & (xpos < xtotal))
        if j < self.tiles:
            ypos = yplace + j * LANES + lane
        else:
            ypos = yplace + jnp.where(lane < SIDE, self.ycount + lane, lane - LANES)
            inside = inside & ((lane < SIDE) | (lane >= LANES - SIDE)) & (ypos >= 0) & (ypos < ytotal)
        xsigma = profile(jnp.full((ROWS, LANES), xpos, jnp.int32).astype(jnp.float32), xtotal)
        return (xsigma + profile(ypos.astype(jnp.float32), ytotal)) * (DT / 2.0), inside

    def magnetic_coefficients(self, x):
        for j in range(self.tiles + 1):
            half, inside = self.place(x, j)
            over = 1.0 / (1.0 + half)
            self.HC[x, j] = jnp.where(inside, (1.0 - half) * over, 0.0)
            self.HB[x, j] = jnp.where(inside, (DT / 6.0) * over, 0.0)

    def electric_coefficients(self, x):
        for j in range(self.tiles + 1):
            half, inside = self.place(x, j)
            for t in range(self.zsteps):
                rows = pl.ds(GUARD + t * ROWS, ROWS)
                eps = self.EC[x, j, rows, :]
                over = 1.0 / jnp.where(inside, eps + half, 1.0)
                self.EC[x, j, rows, :] = jnp.where(inside, (eps - half) * over, 0.0)
                self.EB[x, j, rows, :] = jnp.where(inside, (6.0 * DT) * over, 0.0)

    def guards(self, x):
        zero = jnp.zeros((ROWS, LANES), jnp.float32)
        end = GUARD + self.zsteps * ROWS
        for j in range(self.tiles + 1):
            for c in range(3):
                self.H[c, x, j, 0:GUARD, :] = zero
                self.E[c, x, j, end : end + ROWS, :] = zero

    def load(self, ref, c, x, row):
        return [ref[c, x, j, pl.ds(row, ROWS), :] for j in range(self.tiles + 1)]

    def next_lane(self, v):
        r = [turn(t, -1) for t in v]
        return [jnp.where(self.lane == LANES - 1, r[(j + 1) % len(v)], r[j]) for j in range(len(v))]

    def previous_lane(self, v):
        r = [turn(t, 1) for t in v]
        return [jnp.where(self.lane == 0, r[j - 1], r[j]) for j in range(len(v))]

    def magnetic(self, x):
        E, H = self.E, self.H
        for t in range(self.zsteps):
            row = GUARD + t * ROWS
            rows = pl.ds(row, ROWS)
            ex, ey, ez = (self.load(E, c, x, row) for c in range(3))
            ex_z, ey_z = (self.load(E, c, x, row + 1) for c in (0, 1))
            ey_x, ez_x = (self.load(E, c, x + 1, row) for c in (1, 2))
            ex_y, ez_y = self.next_lane(ex), self.next_lane(ez)
            for j in range(self.tiles + 1):
                hc, hb = self.HC[x, j], self.HB[x, j]
                curls = (
                    (ez_y[j] - ez[j]) - (ey_z[j] - ey[j]),
                    (ex_z[j] - ex[j]) - (ez_x[j] - ez[j]),
                    (ey_x[j] - ey[j]) - (ex_y[j] - ex[j]),
                )
                for c in range(3):
                    H[c, x, j, rows, :] = hc * H[c, x, j, rows, :] - hb * curls[c]

    def electric(self, x, step):
        E, H, R, U = self.E, self.H, self.R, self.U
        last = step == STEPS
        for t in range(self.zsteps - 1 if last else self.zsteps):
            row = self.own + t * ROWS if last else GUARD + t * ROWS
            rows = pl.ds(row, ROWS)
            hx, hy, hz = (self.load(H, c, x, row) for c in range(3))
            hx_z, hy_z = (self.load(H, c, x, row - 1) for c in (0, 1))
            hy_x, hz_x = (self.load(H, c, x - 1, row) for c in (1, 2))
            hx_y, hz_y = self.previous_lane(hx), self.previous_lane(hz)
            for j in range(self.tiles if last else self.tiles + 1):
                ec, eb, bm = (ref[x, j, rows, :] for ref in (self.EC, self.EB, self.BM))
                curls = (
                    (hz[j] - hz_y[j]) - (hy[j] - hy_z[j]),
                    (hx[j] - hx_z[j]) - (hz[j] - hz_x[j]),
                    (hy[j] - hy_x[j]) - (hx[j] - hx_y[j]),
                )
                for c in range(3):
                    e, r = E[c, x, j, rows, :], R[c, x, j, rows, :]
                    u = bm * (e - r)
                    if step > 1:
                        u = KEEP * U[c, x, j, rows, :] + u
                    if not last:
                        U[c, x, j, rows, :] = u
                        R[c, x, j, rows, :] = r + u
                    E[c, x, j, rows, :] = ec * e + eb * (curls[c] - u)


def loop(begin, end, act, unroll):
    def run(x, carry):
        act(x)
        return carry

    lax.fori_loop(begin, end, run, 0, unroll=unroll)


def prepare(e_ref, h_ref, p_ref, eps_ref, res_ref, side_ref, low_ref, high_ref, *state):
    block = Block(eps_ref.shape, state)
    refs = (e_ref, h_ref, p_ref, eps_ref, res_ref)
    per = LANES // SLOT
    for array in range(ARRAYS):
        src = pick(refs, array)

        def own_plane(x, array=array, src=src):
            for j in range(block.tiles):
                lanes = slice(j * LANES, (j + 1) * LANES)
                for z in range(0, block.zcount, ROWS):
                    block.put(array, x + STEPS, block.own + z, j, src[x, z : z + ROWS, lanes])
                block.put(array, x + STEPS, block.halo, j, side_ref[array, x, :, lanes])

        loop(0, block.xcount, own_plane, 4)
        for x in range(block.xcount):
            block.put_ends(array, x + STEPS, low_ref if x < per else high_ref, x % per)
    loop(0, block.extent, block.guards, 1)
    loop(0, block.extent, block.magnetic_coefficients, 2)
    loop(STEPS, STEPS + block.xcount, block.electric_coefficients, 2)


def inner(shape, *state):
    block = Block(shape, state[len(state) // 2 :])
    for step in range(1, STEPS + 1):
        loop(STEPS + step - 1, STEPS + block.xcount - step, block.magnetic, 4)
        loop(STEPS + step, STEPS + block.xcount - step, functools.partial(block.electric, step=step), 4)


def outer(shape, low_ref, low_side_ref, high_ref, high_side_ref, corner_low_ref, corner_high_ref, *rest):
    count = (len(rest) - 2) // 2
    e_out, h_out = rest[count : count + 2]
    block = Block(shape, rest[count + 2 :])
    xcount, zcount = block.xcount, block.zcount
    per = LANES // SLOT
    ups, downs = faces(xcount)
    for parts, face, face_side, corner, above in (
        (ups, low_ref, low_side_ref, corner_low_ref, False),
        (downs, high_ref, high_side_ref, corner_high_ref, True),
    ):
        at = 0
        for array, first, count in parts:
            for i in range(count):
                plane = xcount + STEPS + i if above else first + i - (xcount - STEPS)
                for j in range(block.tiles):
                    lanes = slice(j * LANES, (j + 1) * LANES)
                    for z in range(0, zcount, ROWS):
                        block.put(array, plane, block.own + z, j, face[at + i, z : z + ROWS, lanes])
                    block.put(array, plane, block.halo, j, face_side[at + i, pl.ds(block.near, ROWS), lanes])
                block.put_ends(array, plane, corner, first + i if above else first + i - per)
            at += count
    zero = jnp.zeros((ROWS, LANES), jnp.float32)
    for j in range(block.tiles + 1):
        for t in range(block.zsteps):
            rows = pl.ds(GUARD + t * ROWS, ROWS)
            block.H[0, 0, j, rows, :] = zero
            block.E[0, block.extent - 1, j, rows, :] = zero
            block.R[0, block.extent - 2, j, rows, :] = zero
    loop(1, STEPS, block.electric_coefficients, STEPS - 1)
    loop(STEPS + xcount, block.extent - 1, block.electric_coefficients, STEPS - 1)
    for step in range(1, STEPS + 1):
        above = xcount + STEPS - step

        def both(x, act, gap):
            act(x)
            act(x + gap)

        low = step - 1
        loop(low, low + STEPS, functools.partial(both, act=block.magnetic, gap=above - low), STEPS)
        act = functools.partial(block.electric, step=step)
        loop(step, step + STEPS, functools.partial(both, act=act, gap=above - step), STEPS)

    def finish(x):
        for c in range(3):
            for j in range(block.tiles):
                lanes = slice(j * LANES, (j + 1) * LANES)
                for z in range(0, zcount, ROWS):
                    rows = pl.ds(block.own + z, ROWS)
                    e_out[c, x, z : z + ROWS, lanes] = block.E[c, x + STEPS, j, rows, :]
                    h_out[c, x, z : z + ROWS, lanes] = block.H[c, x + STEPS, j, rows, :] * 6.0

    loop(0, xcount, finish, 2)


def call(kernel, outs, args, flops, aliases=None):
    vmem = pl.BlockSpec(memory_space=pltpu.VMEM)
    return pl.pallas_call(
        kernel,
        out_shape=outs,
        in_specs=[vmem] * len(args),
        out_specs=[vmem] * len(outs),
        input_output_aliases=aliases or {},
        cost_estimate=pl.CostEstimate(flops=flops, bytes_accessed=flops, transcendentals=0),
        compiler_params=pltpu.CompilerParams(vmem_limit_bytes=VMEM_LIMIT),
    )(*[pltpu.with_memory_space_constraint(a, pltpu.VMEM) for a in args])


def shift(value, axis, by):
    count = lax.axis_size(axis)
    return lax.ppermute(value, axis, [(i, i + by) for i in range(count) if 0 <= i + by < count])


def swap(value):
    return lax.ppermute(value, "gz", [(0, 1), (1, 0)])


def kept(*shape):
    return pltpu.VMEM(shape, jnp.float32)


def body(e_field, h_field, polar, permittivity, resonance, dispersive):
    xcount, zcount, ycount = shape = permittivity.shape
    ups, downs = faces(xcount)
    up, down, side, res = call(
        pack_faces,
        [
            kept(planes_of(ups), zcount, ycount),
            kept(planes_of(downs), zcount, ycount),
            kept(ARRAYS, xcount, ROWS, ycount),
            kept(xcount, zcount, ycount),
        ],
        (e_field, h_field, polar, permittivity, resonance, jnp.swapaxes(dispersive, 1, 2)),
        COST,
    )
    side = swap(side)
    low, high = shift(up, "gx", 1), shift(down, "gx", -1)
    fields = (e_field, h_field, polar, permittivity, res, side)
    strips = [kept(ARRAYS, zcount + ROWS, LANES)] * 2
    first, last = call(pack_strips, strips, fields, COST)
    ahead, behind = shift(first, "gy", -1), shift(last, "gy", 1)
    strip_low, strip_high = call(merge_strips, strips, (ahead, behind), COST)
    corner_low, corner_high = shift(strip_high, "gx", 1), shift(strip_low, "gx", -1)
    extent, tiles, rows = xcount + 2 * STEPS, ycount // LANES + 1, zcount + ROWS + 2 * GUARD
    state = [kept(3, extent, tiles, rows, LANES)] * 4
    state += [kept(extent, tiles, rows, LANES)] * 3 + [kept(extent, tiles, ROWS, LANES)] * 2
    count = len(state)
    kept_state = call(prepare, state, (*fields, strip_low, strip_high), 3 * COST)
    low, high, kept_state = lax.optimization_barrier((low, high, kept_state))
    low_side, high_side = swap(low), swap(high)
    kept_state = call(functools.partial(inner, shape), state, kept_state, 6 * COST, {i: i for i in range(count)})
    faces_in = (low, low_side, high, high_side, corner_low, corner_high)
    given = len(faces_in)
    outs = [jax.ShapeDtypeStruct(e_field.shape, jnp.float32), jax.ShapeDtypeStruct(h_field.shape, jnp.float32)]
    aliases = {given + i: 2 + i for i in range(count)}
    return tuple(call(functools.partial(outer, shape), outs + state, (*faces_in, *kept_state), 6 * COST, aliases)[:2])


def solution(mesh):
    field, cell = P(None, "gx", "gz", "gy"), P("gx", "gz", "gy")
    return jax.shard_map(
        body,
        mesh=mesh,
        in_specs=(field, field, field, cell, cell, cell),
        out_specs=(field, field),
        check_vma=False,
    )
```

time: 154 us -> 52.9 us (0.34)
  the two profiles are of different devices: /device:TPU:24 before, /device:TPU:0 now
where the time goes in v2:
time: 52.9 us; the launch traced here: 52.5 us
  Pallas kernels  19 us (36%)
  starting transfers between devices  18.5 us (35%)
  waiting for transfers between devices  8.11 us (15%)
  local copies, waits for them, and re-layouts  6.01 us (11%)
  between operations  0.77 us (1%)
    pallas_call x6, Pallas kernels, call(): pl.pallas_call(kernel, out_shape=outs, in_specs=[vmem] * len(args), out_s...  19 us
    ppermute x6, starting transfers between devices, shift(): lax.ppermute(value, axis, [(i, i + by) for i in range(count) if 0 <= i +...  17.5 us
    ppermute x6, waiting for transfers between devices, shift(): lax.ppermute(value, axis, [(i, i + by) for i in range(count) if 0 <= i +...  8.1 us
    unnamed x14, local copies, waits for them, and re-layouts  6.01 us
  transfers between devices with their start and end apart: 9, of which 3 were waited for; matrix products, arithmetic and copies ran while one was open for 0% of the time, Pallas kernels for 22%

profile of v2, /device:TPU:0, one launch (start us, length us, event | category | flops | bytes accessed | tf_op | source)
XLA Modules:
  0.0 52.5 jit_solution(10100423641547263265)
XLA Ops:
  0.6 0.0 copy-start
  0.6 1.1 %copy-done = f32[3,16,16,256]{3,2,1,0:T(8,128)S(1)} copy-done((f32[3,16,16,256]{3,2,1,0:T(8,128)S(1)}, f32[3,16,16,256]{3,2,1,0:T(8,128)}, u32[]{:S(2)}) %copy-start) | copy-done | bytes 786456
  1.8 0.0 copy-start.2
  1.8 1.1 %copy-done.2 = f32[3,16,16,256]{3,2,1,0:T(8,128)S(1)} copy-done((f32[3,16,16,256]{3,2,1,0:T(8,128)S(1)}, f32[3,16,16,256]{3,2,1,0:T(8,128)}, u32[]{:S(2)}) %copy-start.2) | copy-done | bytes 786456
  2.9 0.0 copy-start.3
  2.9 1.1 %copy-done.3 = f32[3,16,16,256]{3,2,1,0:T(8,128)S(1)} copy-done((f32[3,16,16,256]{3,2,1,0:T(8,128)S(1)}, f32[3,16,16,256]{3,2,1,0:T(8,128)}, u32[]{:S(2)}) %copy-start.3) | copy-done | bytes 786456
  4.0 0.0 copy-start.4
  4.0 0.9 %copy-done.4 = f32[16,16,256]{2,1,0:T(8,128)S(1)} copy-done((f32[16,16,256]{2,1,0:T(8,128)S(1)}, f32[16,16,256]{2,1,0:T(8,128)}, u32[]{:S(2)}) %copy-start.4) | copy-done | bytes 262168
  5.0 0.0 copy-start.5
  5.0 0.9 %copy-done.5 = f32[16,16,256]{2,1,0:T(8,128)S(1)} copy-done((f32[16,16,256]{2,1,0:T(8,128)S(1)}, f32[16,16,256]{2,1,0:T(8,128)}, u32[]{:S(2)}) %copy-start.5) | copy-done | bytes 262168
  5.9 0.0 copy-start.6
  5.9 0.7 %copy-done.6 = s32[16,16,2]{1,2,0:T(2,128)S(1)} copy-done((s32[16,16,2]{1,2,0:T(2,128)S(1)}, s32[16,16,2]{1,2,0:T(2,128)}, u32[]{:S(2)}) %copy-start.6) | copy-done | bytes 2072
  6.7 0.0 copy-start.1
  6.7 0.3 shard_map.77
  6.9 0.5 collective-permute-start.2
  7.4 4.5 %collective-permute-start = (f32[49,16,256]{2,1,0:T(8,128)S(1)}, f32[49,16,256]{2,1,0:T(8,128)S(1)}, u32[]{:S(2)}, u32[]{:S(2)}) collective-permute-start(f32[49,16,256]{2,1,0:T(8,128)S(1)} %get-tuple-element.41), channel_id=1, source_target_pairs={{0,8},{8,16},{16,24},{1,9},{9,17},{17,25},{2,10},{10,18},{18,26},{... | collective-permute-start | bytes 2408456 | tf_op jit(solution)/shard_map/ppermute | solution.py:373
  12.0 1.3 %collective-permute-start.1 = (f32[45,16,256]{2,1,0:T(8,128)S(1)}, f32[45,16,256]{2,1,0:T(8,128)S(1)}, u32[]{:S(2)}, u32[]{:S(2)}) collective-permute-start(f32[45,16,256]{2,1,0:T(8,128)S(1)} %get-tuple-element.42), channel_id=1, source_target_pairs={{8,0},{16,8},{24,16},{9,1},{17,9},{25,17},{10,2},{18,10},{26,18},{... | collective-permute-start | bytes 2211848 | tf_op jit(solution)/shard_map/ppermute | solution.py:373
  13.3 0.0 collective-permute-done.2.side_ref
  13.3 2.4 %shard_map.78 = (f32[11,24,128]{2,1,0:T(8,128)S(1)}, f32[11,24,128]{2,1,0:T(8,128)S(1)}) custom-call(f32[3,16,16,256]{3,2,1,0:T(8,128)S(1)} %copy-done, f32[3,16,16,256]{3,2,1,0:T(8,128)S(1)} %copy-done.2, f32[3,16,16,256]{3,2,1,0:T(8,128)S(1)} %copy-done.3, f32[16,16,256]{2,1,0:T(8,128)S(1)} %copy-done.4, f32[16,16,256]{2,1,0:T(8,128)S(1)} %get-tuple-element.43.res_ref, ...), custom_call_target="tpu_custom_call" | custom-call | flops 3000000 | bytes 3000000 | tf_op jit(solution)/shard_map/pallas_call | solution.py:360
  15.7 1.3 %collective-permute-start.3 = (f32[11,24,128]{2,1,0:T(8,128)S(1)}, f32[11,24,128]{2,1,0:T(8,128)S(1)}, u32[]{:S(2)}, u32[]{:S(2)}) collective-permute-start(f32[11,24,128]{2,1,0:T(8,128)S(1)} %get-tuple-element.45), channel_id=1, source_target_pairs={{2,0},{4,2},{6,4},{3,1},{5,3},{7,5},{10,8},{12,10},{14,12},{11,9},... | collective-permute-start | bytes 405512 | tf_op jit(solution)/shard_map/ppermute | solution.py:373
  17.0 4.6 %collective-permute-start.4 = (f32[11,24,128]{2,1,0:T(8,128)S(1)}, f32[11,24,128]{2,1,0:T(8,128)S(1)}, u32[]{:S(2)}, u32[]{:S(2)}) collective-permute-start(f32[11,24,128]{2,1,0:T(8,128)S(1)} %get-tuple-element.46), channel_id=1, source_target_pairs={{0,2},{2,4},{4,6},{1,3},{3,5},{5,7},{8,10},{10,12},{12,14},{9,11},... | collective-permute-start | bytes 405512 | tf_op jit(solution)/shard_map/ppermute | solution.py:373
  21.6 1.7 %collective-permute-done.3.ahead_ref = f32[11,24,128]{2,1,0:T(8,128)S(1)} collective-permute-done((f32[11,24,128]{2,1,0:T(8,128)S(1)}, f32[11,24,128]{2,1,0:T(8,128)S(1)}, u32[]{:S(2)}, u32[]{:S(2)}) %collective-permute-start.3) | collective-permute-done | bytes 135200 | tf_op jit(solution)/shard_map/ppermute | solution.py:373
  23.3 1.2 %collective-permute-done.4.behind_ref = f32[11,24,128]{2,1,0:T(8,128)S(1)} collective-permute-done((f32[11,24,128]{2,1,0:T(8,128)S(1)}, f32[11,24,128]{2,1,0:T(8,128)S(1)}, u32[]{:S(2)}, u32[]{:S(2)}) %collective-permute-start.4) | collective-permute-done | bytes 135200 | tf_op jit(solution)/shard_map/ppermute | solution.py:373
  24.5 0.1 shard_map.79
  24.7 0.0 copy-done.1
  24.7 2.6 %shard_map.80 = (f32[3,26,3,40,128]{4,3,2,1,0:T(8,128)S(1)}, f32[3,26,3,40,128]{4,3,2,1,0:T(8,128)S(1)}, f32[3,26,3,40,128]{4,3,2,1,0:T(8,128)S(1)}, f32[3,26,3,...) custom-call(f32[3,16,16,256]{3,2,1,0:T(8,128)S(1)} %copy-done.1, ...), custom_call_target="tpu_custom_call" | custom-call | flops 9000000 | bytes 9000000 | tf_op jit(solution)/shard_map/pallas_call | solution.py:360
  27.3 5.2 %collective-permute-done.1.high_ref = f32[45,16,256]{2,1,0:T(8,128)S(1)} collective-permute-done((f32[45,16,256]{2,1,0:T(8,128)S(1)}, f32[45,16,256]{2,1,0:T(8,128)S(1)}, u32[]{:S(2)}, u32[]{:S(2)}) %collective-permute-start.1) | collective-permute-done | bytes 737312 | tf_op jit(solution)/shard_map/ppermute | solution.py:373
  32.5 0.0 collective-permute-done.low_ref
  32.5 0.0 collective-permute-start.5
  32.5 0.5 collective-permute-start.6
  33.0 1.3 %collective-permute-start.8 = (f32[11,24,128]{2,1,0:T(8,128)S(1)}, f32[11,24,128]{2,1,0:T(8,128)S(1)}, u32[]{:S(2)}, u32[]{:S(2)}) collective-permute-start(f32[11,24,128]{2,1,0:T(8,128)S(1)} %get-tuple-element.47.low_ref), channel_id=1, source_target_pairs={{8,0},{16,8},{24,16},{9,1},{17,9},{25,17},{10,2},{18,10},{26,18},{... | collective-permute-start | bytes 405512 | tf_op jit(solution)/shard_map/ppermute | solution.py:373
  34.3 4.6 %collective-permute-start.7 = (f32[11,24,128]{2,1,0:T(8,128)S(1)}, f32[11,24,128]{2,1,0:T(8,128)S(1)}, u32[]{:S(2)}, u32[]{:S(2)}) collective-permute-start(f32[11,24,128]{2,1,0:T(8,128)S(1)} %get-tuple-element.48.high_ref), channel_id=1, source_target_pairs={{0,8},{8,16},{16,24},{1,9},{9,17},{17,25},{2,10},{10,18},{18,26},{... | collective-permute-start | bytes 405512 | tf_op jit(solution)/shard_map/ppermute | solution.py:373
  38.8 6.3 %shard_map.81 = (f32[3,26,3,40,128]{4,3,2,1,0:T(8,128)S(1)}, f32[3,26,3,40,128]{4,3,2,1,0:T(8,128)S(1)}, f32[3,26,3,40,128]{4,3,2,1,0:T(8,128)S(1)}, f32[3,26,3,...) custom-call(f32[3,26,3,40,128]{4,3,2,1,0:T(8,128)S(1)} %get-tuple-el, ...), custom_call_target="tpu_custom_call", output_to_operand_aliasing={{0}: (0, {}), {1}: (1, {}), {2}: (2, {}), {3}: (3, {}), {4}... | custom-call | flops 18000000 | bytes 18000000 | tf_op jit(solution)/shard_map/pallas_call | solution.py:360
  45.1 0.0 collective-permute-done.8.corner_high_ref
  45.1 0.0 collective-permute-done.7.corner_low_ref
  45.1 0.0 collective-permute-done.6.high_side_ref
  45.1 0.0 collective-permute-done.5.low_side_ref
  45.2 7.3 %shard_map.82 = (f32[3,16,16,256]{3,2,1,0:T(8,128)}, f32[3,16,16,256]{3,2,1,0:T(8,128)}, f32[3,26,3,40,128]{4,3,2,1,0:T(8,128)S(1)}, f32[3,26,3,40,128]{4,3,2,1,...) custom-call(f32[49,16,256]{2,1,0:T(8,128)S(1)} %collective-permute-d, ...), custom_call_target="tpu_custom_call", output_to_operand_aliasing={{2}: (6, {}), {3}: (7, {}), {4}: (8, {}), {5}: (9, {}), {6}... | custom-call | flops 18000000 | bytes 18000000 | tf_op jit(solution)/shard_map/pallas_call | solution.py:360
Async XLA Ops:
  0.6 1.1 %copy-start = (f32[3,16,16,256]{3,2,1,0:T(8,128)S(1)}, f32[3,16,16,256]{3,2,1,0:T(8,128)}, u32[]{:S(2)}) copy-start(f32[3,16,16,256]{3,2,1,0:T(8,128)} %e_ref.5) | copy-start | bytes 2359300
  1.8 1.1 %copy-start.2 = (f32[3,16,16,256]{3,2,1,0:T(8,128)S(1)}, f32[3,16,16,256]{3,2,1,0:T(8,128)}, u32[]{:S(2)}) copy-start(f32[3,16,16,256]{3,2,1,0:T(8,128)} %h_ref.5) | copy-start | bytes 2359300
  2.9 1.1 %copy-start.3 = (f32[3,16,16,256]{3,2,1,0:T(8,128)S(1)}, f32[3,16,16,256]{3,2,1,0:T(8,128)}, u32[]{:S(2)}) copy-start(f32[3,16,16,256]{3,2,1,0:T(8,128)} %p_ref.5) | copy-start | bytes 2359300
  4.0 0.9 %copy-start.4 = (f32[16,16,256]{2,1,0:T(8,128)S(1)}, f32[16,16,256]{2,1,0:T(8,128)}, u32[]{:S(2)}) copy-start(f32[16,16,256]{2,1,0:T(8,128)} %eps_ref.5) | copy-start | bytes 786436
  5.0 0.9 %copy-start.5 = (f32[16,16,256]{2,1,0:T(8,128)S(1)}, f32[16,16,256]{2,1,0:T(8,128)}, u32[]{:S(2)}) copy-start(f32[16,16,256]{2,1,0:T(8,128)} %freq_ref.1) | copy-start | bytes 786436
  5.9 0.7 %copy-start.6 = (s32[16,16,2]{1,2,0:T(2,128)S(1)}, s32[16,16,2]{1,2,0:T(2,128)}, u32[]{:S(2)}) copy-start(s32[16,16,2]{1,2,0:T(2,128)} %param.11) | copy-start | bytes 6148
  6.7 18.0 %copy-start.1 = (f32[3,16,16,256]{3,2,1,0:T(8,128)S(1)}, f32[3,16,16,256]{3,2,1,0:T(8,128)}, u32[]{:S(2)}) copy-start(f32[3,16,16,256]{3,2,1,0:T(8,128)} %e_ref.5) | copy-start | bytes 2359300
  6.9 6.4 %collective-permute-start.2 = (f32[11,16,8,256]{3,2,1,0:T(8,128)S(1)}, f32[11,16,8,256]{3,2,1,0:T(8,128)S(1)}, u32[]{:S(2)}, u32[]{:S(2)}) collective-permute-start(f32[11,16,8,256]{3,2,1,0:T(8,128)S(1)} %get-tuple-element.44), channel_id=1, source_target_pairs={{0,1},{1,0},{2,3},{3,2},{4,5},{5,4},{6,7},{7,6},{8,9},{9,8},{10,11... | collective-permute-start | bytes 4325384 | tf_op jit(solution)/shard_map/ppermute | solution.py:377
  7.4 25.0 %collective-permute-start = (f32[49,16,256]{2,1,0:T(8,128)S(1)}, f32[49,16,256]{2,1,0:T(8,128)S(1)}, u32[]{:S(2)}, u32[]{:S(2)}) collective-permute-start(f32[49,16,256]{2,1,0:T(8,128)S(1)} %get-tuple-element.41), channel_id=1, source_target_pairs={{0,8},{8,16},{16,24},{1,9},{9,17},{17,25},{2,10},{10,18},{18,26},{... | collective-permute-start | bytes 2408456 | tf_op jit(solution)/shard_map/ppermute | solution.py:373
  12.0 20.5 %collective-permute-start.1 = (f32[45,16,256]{2,1,0:T(8,128)S(1)}, f32[45,16,256]{2,1,0:T(8,128)S(1)}, u32[]{:S(2)}, u32[]{:S(2)}) collective-permute-start(f32[45,16,256]{2,1,0:T(8,128)S(1)} %get-tuple-element.42), channel_id=1, source_target_pairs={{8,0},{16,8},{24,16},{9,1},{17,9},{25,17},{10,2},{18,10},{26,18},{... | collective-permute-start | bytes 2211848 | tf_op jit(solution)/shard_map/ppermute | solution.py:373
  15.7 7.6 %collective-permute-start.3 = (f32[11,24,128]{2,1,0:T(8,128)S(1)}, f32[11,24,128]{2,1,0:T(8,128)S(1)}, u32[]{:S(2)}, u32[]{:S(2)}) collective-permute-start(f32[11,24,128]{2,1,0:T(8,128)S(1)} %get-tuple-element.45), channel_id=1, source_target_pairs={{2,0},{4,2},{6,4},{3,1},{5,3},{7,5},{10,8},{12,10},{14,12},{11,9},... | collective-permute-start | bytes 405512 | tf_op jit(solution)/shard_map/ppermute | solution.py:373
  17.0 7.5 %collective-permute-start.4 = (f32[11,24,128]{2,1,0:T(8,128)S(1)}, f32[11,24,128]{2,1,0:T(8,128)S(1)}, u32[]{:S(2)}, u32[]{:S(2)}) collective-permute-start(f32[11,24,128]{2,1,0:T(8,128)S(1)} %get-tuple-element.46), channel_id=1, source_target_pairs={{0,2},{2,4},{4,6},{1,3},{3,5},{5,7},{8,10},{10,12},{12,14},{9,11},... | collective-permute-start | bytes 405512 | tf_op jit(solution)/shard_map/ppermute | solution.py:373
  32.5 12.7 %collective-permute-start.5 = (f32[49,16,256]{2,1,0:T(8,128)S(1)}, f32[49,16,256]{2,1,0:T(8,128)S(1)}, u32[]{:S(2)}, u32[]{:S(2)}) collective-permute-start(f32[49,16,256]{2,1,0:T(8,128)S(1)} %collective-permute-done.low_ref), channel_id=1, source_target_pairs={{0,1},{1,0},{2,3},{3,2},{4,5},{5,4},{6,7},{7,6},{8,9},{9,8},{10,11... | collective-permute-start | bytes 2408456 | tf_op jit(solution)/shard_map/ppermute | solution.py:377
  32.5 12.7 %collective-permute-start.6 = (f32[45,16,256]{2,1,0:T(8,128)S(1)}, f32[45,16,256]{2,1,0:T(8,128)S(1)}, u32[]{:S(2)}, u32[]{:S(2)}) collective-permute-start(f32[45,16,256]{2,1,0:T(8,128)S(1)} %collective-permute-done.1.high_ref), channel_id=1, source_target_pairs={{0,1},{1,0},{2,3},{3,2},{4,5},{5,4},{6,7},{7,6},{8,9},{9,8},{10,11... | collective-permute-start | bytes 2211848 | tf_op jit(solution)/shard_map/ppermute | solution.py:377
  33.0 12.1 %collective-permute-start.8 = (f32[11,24,128]{2,1,0:T(8,128)S(1)}, f32[11,24,128]{2,1,0:T(8,128)S(1)}, u32[]{:S(2)}, u32[]{:S(2)}) collective-permute-start(f32[11,24,128]{2,1,0:T(8,128)S(1)} %get-tuple-element.47.low_ref), channel_id=1, source_target_pairs={{8,0},{16,8},{24,16},{9,1},{17,9},{25,17},{10,2},{18,10},{26,18},{... | collective-permute-start | bytes 405512 | tf_op jit(solution)/shard_map/ppermute | solution.py:373
  34.3 10.8 %collective-permute-start.7 = (f32[11,24,128]{2,1,0:T(8,128)S(1)}, f32[11,24,128]{2,1,0:T(8,128)S(1)}, u32[]{:S(2)}, u32[]{:S(2)}) collective-permute-start(f32[11,24,128]{2,1,0:T(8,128)S(1)} %get-tuple-element.48.high_ref), channel_id=1, source_target_pairs={{0,8},{8,16},{16,24},{1,9},{9,17},{17,25},{2,10},{10,18},{18,26},{... | collective-permute-start | bytes 405512 | tf_op jit(solution)/shard_map/ppermute | solution.py:373

commit v3 on v2

--- a/solution.py
+++ b/solution.py
@@ -7,6 +7,7 @@
 from jax.sharding import PartitionSpec as P
 
 STEPS = 5
+SPLIT = 4
 NPML = 8
 DT = 0.5
 DAMPING = 0.1
@@ -28,26 +29,15 @@
 COST = 3_000_000
 
 
-def faces(count):
-    up, down = [], []
-    last = count - STEPS
-    for c in range(3):
-        up.append((EX + c, last, STEPS))
-        down.append((EX + c, 0, STEPS if c > 0 else STEPS - 1))
-    for c in range(3):
-        up.append((HX + c, last if c > 0 else last + 1, STEPS if c > 0 else STEPS - 1))
-        down.append((HX + c, 0, STEPS - 1))
-    for c in range(3):
-        up.append((PX + c, last + 1, STEPS - 1))
-        down.append((PX + c, 0, STEPS - 1 if c > 0 else STEPS - 2))
-    for a in (EPS, RES):
-        up.append((a, last + 1, STEPS - 1))
-        down.append((a, 0, STEPS - 1))
-    return up, down
+def faces():
+    parts = [(EX + c, STEPS) for c in range(3)]
+    parts += [(HX + c, STEPS if c > 0 else STEPS - 1) for c in range(3)]
+    parts += [(a, STEPS - 1) for a in (PX, PX + 1, PX + 2, EPS, RES)]
+    return parts
 
 
 def planes_of(parts):
-    return sum(count for _, _, count in parts)
+    return sum(count for _, count in parts)
 
 
 def pick(refs, array):
@@ -61,11 +51,36 @@
     return eps_ref if array == EPS else res_ref
 
 
-def pack_faces(e_ref, h_ref, p_ref, eps_ref, freq_ref, mark_ref, up_ref, down_ref, side_ref, res_ref):
+def even(axis):
+    return lax.axis_index(axis) % 2 == 0
+
+
+def pack_faces(
+    e_hbm, h_hbm, p_hbm, eps_hbm, freq_hbm, mark_hbm,
+    first_ref, second_ref, side_ref, e_ref, h_ref, p_ref, eps_ref, res_ref,
+    freq_ref, mark_ref, arrived,
+):
     xcount, zcount, ycount = eps_ref.shape
+    moves = [
+        pltpu.make_async_copy(src, dst, arrived.at[i])
+        for i, (src, dst) in enumerate(
+            (
+                (mark_hbm, mark_ref),
+                (freq_hbm, freq_ref),
+                (eps_hbm, eps_ref),
+                (e_hbm, e_ref),
+                (h_hbm, h_ref),
+                (p_hbm, p_ref),
+            )
+        )
+    ]
+    for move in moves:
+        move.start()
     core = lax.axis_index("gz")
     shape = (zcount, zcount)
     diagonal = lax.broadcasted_iota(jnp.int32, shape, 0) == lax.broadcasted_iota(jnp.int32, shape, 1)
+    moves[0].wait()
+    moves[1].wait()
     for x in range(xcount):
         for j in range(ycount // LANES):
             lanes = slice(j * LANES, (j + 1) * LANES)
@@ -73,11 +88,14 @@
             mark = jnp.sum(jnp.where(diagonal, row, 0.0), axis=1, keepdims=True)
             freq = freq_ref[x, :, lanes] * DT
             res_ref[x, :, lanes] = mark * (freq * freq / DENOM)
+    for move in moves[2:]:
+        move.wait()
     refs = (e_ref, h_ref, p_ref, eps_ref, res_ref)
-    for parts, out_ref in zip(faces(xcount), (up_ref, down_ref)):
+    for up, out_ref in ((even("gx"), first_ref), (jnp.logical_not(even("gx")), second_ref)):
         at = 0
-        for array, first, count in parts:
-            out_ref[at : at + count] = pick(refs, array)[first : first + count]
+        for array, count in faces():
+            for i in range(count):
+                out_ref[at + i] = pick(refs, array)[jnp.where(up, xcount - 1 - i, i)]
             at += count
     begin = pl.multiple_of((1 - core) * (zcount - ROWS), ROWS)
     for array in range(ARRAYS):
@@ -94,7 +112,7 @@
     return pltpu.roll(value, shift, 1) if shift else value
 
 
-def pack_strips(e_ref, h_ref, p_ref, eps_ref, res_ref, side_ref, low_ref, high_ref):
+def pack_strips(e_ref, h_ref, p_ref, eps_ref, res_ref, side_ref, first_ref, second_ref):
     xcount, zcount, ycount = eps_ref.shape
     core = lax.axis_index("gz")
     refs = (e_ref, h_ref, p_ref, eps_ref, res_ref)
@@ -102,7 +120,8 @@
     halo = pl.multiple_of((1 - core) * zcount, ROWS)
     lane, slot, left = slots()
     per = LANES // SLOT
-    assert per < xcount <= 2 * per and xcount - STEPS >= per >= STEPS
+    assert xcount == 2 * per and per >= STEPS
+    up = even("gy")
     for array in range(ARRAYS):
         src = pick(refs, array)
         for z in range(0, zcount + ROWS, ROWS):
@@ -115,18 +134,26 @@
                 ends = turn(jnp.where(lane < SIDE, first, last), SLOT * (x % per) + SIDE)
                 packed[x // per] = jnp.where(slot == x % per, ends, packed[x // per])
             rows = pl.ds(own + z, ROWS) if z < zcount else pl.ds(halo, ROWS)
-            low_ref[array, rows, :] = jnp.where(left, turn(packed[1], -SIDE), packed[0])
-            high_ref[array, rows, :] = jnp.where(left, packed[0], turn(packed[1], SIDE))
-
-
-def merge_strips(ahead_ref, behind_ref, low_ref, high_ref):
+            low = jnp.where(left, turn(packed[1], -SIDE), packed[0])
+            high = jnp.where(left, packed[0], turn(packed[1], SIDE))
+            first_ref[array, rows, :] = jnp.where(up, high, low)
+            second_ref[array, rows, :] = jnp.where(up, low, high)
+
+
+def merge_strips(first_ref, second_ref, low_ref, high_ref, corner_first_ref, corner_second_ref):
     _, _, left = slots()
+    up, over = even("gy"), even("gx")
     for array in range(ARRAYS):
-        for t in range(ahead_ref.shape[1] // ROWS):
+        for t in range(first_ref.shape[1] // ROWS):
             rows = slice(t * ROWS, (t + 1) * ROWS)
-            ahead, behind = ahead_ref[array, rows, :], behind_ref[array, rows, :]
-            low_ref[array, rows, :] = jnp.where(left, behind, ahead)
-            high_ref[array, rows, :] = jnp.where(left, turn(behind, -SIDE), turn(ahead, SIDE))
+            first, second = first_ref[array, rows, :], second_ref[array, rows, :]
+            ahead, behind = jnp.where(up, first, second), jnp.where(up, second, first)
+            low = jnp.where(left, behind, ahead)
+            high = jnp.where(left, turn(behind, -SIDE), turn(ahead, SIDE))
+            low_ref[array, rows, :] = low
+            high_ref[array, rows, :] = high
+            corner_first_ref[array, rows, :] = jnp.where(over, high, low)
+            corner_second_ref[array, rows, :] = jnp.where(over, low, high)
 
 
 def profile(index, total):
@@ -162,7 +189,7 @@
 
     def put_ends(self, array, plane, packed, slot):
         for t in range(self.zsteps):
-            ends = turn(packed[array, t * ROWS : (t + 1) * ROWS, :], -(SLOT * slot + SIDE))
+            ends = pltpu.roll(packed[array, t * ROWS : (t + 1) * ROWS, :], LANES - SIDE - SLOT * slot, 1)
             self.put(array, plane, GUARD + t * ROWS, self.tiles, ends)
 
     def place(self, x, j):
@@ -271,10 +298,9 @@
     lax.fori_loop(begin, end, run, 0, unroll=unroll)
 
 
-def prepare(e_ref, h_ref, p_ref, eps_ref, res_ref, side_ref, low_ref, high_ref, *state):
+def prepare(e_ref, h_ref, p_ref, eps_ref, res_ref, side_ref, *state):
     block = Block(eps_ref.shape, state)
     refs = (e_ref, h_ref, p_ref, eps_ref, res_ref)
-    per = LANES // SLOT
     for array in range(ARRAYS):
         src = pick(refs, array)
 
@@ -286,49 +312,49 @@
                 block.put(array, x + STEPS, block.halo, j, side_ref[array, x, :, lanes])
 
         loop(0, block.xcount, own_plane, 4)
+    loop(0, block.extent, block.guards, 1)
+    loop(0, block.extent, block.magnetic_coefficients, 2)
+
+
+def prepare_ends(shape, low_ref, high_ref, *states):
+    block = Block(shape, states[len(states) // 2 :])
+    per = LANES // SLOT
+    for array in range(ARRAYS):
         for x in range(block.xcount):
             block.put_ends(array, x + STEPS, low_ref if x < per else high_ref, x % per)
-    loop(0, block.extent, block.guards, 1)
-    loop(0, block.extent, block.magnetic_coefficients, 2)
     loop(STEPS, STEPS + block.xcount, block.electric_coefficients, 2)
 
 
-def inner(shape, *state):
-    block = Block(shape, state[len(state) // 2 :])
-    for step in range(1, STEPS + 1):
+def inner(shape, begin, end, *states):
+    block = Block(shape, states[len(states) // 2 :])
+    for step in range(begin, end):
         loop(STEPS + step - 1, STEPS + block.xcount - step, block.magnetic, 4)
         loop(STEPS + step, STEPS + block.xcount - step, functools.partial(block.electric, step=step), 4)
 
 
-def outer(shape, low_ref, low_side_ref, high_ref, high_side_ref, corner_low_ref, corner_high_ref, *rest):
+def outer(
+    shape, first_ref, first_side_ref, second_ref, second_side_ref, corner_first_ref, corner_second_ref, *rest
+):
     count = (len(rest) - 2) // 2
     e_out, h_out = rest[count : count + 2]
     block = Block(shape, rest[count + 2 :])
     xcount, zcount = block.xcount, block.zcount
     per = LANES // SLOT
-    ups, downs = faces(xcount)
-    for parts, face, face_side, corner, above in (
-        (ups, low_ref, low_side_ref, corner_low_ref, False),
-        (downs, high_ref, high_side_ref, corner_high_ref, True),
+    for above, face, face_side, corner in (
+        (even("gx"), first_ref, first_side_ref, corner_first_ref),
+        (jnp.logical_not(even("gx")), second_ref, second_side_ref, corner_second_ref),
     ):
         at = 0
-        for array, first, count in parts:
+        for array, count in faces():
             for i in range(count):
-                plane = xcount + STEPS + i if above else first + i - (xcount - STEPS)
+                plane = jnp.where(above, xcount + STEPS + i, STEPS - 1 - i)
                 for j in range(block.tiles):
                     lanes = slice(j * LANES, (j + 1) * LANES)
                     for z in range(0, zcount, ROWS):
                         block.put(array, plane, block.own + z, j, face[at + i, z : z + ROWS, lanes])
                     block.put(array, plane, block.halo, j, face_side[at + i, pl.ds(block.near, ROWS), lanes])
-                block.put_ends(array, plane, corner, first + i if above else first + i - per)
+                block.put_ends(array, plane, corner, jnp.where(above, i, per - 1 - i))
             at += count
-    zero = jnp.zeros((ROWS, LANES), jnp.float32)
-    for j in range(block.tiles + 1):
-        for t in range(block.zsteps):
-            rows = pl.ds(GUARD + t * ROWS, ROWS)
-            block.H[0, 0, j, rows, :] = zero
-            block.E[0, block.extent - 1, j, rows, :] = zero
-            block.R[0, block.extent - 2, j, rows, :] = zero
     loop(1, STEPS, block.electric_coefficients, STEPS - 1)
     loop(STEPS + xcount, block.extent - 1, block.electric_coefficients, STEPS - 1)
     for step in range(1, STEPS + 1):
@@ -355,26 +381,24 @@
     loop(0, xcount, finish, 2)
 
 
-def call(kernel, outs, args, flops, aliases=None):
-    vmem = pl.BlockSpec(memory_space=pltpu.VMEM)
+def call(kernel, outs, args, cost, aliases=None, scratch=(), spec=pltpu.VMEM):
+    args = [pltpu.with_memory_space_constraint(a, spec) for a in args]
+    work = int(cost * COST)
     return pl.pallas_call(
         kernel,
         out_shape=outs,
-        in_specs=[vmem] * len(args),
-        out_specs=[vmem] * len(outs),
+        in_specs=[pl.BlockSpec(memory_space=spec)] * len(args),
+        out_specs=[pl.BlockSpec(memory_space=pltpu.VMEM)] * len(outs),
+        scratch_shapes=scratch,
         input_output_aliases=aliases or {},
-        cost_estimate=pl.CostEstimate(flops=flops, bytes_accessed=flops, transcendentals=0),
+        cost_estimate=pl.CostEstimate(flops=work, bytes_accessed=work, transcendentals=0),
         compiler_params=pltpu.CompilerParams(vmem_limit_bytes=VMEM_LIMIT),
-    )(*[pltpu.with_memory_space_constraint(a, pltpu.VMEM) for a in args])
-
-
-def shift(value, axis, by):
-    count = lax.axis_size(axis)
-    return lax.ppermute(value, axis, [(i, i + by) for i in range(count) if 0 <= i + by < count])
-
-
-def swap(value):
-    return lax.ppermute(value, "gz", [(0, 1), (1, 0)])
+    )(*args)
+
+
+def swap(value, axis, begin=0):
+    pairs = [(i, i + 1) for i in range(begin, lax.axis_size(axis) - 1, 2)]
+    return lax.ppermute(value, axis, pairs + [(b, a) for a, b in pairs])
 
 
 def kept(*shape):
@@ -383,39 +407,48 @@
 
 def body(e_field, h_field, polar, permittivity, resonance, dispersive):
     xcount, zcount, ycount = shape = permittivity.shape
-    ups, downs = faces(xcount)
-    up, down, side, res = call(
+    marks = jnp.swapaxes(dispersive, 1, 2)
+    face = kept(planes_of(faces()), zcount, ycount)
+    first, second, side, *fields = call(
         pack_faces,
-        [
-            kept(planes_of(ups), zcount, ycount),
-            kept(planes_of(downs), zcount, ycount),
-            kept(ARRAYS, xcount, ROWS, ycount),
-            kept(xcount, zcount, ycount),
+        [face, face, kept(ARRAYS, xcount, ROWS, ycount)]
+        + [kept(*a.shape) for a in (e_field, h_field, polar, permittivity, resonance)],
+        (e_field, h_field, polar, permittivity, resonance, marks),
+        1,
+        scratch=[
+            pltpu.VMEM(shape, jnp.float32),
+            pltpu.VMEM(marks.shape, marks.dtype),
+            pltpu.SemaphoreType.DMA((6,)),
         ],
-        (e_field, h_field, polar, permittivity, resonance, jnp.swapaxes(dispersive, 1, 2)),
-        COST,
+        spec=pltpu.HBM,
     )
-    side = swap(side)
-    low, high = shift(up, "gx", 1), shift(down, "gx", -1)
-    fields = (e_field, h_field, polar, permittivity, res, side)
-    strips = [kept(ARRAYS, zcount + ROWS, LANES)] * 2
-    first, last = call(pack_strips, strips, fields, COST)
-    ahead, behind = shift(first, "gy", -1), shift(last, "gy", 1)
-    strip_low, strip_high = call(merge_strips, strips, (ahead, behind), COST)
-    corner_low, corner_high = shift(strip_high, "gx", 1), shift(strip_low, "gx", -1)
+    side = swap(side, "gz")
+    second, first = swap(second, "gx", 1), swap(first, "gx")
+    fields = (*fields, side)
+    strip = kept(ARRAYS, zcount + ROWS, LANES)
+    strips = call(pack_strips, [strip] * 2, fields, 1)
+    *strips, fields = lax.optimization_barrier((*strips, fields))
+    strip_second, strip_first = swap(strips[1], "gy", 1), swap(strips[0], "gy")
     extent, tiles, rows = xcount + 2 * STEPS, ycount // LANES + 1, zcount + ROWS + 2 * GUARD
-    state = [kept(3, extent, tiles, rows, LANES)] * 4
-    state += [kept(extent, tiles, rows, LANES)] * 3 + [kept(extent, tiles, ROWS, LANES)] * 2
-    count = len(state)
-    kept_state = call(prepare, state, (*fields, strip_low, strip_high), 3 * COST)
-    low, high, kept_state = lax.optimization_barrier((low, high, kept_state))
-    low_side, high_side = swap(low), swap(high)
-    kept_state = call(functools.partial(inner, shape), state, kept_state, 6 * COST, {i: i for i in range(count)})
-    faces_in = (low, low_side, high, high_side, corner_low, corner_high)
-    given = len(faces_in)
+    states = [kept(3, extent, tiles, rows, LANES)] * 4
+    states += [kept(extent, tiles, rows, LANES)] * 3 + [kept(extent, tiles, ROWS, LANES)] * 2
+    count = len(states)
+    state = call(prepare, states, fields, 2)
+    low, high, corner_first, corner_second = call(merge_strips, [strip] * 4, (strip_first, strip_second), 0.2)
+    corner_second, corner_first = swap(corner_second, "gx", 1), swap(corner_first, "gx")
+    ends = functools.partial(prepare_ends, shape)
+    state = call(ends, states, (low, high, *state), 0.1, {2 + i: i for i in range(count)})
+    same = {i: i for i in range(count)}
+    state = call(functools.partial(inner, shape, 1, SPLIT), states, state, 0.1, same)
+    barrier = (first, second, corner_first, corner_second, state)
+    first, second, corner_first, corner_second, state = lax.optimization_barrier(barrier)
+    first_side, second_side = swap(first, "gz"), swap(second, "gz")
+    state = call(functools.partial(inner, shape, SPLIT, STEPS + 1), states, state, 0.1, same)
+    arrived = (first, first_side, second, second_side, corner_first, corner_second)
+    given = len(arrived)
     outs = [jax.ShapeDtypeStruct(e_field.shape, jnp.float32), jax.ShapeDtypeStruct(h_field.shape, jnp.float32)]
     aliases = {given + i: 2 + i for i in range(count)}
-    return tuple(call(functools.partial(outer, shape), outs + state, (*faces_in, *kept_state), 6 * COST, aliases)[:2])
+    return tuple(call(functools.partial(outer, shape), outs + states, (*arrived, *state), 1, aliases)[:2])
 
 
 def solution(mesh):

time: 52.9 us -> 41.4 us (0.78)
  the two profiles are of different devices: /device:TPU:0 before, /device:TPU:13 now
where the time goes in v3:
time: 41.4 us; the launch traced here: 41.1 us
  Pallas kernels  20.2 us (49%)
  starting transfers between devices  13.8 us (33%)
  waiting for transfers between devices  6.31 us (15%)
  between operations  0.75 us (2%)
    pallas_call x8, Pallas kernels, call(): pl.pallas_call(kernel, out_shape=outs, in_specs=[pl.BlockSpec(memory_spac...  20.2 us
    ppermute x9, starting transfers between devices, swap(): return lax.ppermute(value, axis, pairs + [(b, a) for a, b in pairs])  13.8 us
    ppermute x9, waiting for transfers between devices, swap(): return lax.ppermute(value, axis, pairs + [(b, a) for a, b in pairs])  6.31 us
  transfers between devices with their start and end apart: 9, of which 5 were waited for; matrix products, arithmetic and copies ran while one was open for 0% of the time, Pallas kernels for 27%

profile of v3, /device:TPU:13, one launch (start us, length us, event | category | flops | bytes accessed | tf_op | source)
XLA Modules:
  0.0 41.1 jit_solution(17450983146075284667)
XLA Ops:
  0.6 2.0 %shard_map.77 = (f32[49,16,256]{2,1,0:T(8,128)S(1)}, f32[49,16,256]{2,1,0:T(8,128)S(1)}, f32[11,16,8,256]{3,2,1,0:T(8,128)S(1)}, f32[3,16,16,256]{3,2,1,0:T(8,12...) custom-call(f32[3,16,16,256]{3,2,1,0:T(8,128)} %e_hbm.1, ...), custom_call_target="tpu_custom_call" | custom-call | flops 3000000 | bytes 3000000 | tf_op jit(solution)/shard_map/pallas_call | solution.py:387
  2.7 0.7 %collective-permute-start.2 = (f32[11,16,8,256]{3,2,1,0:T(8,128)S(1)}, f32[11,16,8,256]{3,2,1,0:T(8,128)S(1)}, u32[]{:S(2)}, u32[]{:S(2)}) collective-permute-start(f32[11,16,8,256]{3,2,1,0:T(8,128)S(1)} %get-tuple-element.82), channel_id=1, source_target_pairs={{0,1},{1,0},{2,3},{3,2},{4,5},{5,4},{6,7},{7,6},{8,9},{9,8},{10,11... | collective-permute-start | bytes 4325384 | tf_op jit(solution)/shard_map/ppermute | solution.py:401
  3.4 0.2 collective-permute-start
  3.6 4.3 %collective-permute-start.1 = (f32[49,16,256]{2,1,0:T(8,128)S(1)}, f32[49,16,256]{2,1,0:T(8,128)S(1)}, u32[]{:S(2)}, u32[]{:S(2)}) collective-permute-start(f32[49,16,256]{2,1,0:T(8,128)S(1)} %get-tuple-element.76), channel_id=1, source_target_pairs={{8,16},{16,8},{9,17},{17,9},{10,18},{18,10},{11,19},{19,11},{12,20... | collective-permute-start | bytes 2408456 | tf_op jit(solution)/shard_map/ppermute | solution.py:401
  7.9 0.0 collective-permute-done.2.side_ref
  7.9 2.4 %shard_map.78 = (f32[11,24,128]{2,1,0:T(8,128)S(1)}, f32[11,24,128]{2,1,0:T(8,128)S(1)}) custom-call(f32[3,16,16,256]{3,2,1,0:T(8,128)S(1)} %get-tuple-element.91.e_ref, f32[3,16,16,256]{3,2,1,0:T(8,128)S(1)} %get-tuple-element.92.h_ref, f32[3,16,16,256]{3,2,1,0:T(8,128)S(1)} %get-tuple-element.93.p_ref, f32[16,16,256]{2,1,0:T(8,128)S(1)} %get-tuple-element.94.eps_ref, ...), custom_call_target="tpu_custom_call" | custom-call | flops 3000000 | bytes 3000000 | tf_op jit(solution)/shard_map/pallas_call | solution.py:387
  10.4 1.3 %collective-permute-start.3 = (f32[11,24,128]{2,1,0:T(8,128)S(1)}, f32[11,24,128]{2,1,0:T(8,128)S(1)}, u32[]{:S(2)}, u32[]{:S(2)}) collective-permute-start(f32[11,24,128]{2,1,0:T(8,128)S(1)} %get-tuple-element.85), channel_id=1, source_target_pairs={{0,2},{4,6},{2,0},{6,4},{1,3},{5,7},{3,1},{7,5},{8,10},{12,14},{10... | collective-permute-start | bytes 405512 | tf_op jit(solution)/shard_map/ppermute | solution.py:401
  11.7 2.1 %collective-permute-start.4 = (f32[11,24,128]{2,1,0:T(8,128)S(1)}, f32[11,24,128]{2,1,0:T(8,128)S(1)}, u32[]{:S(2)}, u32[]{:S(2)}) collective-permute-start(f32[11,24,128]{2,1,0:T(8,128)S(1)} %get-tuple-element.86), channel_id=1, source_target_pairs={{2,4},{4,2},{3,5},{5,3},{10,12},{12,10},{11,13},{13,11},{18,20},{2... | collective-permute-start | bytes 405512 | tf_op jit(solution)/shard_map/ppermute | solution.py:401
  13.8 1.2 %collective-permute-done.3.first_ref = f32[11,24,128]{2,1,0:T(8,128)S(1)} collective-permute-done((f32[11,24,128]{2,1,0:T(8,128)S(1)}, f32[11,24,128]{2,1,0:T(8,128)S(1)}, u32[]{:S(2)}, u32[]{:S(2)}) %collective-permute-start.3) | collective-permute-done | bytes 135200 | tf_op jit(solution)/shard_map/ppermute | solution.py:401
  15.0 3.7 %collective-permute-done.4.second_ref = f32[11,24,128]{2,1,0:T(8,128)S(1)} collective-permute-done((f32[11,24,128]{2,1,0:T(8,128)S(1)}, f32[11,24,128]{2,1,0:T(8,128)S(1)}, u32[]{:S(2)}, u32[]{:S(2)}) %collective-permute-start.4) | collective-permute-done | bytes 135200 | tf_op jit(solution)/shard_map/ppermute | solution.py:401
  18.6 0.1 shard_map.79
  18.8 0.1 collective-permute-start.5
  18.9 3.1 %collective-permute-start.6 = (f32[11,24,128]{2,1,0:T(8,128)S(1)}, f32[11,24,128]{2,1,0:T(8,128)S(1)}, u32[]{:S(2)}, u32[]{:S(2)}) collective-permute-start(f32[11,24,128]{2,1,0:T(8,128)S(1)} %get-tuple-element.88), channel_id=1, source_target_pairs={{8,16},{16,8},{9,17},{17,9},{10,18},{18,10},{11,19},{19,11},{12,20... | collective-permute-start | bytes 405512 | tf_op jit(solution)/shard_map/ppermute | solution.py:401
  22.0 1.1 %shard_map.80 = (f32[3,26,3,40,128]{4,3,2,1,0:T(8,128)S(1)}, f32[3,26,3,40,128]{4,3,2,1,0:T(8,128)S(1)}, f32[3,26,3,40,128]{4,3,2,1,0:T(8,128)S(1)}, f32[3,26,3,...) custom-call(f32[3,16,16,256]{3,2,1,0:T(8,128)S(1)} %get-tuple-elemen, ...), custom_call_target="tpu_custom_call" | custom-call | flops 6000000 | bytes 6000000 | tf_op jit(solution)/shard_map/pallas_call | solution.py:387
  23.1 1.0 %shard_map.81 = (f32[3,26,3,40,128]{4,3,2,1,0:T(8,128)S(1)}, f32[3,26,3,40,128]{4,3,2,1,0:T(8,128)S(1)}, f32[3,26,3,40,128]{4,3,2,1,0:T(8,128)S(1)}, f32[3,26,3,...) custom-call(f32[11,24,128]{2,1,0:T(8,128)S(1)} %get-tuple-element.89, ...), custom_call_target="tpu_custom_call", output_to_operand_aliasing={{0}: (2, {}), {1}: (3, {}), {2}: (4, {}), {3}: (5, {}), {4}... | custom-call | flops 300000 | bytes 300000 | tf_op jit(solution)/shard_map/pallas_call | solution.py:387
  24.1 4.5 %shard_map.82 = (f32[3,26,3,40,128]{4,3,2,1,0:T(8,128)S(1)}, f32[3,26,3,40,128]{4,3,2,1,0:T(8,128)S(1)}, f32[3,26,3,40,128]{4,3,2,1,0:T(8,128)S(1)}, f32[3,26,3,...) custom-call(f32[3,26,3,40,128]{4,3,2,1,0:T(8,128)S(1)} %get-tuple-el, ...), custom_call_target="tpu_custom_call", output_to_operand_aliasing={{0}: (0, {}), {1}: (1, {}), {2}: (2, {}), {3}: (3, {}), {4}... | custom-call | flops 300000 | bytes 300000 | tf_op jit(solution)/shard_map/pallas_call | solution.py:387
  28.6 0.0 collective-permute-done.first_ref
  28.6 0.0 collective-permute-done.1.second_ref
  28.6 0.0 collective-permute-done.5.corner_first_ref
  28.6 0.2 collective-permute-done.6.corner_second_ref
  28.8 2.0 %collective-permute-start.7 = (f32[49,16,256]{2,1,0:T(8,128)S(1)}, f32[49,16,256]{2,1,0:T(8,128)S(1)}, u32[]{:S(2)}, u32[]{:S(2)}) collective-permute-start(f32[49,16,256]{2,1,0:T(8,128)S(1)} %collective-permute-done.first_ref), channel_id=1, source_target_pairs={{0,1},{1,0},{2,3},{3,2},{4,5},{5,4},{6,7},{7,6},{8,9},{9,8},{10,11... | collective-permute-start | bytes 2408456 | tf_op jit(solution)/shard_map/ppermute | solution.py:401
  30.8 0.1 collective-permute-start.8
  30.9 1.8 %shard_map.83 = (f32[3,26,3,40,128]{4,3,2,1,0:T(8,128)S(1)}, f32[3,26,3,40,128]{4,3,2,1,0:T(8,128)S(1)}, f32[3,26,3,40,128]{4,3,2,1,0:T(8,128)S(1)}, f32[3,26,3,...) custom-call(f32[3,26,3,40,128]{4,3,2,1,0:T(8,128)S(1)} %get-tuple-el, ...), custom_call_target="tpu_custom_call", output_to_operand_aliasing={{0}: (0, {}), {1}: (1, {}), {2}: (2, {}), {3}: (3, {}), {4}... | custom-call | flops 300000 | bytes 300000 | tf_op jit(solution)/shard_map/pallas_call | solution.py:387
  32.6 0.1 collective-permute-done.7.first_side_ref
  32.7 1.1 %collective-permute-done.8.second_side_ref = f32[49,16,256]{2,1,0:T(8,128)S(1)} collective-permute-done((f32[49,16,256]{2,1,0:T(8,128)S(1)}, f32[49,16,256]{2,1,0:T(8,128)S(1)}, u32[]{:S(2)}, u32[]{:S(2)}) %collective-permute-start.8) | collective-permute-done | bytes 802848 | tf_op jit(solution)/shard_map/ppermute | solution.py:401
  33.9 7.2 %shard_map.84 = (f32[3,16,16,256]{3,2,1,0:T(8,128)}, f32[3,16,16,256]{3,2,1,0:T(8,128)}, f32[3,26,3,40,128]{4,3,2,1,0:T(8,128)S(1)}, f32[3,26,3,40,128]{4,3,2,1,...) custom-call(f32[49,16,256]{2,1,0:T(8,128)S(1)} %collective-permute-d, ...), custom_call_target="tpu_custom_call", output_to_operand_aliasing={{2}: (6, {}), {3}: (7, {}), {4}: (8, {}), {5}: (9, {}), {6}... | custom-call | flops 3000000 | bytes 3000000 | tf_op jit(solution)/shard_map/pallas_call | solution.py:387
Async XLA Ops:
  2.7 5.3 %collective-permute-start.2 = (f32[11,16,8,256]{3,2,1,0:T(8,128)S(1)}, f32[11,16,8,256]{3,2,1,0:T(8,128)S(1)}, u32[]{:S(2)}, u32[]{:S(2)}) collective-permute-start(f32[11,16,8,256]{3,2,1,0:T(8,128)S(1)} %get-tuple-element.82), channel_id=1, source_target_pairs={{0,1},{1,0},{2,3},{3,2},{4,5},{5,4},{6,7},{7,6},{8,9},{9,8},{10,11... | collective-permute-start | bytes 4325384 | tf_op jit(solution)/shard_map/ppermute | solution.py:401
  3.4 25.2 %collective-permute-start = (f32[49,16,256]{2,1,0:T(8,128)S(1)}, f32[49,16,256]{2,1,0:T(8,128)S(1)}, u32[]{:S(2)}, u32[]{:S(2)}) collective-permute-start(f32[49,16,256]{2,1,0:T(8,128)S(1)} %get-tuple-element.75), channel_id=1, source_target_pairs={{0,8},{16,24},{8,0},{24,16},{1,9},{17,25},{9,1},{25,17},{2,10},{18... | collective-permute-start | bytes 2408456 | tf_op jit(solution)/shard_map/ppermute | solution.py:401
  3.6 25.0 %collective-permute-start.1 = (f32[49,16,256]{2,1,0:T(8,128)S(1)}, f32[49,16,256]{2,1,0:T(8,128)S(1)}, u32[]{:S(2)}, u32[]{:S(2)}) collective-permute-start(f32[49,16,256]{2,1,0:T(8,128)S(1)} %get-tuple-element.76), channel_id=1, source_target_pairs={{8,16},{16,8},{9,17},{17,9},{10,18},{18,10},{11,19},{19,11},{12,20... | collective-permute-start | bytes 2408456 | tf_op jit(solution)/shard_map/ppermute | solution.py:401
  10.4 4.6 %collective-permute-start.3 = (f32[11,24,128]{2,1,0:T(8,128)S(1)}, f32[11,24,128]{2,1,0:T(8,128)S(1)}, u32[]{:S(2)}, u32[]{:S(2)}) collective-permute-start(f32[11,24,128]{2,1,0:T(8,128)S(1)} %get-tuple-element.85), channel_id=1, source_target_pairs={{0,2},{4,6},{2,0},{6,4},{1,3},{5,7},{3,1},{7,5},{8,10},{12,14},{10... | collective-permute-start | bytes 405512 | tf_op jit(solution)/shard_map/ppermute | solution.py:401
  11.7 7.0 %collective-permute-start.4 = (f32[11,24,128]{2,1,0:T(8,128)S(1)}, f32[11,24,128]{2,1,0:T(8,128)S(1)}, u32[]{:S(2)}, u32[]{:S(2)}) collective-permute-start(f32[11,24,128]{2,1,0:T(8,128)S(1)} %get-tuple-element.86), channel_id=1, source_target_pairs={{2,4},{4,2},{3,5},{5,3},{10,12},{12,10},{11,13},{13,11},{18,20},{2... | collective-permute-start | bytes 405512 | tf_op jit(solution)/shard_map/ppermute | solution.py:401
  18.8 9.8 %collective-permute-start.5 = (f32[11,24,128]{2,1,0:T(8,128)S(1)}, f32[11,24,128]{2,1,0:T(8,128)S(1)}, u32[]{:S(2)}, u32[]{:S(2)}) collective-permute-start(f32[11,24,128]{2,1,0:T(8,128)S(1)} %get-tuple-element.87), channel_id=1, source_target_pairs={{0,8},{16,24},{8,0},{24,16},{1,9},{17,25},{9,1},{25,17},{2,10},{18... | collective-permute-start | bytes 405512 | tf_op jit(solution)/shard_map/ppermute | solution.py:401
  18.9 9.9 %collective-permute-start.6 = (f32[11,24,128]{2,1,0:T(8,128)S(1)}, f32[11,24,128]{2,1,0:T(8,128)S(1)}, u32[]{:S(2)}, u32[]{:S(2)}) collective-permute-start(f32[11,24,128]{2,1,0:T(8,128)S(1)} %get-tuple-element.88), channel_id=1, source_target_pairs={{8,16},{16,8},{9,17},{17,9},{10,18},{18,10},{11,19},{19,11},{12,20... | collective-permute-start | bytes 405512 | tf_op jit(solution)/shard_map/ppermute | solution.py:401
  28.8 3.9 %collective-permute-start.7 = (f32[49,16,256]{2,1,0:T(8,128)S(1)}, f32[49,16,256]{2,1,0:T(8,128)S(1)}, u32[]{:S(2)}, u32[]{:S(2)}) collective-permute-start(f32[49,16,256]{2,1,0:T(8,128)S(1)} %collective-permute-done.first_ref), channel_id=1, source_target_pairs={{0,1},{1,0},{2,3},{3,2},{4,5},{5,4},{6,7},{7,6},{8,9},{9,8},{10,11... | collective-permute-start | bytes 2408456 | tf_op jit(solution)/shard_map/ppermute | solution.py:401
  30.8 3.1 %collective-permute-start.8 = (f32[49,16,256]{2,1,0:T(8,128)S(1)}, f32[49,16,256]{2,1,0:T(8,128)S(1)}, u32[]{:S(2)}, u32[]{:S(2)}) collective-permute-start(f32[49,16,256]{2,1,0:T(8,128)S(1)} %collective-permute-done.1.second_ref), channel_id=1, source_target_pairs={{0,1},{1,0},{2,3},{3,2},{4,5},{5,4},{6,7},{7,6},{8,9},{9,8},{10,11... | collective-permute-start | bytes 2408456 | tf_op jit(solution)/shard_map/ppermute | solution.py:401

commit v4 on v3

--- a/solution.py
+++ b/solution.py
@@ -7,7 +7,9 @@
 from jax.sharding import PartitionSpec as P
 
 STEPS = 5
-SPLIT = 4
+SPLIT = 3
+AHEAD = 2
+GROUP = 8
 NPML = 8
 DT = 0.5
 DAMPING = 0.1
@@ -61,22 +63,25 @@
     freq_ref, mark_ref, arrived,
 ):
     xcount, zcount, ycount = eps_ref.shape
-    moves = [
-        pltpu.make_async_copy(src, dst, arrived.at[i])
-        for i, (src, dst) in enumerate(
-            (
-                (mark_hbm, mark_ref),
-                (freq_hbm, freq_ref),
-                (eps_hbm, eps_ref),
-                (e_hbm, e_ref),
-                (h_hbm, h_ref),
-                (p_hbm, p_ref),
-            )
-        )
-    ]
+    xcount = eps_ref.shape[0]
+    pairs = ((mark_hbm, mark_ref), (freq_hbm, freq_ref), (eps_hbm, eps_ref))
+    pairs += ((e_hbm, e_ref), (h_hbm, h_ref), (p_hbm, p_ref))
+    moves = [pltpu.make_async_copy(src, dst, arrived.at[i]) for i, (src, dst) in enumerate(pairs)]
     for move in moves:
         move.start()
-    core = lax.axis_index("gz")
+    refs = (e_ref, h_ref, p_ref, eps_ref, res_ref)
+    begin = pl.multiple_of((1 - lax.axis_index("gz")) * (zcount - ROWS), ROWS)
+
+    def pack(arrays):
+        for up, out_ref in ((even("gx"), first_ref), (jnp.logical_not(even("gx")), second_ref)):
+            at = 0
+            for array, count in faces():
+                for i in range(count if array in arrays else 0):
+                    out_ref[at + i] = pick(refs, array)[jnp.where(up, xcount - 1 - i, i)]
+                at += count
+        for array in arrays:
+            side_ref[array] = pick(refs, array)[:, pl.ds(begin, ROWS), :]
+
     shape = (zcount, zcount)
     diagonal = lax.broadcasted_iota(jnp.int32, shape, 0) == lax.broadcasted_iota(jnp.int32, shape, 1)
     moves[0].wait()
@@ -88,18 +93,11 @@
             mark = jnp.sum(jnp.where(diagonal, row, 0.0), axis=1, keepdims=True)
             freq = freq_ref[x, :, lanes] * DT
             res_ref[x, :, lanes] = mark * (freq * freq / DENOM)
-    for move in moves[2:]:
+    moves[2].wait()
+    pack((EPS, RES))
+    for move, array in zip(moves[3:], (EX, HX, PX)):
         move.wait()
-    refs = (e_ref, h_ref, p_ref, eps_ref, res_ref)
-    for up, out_ref in ((even("gx"), first_ref), (jnp.logical_not(even("gx")), second_ref)):
-        at = 0
-        for array, count in faces():
-            for i in range(count):
-                out_ref[at + i] = pick(refs, array)[jnp.where(up, xcount - 1 - i, i)]
-            at += count
-    begin = pl.multiple_of((1 - core) * (zcount - ROWS), ROWS)
-    for array in range(ARRAYS):
-        side_ref[array] = pick(refs, array)[:, pl.ds(begin, ROWS), :]
+        pack(range(array, array + 3))
 
 
 def slots():
@@ -122,20 +120,24 @@
     per = LANES // SLOT
     assert xcount == 2 * per and per >= STEPS
     up = even("gy")
+    zs = range(0, zcount + ROWS, ROWS)
     for array in range(ARRAYS):
         src = pick(refs, array)
-        for z in range(0, zcount + ROWS, ROWS):
-            packed = [jnp.zeros((ROWS, LANES), jnp.float32)] * 2
-            for x in range(xcount):
+        packed = [[None, None] for _ in zs]
+        for x in range(xcount):
+            for n, z in enumerate(zs):
                 if z < zcount:
                     first, last = src[x, z : z + ROWS, 0:LANES], src[x, z : z + ROWS, ycount - LANES : ycount]
                 else:
                     first, last = side_ref[array, x, :, 0:LANES], side_ref[array, x, :, ycount - LANES : ycount]
                 ends = turn(jnp.where(lane < SIDE, first, last), SLOT * (x % per) + SIDE)
-                packed[x // per] = jnp.where(slot == x % per, ends, packed[x // per])
+                before = packed[n][x // per]
+                packed[n][x // per] = ends if before is None else jnp.where(slot == x % per, ends, before)
+        for n, z in enumerate(zs):
+            p = packed[n]
             rows = pl.ds(own + z, ROWS) if z < zcount else pl.ds(halo, ROWS)
-            low = jnp.where(left, turn(packed[1], -SIDE), packed[0])
-            high = jnp.where(left, packed[0], turn(packed[1], SIDE))
+            low = jnp.where(left, turn(p[1], -SIDE), p[0])
+            high = jnp.where(left, p[0], turn(p[1], SIDE))
             first_ref[array, rows, :] = jnp.where(up, high, low)
             second_ref[array, rows, :] = jnp.where(up, low, high)
 
@@ -214,8 +216,8 @@
             self.HC[x, j] = jnp.where(inside, (1.0 - half) * over, 0.0)
             self.HB[x, j] = jnp.where(inside, (DT / 6.0) * over, 0.0)
 
-    def electric_coefficients(self, x):
-        for j in range(self.tiles + 1):
+    def electric_coefficients(self, x, columns):
+        for j in columns:
             half, inside = self.place(x, j)
             for t in range(self.zsteps):
                 rows = pl.ds(GUARD + t * ROWS, ROWS)
@@ -243,15 +245,25 @@
         r = [turn(t, 1) for t in v]
         return [jnp.where(self.lane == 0, r[j - 1], r[j]) for j in range(len(v))]
 
-    def magnetic(self, x):
+    def magnetic(self, *planes):
         E, H = self.E, self.H
-        for t in range(self.zsteps):
-            row = GUARD + t * ROWS
+        places = [(x, GUARD + t * ROWS) for x in planes for t in range(self.zsteps)]
+        rolled = {}
+
+        def turned(n):
+            x, row = places[n]
+            rolled[n] = [self.next_lane(self.load(E, c, x, row)) for c in (0, 2)]
+
+        for n in range(min(AHEAD, len(places))):
+            turned(n)
+        for n, (x, row) in enumerate(places):
+            if n + AHEAD < len(places):
+                turned(n + AHEAD)
             rows = pl.ds(row, ROWS)
             ex, ey, ez = (self.load(E, c, x, row) for c in range(3))
             ex_z, ey_z = (self.load(E, c, x, row + 1) for c in (0, 1))
             ey_x, ez_x = (self.load(E, c, x + 1, row) for c in (1, 2))
-            ex_y, ez_y = self.next_lane(ex), self.next_lane(ez)
+            ex_y, ez_y = rolled.pop(n)
             for j in range(self.tiles + 1):
                 hc, hb = self.HC[x, j], self.HB[x, j]
                 curls = (
@@ -262,16 +274,27 @@
                 for c in range(3):
                     H[c, x, j, rows, :] = hc * H[c, x, j, rows, :] - hb * curls[c]
 
-    def electric(self, x, step):
+    def electric(self, *planes, step, out=None):
         E, H, R, U = self.E, self.H, self.R, self.U
         last = step == STEPS
-        for t in range(self.zsteps - 1 if last else self.zsteps):
-            row = self.own + t * ROWS if last else GUARD + t * ROWS
+        zsteps = range(self.zsteps - 1 if last else self.zsteps)
+        places = [(x, self.own + t * ROWS if last else GUARD + t * ROWS) for x in planes for t in zsteps]
+        rolled = {}
+
+        def turned(n):
+            x, row = places[n]
+            rolled[n] = [self.previous_lane(self.load(H, c, x, row)) for c in (0, 2)]
+
+        for n in range(min(AHEAD, len(places))):
+            turned(n)
+        for n, (x, row) in enumerate(places):
+            if n + AHEAD < len(places):
+                turned(n + AHEAD)
             rows = pl.ds(row, ROWS)
             hx, hy, hz = (self.load(H, c, x, row) for c in range(3))
             hx_z, hy_z = (self.load(H, c, x, row - 1) for c in (0, 1))
             hy_x, hz_x = (self.load(H, c, x - 1, row) for c in (1, 2))
-            hx_y, hz_y = self.previous_lane(hx), self.previous_lane(hz)
+            hx_y, hz_y = rolled.pop(n)
             for j in range(self.tiles if last else self.tiles + 1):
                 ec, eb, bm = (ref[x, j, rows, :] for ref in (self.EC, self.EB, self.BM))
                 curls = (
@@ -287,7 +310,28 @@
                     if not last:
                         U[c, x, j, rows, :] = u
                         R[c, x, j, rows, :] = r + u
-                    E[c, x, j, rows, :] = ec * e + eb * (curls[c] - u)
+                    value = ec * e + eb * (curls[c] - u)
+                    if out is None:
+                        E[c, x, j, rows, :] = value
+                    else:
+                        z = (n % len(zsteps)) * ROWS
+                        out[c, x - STEPS, z : z + ROWS, j * LANES : (j + 1) * LANES] = value
+
+
+def groups(begin, end, act, size):
+    whole = (end - begin) // size
+
+    def run(n, carry):
+        x = begin + n * size
+        act(*(x + i for i in range(size)))
+        return carry
+
+    if whole > 1:
+        lax.fori_loop(0, whole, run, 0)
+    elif whole:
+        act(*range(begin, begin + size))
+    if begin + whole * size < end:
+        act(*range(begin + whole * size, end))
 
 
 def loop(begin, end, act, unroll):
@@ -314,6 +358,8 @@
         loop(0, block.xcount, own_plane, 4)
     loop(0, block.extent, block.guards, 1)
     loop(0, block.extent, block.magnetic_coefficients, 2)
+    coefficients = functools.partial(block.electric_coefficients, columns=range(block.tiles))
+    loop(STEPS, STEPS + block.xcount, coefficients, 2)
 
 
 def prepare_ends(shape, low_ref, high_ref, *states):
@@ -322,73 +368,116 @@
     for array in range(ARRAYS):
         for x in range(block.xcount):
             block.put_ends(array, x + STEPS, low_ref if x < per else high_ref, x % per)
-    loop(STEPS, STEPS + block.xcount, block.electric_coefficients, 2)
+    coefficients = functools.partial(block.electric_coefficients, columns=(block.tiles,))
+    loop(STEPS, STEPS + block.xcount, coefficients, 2)
+
+
+def groups(begin, end, act, size):
+    whole = (end - begin) // size
+
+    def run(n, carry):
+        x = begin + n * size
+        act(*(x + i for i in range(size)))
+        return carry
+
+    if whole > 1:
+        lax.fori_loop(0, whole, run, 0)
+    elif whole:
+        act(*range(begin, begin + size))
+    if begin + whole * size < end:
+        act(*range(begin + whole * size, end))
 
 
 def inner(shape, begin, end, *states):
     block = Block(shape, states[len(states) // 2 :])
     for step in range(begin, end):
-        loop(STEPS + step - 1, STEPS + block.xcount - step, block.magnetic, 4)
-        loop(STEPS + step, STEPS + block.xcount - step, functools.partial(block.electric, step=step), 4)
-
-
-def outer(
-    shape, first_ref, first_side_ref, second_ref, second_side_ref, corner_first_ref, corner_second_ref, *rest
-):
-    count = (len(rest) - 2) // 2
-    e_out, h_out = rest[count : count + 2]
-    block = Block(shape, rest[count + 2 :])
-    xcount, zcount = block.xcount, block.zcount
+        last = STEPS + block.xcount - step
+        groups(STEPS + step - 1, last, block.magnetic, GROUP)
+        groups(STEPS + step, last, functools.partial(block.electric, step=step), GROUP)
+
+
+def arrivals(block, first, second):
     per = LANES // SLOT
-    for above, face, face_side, corner in (
-        (even("gx"), first_ref, first_side_ref, corner_first_ref),
-        (jnp.logical_not(even("gx")), second_ref, second_side_ref, corner_second_ref),
-    ):
+    for above, refs in ((even("gx"), first), (jnp.logical_not(even("gx")), second)):
         at = 0
         for array, count in faces():
             for i in range(count):
-                plane = jnp.where(above, xcount + STEPS + i, STEPS - 1 - i)
+                plane = jnp.where(above, block.xcount + STEPS + i, STEPS - 1 - i)
+                yield array, plane, at + i, jnp.where(above, i, per - 1 - i), *refs
+            at += count
+
+
+def inner_end(shape, first_ref, second_ref, corner_first_ref, corner_second_ref, *states):
+    inner(shape, SPLIT, STEPS + 1, *states)
+    block = Block(shape, states[len(states) // 2 :])
+    came = arrivals(block, (first_ref, corner_first_ref), (second_ref, corner_second_ref))
+    for array, plane, at, slot, face, corner in came:
+        for j in range(block.tiles):
+            for z in range(0, block.zcount, ROWS):
+                block.put(array, plane, block.own + z, j, face[at, z : z + ROWS, j * LANES : (j + 1) * LANES])
+        block.put_ends(array, plane, corner, slot)
+
+
+def outer(shape, first_side_ref, second_side_ref, *rest):
+    e_stage, h_stage, sent = rest[-3:]
+    count = (len(rest) - 5) // 2
+    e_out, h_out = rest[count : count + 2]
+    block = Block(shape, rest[count + 2 : -3])
+    xcount, zcount = block.xcount, block.zcount
+    moves = []
+
+    def send(stage, out, begin, end):
+        part = slice(begin - STEPS, end - STEPS)
+        move = pltpu.make_async_copy(stage.at[:, part], out.at[:, part], sent.at[len(moves)])
+        move.start()
+        moves.append(move)
+
+    def stage(ref, into, scale, begin, end):
+        for x in range(begin, end):
+            for c in range(3):
                 for j in range(block.tiles):
                     lanes = slice(j * LANES, (j + 1) * LANES)
                     for z in range(0, zcount, ROWS):
-                        block.put(array, plane, block.own + z, j, face[at + i, z : z + ROWS, lanes])
-                    block.put(array, plane, block.halo, j, face_side[at + i, pl.ds(block.near, ROWS), lanes])
-                block.put_ends(array, plane, corner, jnp.where(above, i, per - 1 - i))
-            at += count
-    loop(1, STEPS, block.electric_coefficients, STEPS - 1)
-    loop(STEPS + xcount, block.extent - 1, block.electric_coefficients, STEPS - 1)
+                        value = ref[c, x, j, pl.ds(block.own + z, ROWS), :]
+                        into[c, x - STEPS, z : z + ROWS, lanes] = value if scale is None else value * scale
+
+    middle = (2 * STEPS, xcount)
+    stage(block.E, e_stage, None, *middle)
+    send(e_stage, e_out, *middle)
+    stage(block.H, h_stage, 6.0, *middle)
+    send(h_stage, h_out, *middle)
+    for array, plane, at, _, side in arrivals(block, (first_side_ref,), (second_side_ref,)):
+        for j in range(block.tiles):
+            value = side[at, pl.ds(block.near, ROWS), j * LANES : (j + 1) * LANES]
+            block.put(array, plane, block.halo, j, value)
+    coefficients = functools.partial(block.electric_coefficients, columns=range(block.tiles + 1))
+    loop(1, STEPS, coefficients, STEPS - 1)
+    loop(STEPS + xcount, block.extent - 1, coefficients, STEPS - 1)
     for step in range(1, STEPS + 1):
         above = xcount + STEPS - step
-
-        def both(x, act, gap):
-            act(x)
-            act(x + gap)
-
-        low = step - 1
-        loop(low, low + STEPS, functools.partial(both, act=block.magnetic, gap=above - low), STEPS)
+        block.magnetic(*range(step - 1, step - 1 + STEPS), *range(above, above + STEPS))
         act = functools.partial(block.electric, step=step)
-        loop(step, step + STEPS, functools.partial(both, act=act, gap=above - step), STEPS)
-
-    def finish(x):
-        for c in range(3):
-            for j in range(block.tiles):
-                lanes = slice(j * LANES, (j + 1) * LANES)
-                for z in range(0, zcount, ROWS):
-                    rows = pl.ds(block.own + z, ROWS)
-                    e_out[c, x, z : z + ROWS, lanes] = block.E[c, x + STEPS, j, rows, :]
-                    h_out[c, x, z : z + ROWS, lanes] = block.H[c, x + STEPS, j, rows, :] * 6.0
-
-    loop(0, xcount, finish, 2)
-
-
-def call(kernel, outs, args, cost, aliases=None, scratch=(), spec=pltpu.VMEM):
+        low, high = range(step, step + STEPS), range(above, above + STEPS)
+        if step < STEPS:
+            act(*low, *high)
+        else:
+            for part in (low, high):
+                stage(block.H, h_stage, 6.0, part.start, part.stop)
+                send(h_stage, h_out, part.start, part.stop)
+                act(*part, out=e_stage)
+                send(e_stage, e_out, part.start, part.stop)
+    for move in moves:
+        move.wait()
+
+
+def call(kernel, outs, args, cost, aliases=None, scratch=(), spec=pltpu.VMEM, hbm=0):
     args = [pltpu.with_memory_space_constraint(a, spec) for a in args]
     work = int(cost * COST)
     return pl.pallas_call(
         kernel,
         out_shape=outs,
         in_specs=[pl.BlockSpec(memory_space=spec)] * len(args),
-        out_specs=[pl.BlockSpec(memory_space=pltpu.VMEM)] * len(outs),
+        out_specs=[pl.BlockSpec(memory_space=pltpu.HBM if i < hbm else pltpu.VMEM) for i in range(len(outs))],
         scratch_shapes=scratch,
         input_output_aliases=aliases or {},
         cost_estimate=pl.CostEstimate(flops=work, bytes_accessed=work, transcendentals=0),
@@ -434,6 +523,7 @@
     states += [kept(extent, tiles, rows, LANES)] * 3 + [kept(extent, tiles, ROWS, LANES)] * 2
     count = len(states)
     state = call(prepare, states, fields, 2)
+    strip_first, strip_second, state = lax.optimization_barrier((strip_first, strip_second, state))
     low, high, corner_first, corner_second = call(merge_strips, [strip] * 4, (strip_first, strip_second), 0.2)
     corner_second, corner_first = swap(corner_second, "gx", 1), swap(corner_first, "gx")
     ends = functools.partial(prepare_ends, shape)
@@ -443,12 +533,15 @@
     barrier = (first, second, corner_first, corner_second, state)
     first, second, corner_first, corner_second, state = lax.optimization_barrier(barrier)
     first_side, second_side = swap(first, "gz"), swap(second, "gz")
-    state = call(functools.partial(inner, shape, SPLIT, STEPS + 1), states, state, 0.1, same)
-    arrived = (first, first_side, second, second_side, corner_first, corner_second)
-    given = len(arrived)
+    came = (first, second, corner_first, corner_second)
+    given = len(came)
+    aliases = {given + i: i for i in range(count)}
+    state = call(functools.partial(inner_end, shape), states, (*came, *state), 0.1, aliases)
     outs = [jax.ShapeDtypeStruct(e_field.shape, jnp.float32), jax.ShapeDtypeStruct(h_field.shape, jnp.float32)]
-    aliases = {given + i: 2 + i for i in range(count)}
-    return tuple(call(functools.partial(outer, shape), outs + states, (*arrived, *state), 1, aliases)[:2])
+    scratch = [pltpu.VMEM(e_field.shape, jnp.float32)] * 2 + [pltpu.SemaphoreType.DMA((6,))]
+    aliases = {2 + i: 2 + i for i in range(count)}
+    ends = (first_side, second_side, *state)
+    return tuple(call(functools.partial(outer, shape), outs + states, ends, 1, aliases, scratch, hbm=2)[:2])
 
 
 def solution(mesh):

time: 41.4 us -> 38.6 us (0.932)
  Pallas kernels: 20.2 us -> 16.3 us
  waiting for transfers between devices: 6.31 us -> 8.56 us
  starting transfers between devices: 13.8 us -> 12.6 us
    pallas_call x8, Pallas kernels: 20.2 us -> 16.3 us  [call(): pl.pallas_call(kernel, out_shape=outs, in_specs=[pl.BlockSpec(memory_spac...]
    ppermute x9, waiting for transfers between devices: 6.31 us -> 8.56 us  [swap(): return lax.ppermute(value, axis, pairs + [(b, a) for a, b in pairs])]
    ppermute x9, starting transfers between devices: 13.8 us -> 12.6 us  [swap(): return lax.ppermute(value, axis, pairs + [(b, a) for a, b in pairs])]
  transfers between devices with their start and end apart: 9 -> 9, of which waited for: 5 -> 4; matrix products, arithmetic and copies ran while one was open for 0% -> 0% of each run, Pallas kernels for 27% -> 23%
where the time goes in v4:
time: 38.6 us; the launch traced here: 38.2 us
  Pallas kernels  16.3 us (42%)
  starting transfers between devices  12.6 us (33%)
  waiting for transfers between devices  8.56 us (22%)
  between operations  0.75 us (2%)
    pallas_call x8, Pallas kernels, call(): pl.pallas_call(kernel, out_shape=outs, in_specs=[pl.BlockSpec(memory_spac...  16.3 us
    ppermute x9, starting transfers between devices, swap(): return lax.ppermute(value, axis, pairs + [(b, a) for a, b in pairs])  12.6 us
    ppermute x9, waiting for transfers between devices, swap(): return lax.ppermute(value, axis, pairs + [(b, a) for a, b in pairs])  8.56 us
  transfers between devices with their start and end apart: 9, of which 4 were waited for; matrix products, arithmetic and copies ran while one was open for 0% of the time, Pallas kernels for 23%

profile of v4, /device:TPU:13, one launch (start us, length us, event | category | flops | bytes accessed | tf_op | source)
XLA Modules:
  0.0 38.2 jit_solution(12829235404624447103)
XLA Ops:
  0.6 1.9 %shard_map.77 = (f32[49,16,256]{2,1,0:T(8,128)S(1)}, f32[49,16,256]{2,1,0:T(8,128)S(1)}, f32[11,16,8,256]{3,2,1,0:T(8,128)S(1)}, f32[3,16,16,256]{3,2,1,0:T(8,12...) custom-call(f32[3,16,16,256]{3,2,1,0:T(8,128)} %e_hbm.1, ...), custom_call_target="tpu_custom_call" | custom-call | flops 3000000 | bytes 3000000 | tf_op jit(solution)/shard_map/pallas_call | solution.py:476
  2.5 0.7 %collective-permute-start.2 = (f32[11,16,8,256]{3,2,1,0:T(8,128)S(1)}, f32[11,16,8,256]{3,2,1,0:T(8,128)S(1)}, u32[]{:S(2)}, u32[]{:S(2)}) collective-permute-start(f32[11,16,8,256]{3,2,1,0:T(8,128)S(1)} %get-tuple-element.93), channel_id=1, source_target_pairs={{0,1},{1,0},{2,3},{3,2},{4,5},{5,4},{6,7},{7,6},{8,9},{9,8},{10,11... | collective-permute-start | bytes 4325384 | tf_op jit(solution)/shard_map/ppermute | solution.py:490
  3.3 0.2 collective-permute-start
  3.5 4.3 %collective-permute-start.1 = (f32[49,16,256]{2,1,0:T(8,128)S(1)}, f32[49,16,256]{2,1,0:T(8,128)S(1)}, u32[]{:S(2)}, u32[]{:S(2)}) collective-permute-start(f32[49,16,256]{2,1,0:T(8,128)S(1)} %get-tuple-element.87), channel_id=1, source_target_pairs={{8,16},{16,8},{9,17},{17,9},{10,18},{18,10},{11,19},{19,11},{12,20... | collective-permute-start | bytes 2408456 | tf_op jit(solution)/shard_map/ppermute | solution.py:490
  7.8 0.0 collective-permute-done.2.side_ref
  7.8 1.3 %shard_map.78 = (f32[11,24,128]{2,1,0:T(8,128)S(1)}, f32[11,24,128]{2,1,0:T(8,128)S(1)}) custom-call(f32[3,16,16,256]{3,2,1,0:T(8,128)S(1)} %get-tuple-element.98.e_ref, f32[3,16,16,256]{3,2,1,0:T(8,128)S(1)} %get-tuple-element.99.h_ref, f32[3,16,16,256]{3,2,1,0:T(8,128)S(1)} %get-tuple-element.100.p_ref, f32[16,16,256]{2,1,0:T(8,128)S(1)} %get-tuple-element.101.eps_ref, ...), custom_call_target="tpu_custom_call" | custom-call | flops 3000000 | bytes 3000000 | tf_op jit(solution)/shard_map/pallas_call | solution.py:476
  9.1 1.3 %collective-permute-start.3 = (f32[11,24,128]{2,1,0:T(8,128)S(1)}, f32[11,24,128]{2,1,0:T(8,128)S(1)}, u32[]{:S(2)}, u32[]{:S(2)}) collective-permute-start(f32[11,24,128]{2,1,0:T(8,128)S(1)} %get-tuple-element.96), channel_id=1, source_target_pairs={{0,2},{4,6},{2,0},{6,4},{1,3},{5,7},{3,1},{7,5},{8,10},{12,14},{10... | collective-permute-start | bytes 405512 | tf_op jit(solution)/shard_map/ppermute | solution.py:490
  10.4 2.1 %collective-permute-start.4 = (f32[11,24,128]{2,1,0:T(8,128)S(1)}, f32[11,24,128]{2,1,0:T(8,128)S(1)}, u32[]{:S(2)}, u32[]{:S(2)}) collective-permute-start(f32[11,24,128]{2,1,0:T(8,128)S(1)} %get-tuple-element.97), channel_id=1, source_target_pairs={{2,4},{4,2},{3,5},{5,3},{10,12},{12,10},{11,13},{13,11},{18,20},{2... | collective-permute-start | bytes 405512 | tf_op jit(solution)/shard_map/ppermute | solution.py:490
  12.5 1.4 %shard_map.79 = (f32[3,26,3,40,128]{4,3,2,1,0:T(8,128)S(1)}, f32[3,26,3,40,128]{4,3,2,1,0:T(8,128)S(1)}, f32[3,26,3,40,128]{4,3,2,1,0:T(8,128)S(1)}, f32[3,26,3,...) custom-call(f32[3,16,16,256]{3,2,1,0:T(8,128)S(1)} %get-tuple-elemen, ...), custom_call_target="tpu_custom_call" | custom-call | flops 6000000 | bytes 6000000 | tf_op jit(solution)/shard_map/pallas_call | solution.py:476
  13.8 0.0 collective-permute-done.3.first_ref
  13.8 3.5 %collective-permute-done.4.second_ref = f32[11,24,128]{2,1,0:T(8,128)S(1)} collective-permute-done((f32[11,24,128]{2,1,0:T(8,128)S(1)}, f32[11,24,128]{2,1,0:T(8,128)S(1)}, u32[]{:S(2)}, u32[]{:S(2)}) %collective-permute-start.4) | collective-permute-done | bytes 135200 | tf_op jit(solution)/shard_map/ppermute | solution.py:490
  17.3 0.1 shard_map.80
  17.5 0.1 collective-permute-start.5
  17.6 3.1 %collective-permute-start.6 = (f32[11,24,128]{2,1,0:T(8,128)S(1)}, f32[11,24,128]{2,1,0:T(8,128)S(1)}, u32[]{:S(2)}, u32[]{:S(2)}) collective-permute-start(f32[11,24,128]{2,1,0:T(8,128)S(1)} %get-tuple-element.116), channel_id=1, source_target_pairs={{8,16},{16,8},{9,17},{17,9},{10,18},{18,10},{11,19},{19,11},{12,20... | collective-permute-start | bytes 405512 | tf_op jit(solution)/shard_map/ppermute | solution.py:490
  20.7 0.9 %shard_map.81 = (f32[3,26,3,40,128]{4,3,2,1,0:T(8,128)S(1)}, f32[3,26,3,40,128]{4,3,2,1,0:T(8,128)S(1)}, f32[3,26,3,40,128]{4,3,2,1,0:T(8,128)S(1)}, f32[3,26,3,...) custom-call(f32[11,24,128]{2,1,0:T(8,128)S(1)} %get-tuple-element.11, ...), custom_call_target="tpu_custom_call", output_to_operand_aliasing={{0}: (2, {}), {1}: (3, {}), {2}: (4, {}), {3}: (5, {}), {4}... | custom-call | flops 300000 | bytes 300000 | tf_op jit(solution)/shard_map/pallas_call | solution.py:476
  21.5 2.4 %shard_map.82 = (f32[3,26,3,40,128]{4,3,2,1,0:T(8,128)S(1)}, f32[3,26,3,40,128]{4,3,2,1,0:T(8,128)S(1)}, f32[3,26,3,40,128]{4,3,2,1,0:T(8,128)S(1)}, f32[3,26,3,...) custom-call(f32[3,26,3,40,128]{4,3,2,1,0:T(8,128)S(1)} %get-tuple-el, ...), custom_call_target="tpu_custom_call", output_to_operand_aliasing={{0}: (0, {}), {1}: (1, {}), {2}: (2, {}), {3}: (3, {}), {4}... | custom-call | flops 300000 | bytes 300000 | tf_op jit(solution)/shard_map/pallas_call | solution.py:476
  24.0 0.0 collective-permute-done.first_ref
  24.0 1.8 %collective-permute-done.1.second_ref = f32[49,16,256]{2,1,0:T(8,128)S(1)} collective-permute-done((f32[49,16,256]{2,1,0:T(8,128)S(1)}, f32[49,16,256]{2,1,0:T(8,128)S(1)}, u32[]{:S(2)}, u32[]{:S(2)}) %collective-permute-start.1) | collective-permute-done | bytes 802848 | tf_op jit(solution)/shard_map/ppermute | solution.py:490
  25.8 0.0 collective-permute-done.5.corner_first_ref
  25.8 2.9 %collective-permute-done.6.corner_second_ref = f32[11,24,128]{2,1,0:T(8,128)S(1)} collective-permute-done((f32[11,24,128]{2,1,0:T(8,128)S(1)}, f32[11,24,128]{2,1,0:T(8,128)S(1)}, u32[]{:S(2)}, u32[]{:S(2)}) %collective-permute-start.6) | collective-permute-done | bytes 135200 | tf_op jit(solution)/shard_map/ppermute | solution.py:490
  28.7 0.8 %collective-permute-start.7 = (f32[49,16,256]{2,1,0:T(8,128)S(1)}, f32[49,16,256]{2,1,0:T(8,128)S(1)}, u32[]{:S(2)}, u32[]{:S(2)}) collective-permute-start(f32[49,16,256]{2,1,0:T(8,128)S(1)} %collective-permute-done.first_ref), channel_id=1, source_target_pairs={{0,1},{1,0},{2,3},{3,2},{4,5},{5,4},{6,7},{7,6},{8,9},{9,8},{10,11... | collective-permute-start | bytes 2408456 | tf_op jit(solution)/shard_map/ppermute | solution.py:490
  29.5 0.0 collective-permute-start.8
  29.5 2.7 %shard_map.83 = (f32[3,26,3,40,128]{4,3,2,1,0:T(8,128)S(1)}, f32[3,26,3,40,128]{4,3,2,1,0:T(8,128)S(1)}, f32[3,26,3,40,128]{4,3,2,1,0:T(8,128)S(1)}, f32[3,26,3,...) custom-call(f32[49,16,256]{2,1,0:T(8,128)S(1)} %collective-permute-d, ...), custom_call_target="tpu_custom_call", output_to_operand_aliasing={{0}: (4, {}), {1}: (5, {}), {2}: (6, {}), {3}: (7, {}), {4}... | custom-call | flops 300000 | bytes 300000 | tf_op jit(solution)/shard_map/pallas_call | solution.py:476
  32.2 0.0 collective-permute-done.7.first_side_ref
  32.2 0.4 collective-permute-done.8.second_side_ref
  32.6 5.6 %shard_map.84 = (f32[3,16,16,256]{3,2,1,0:T(8,128)}, f32[3,16,16,256]{3,2,1,0:T(8,128)}, f32[3,26,3,40,128]{4,3,2,1,0:T(8,128)S(1)}, f32[3,26,3,40,128]{4,3,2,1,...) custom-call(f32[49,16,256]{2,1,0:T(8,128)S(1)} %collective-permute-d, ...), custom_call_target="tpu_custom_call", output_to_operand_aliasing={{2}: (2, {}), {3}: (3, {}), {4}: (4, {}), {5}: (5, {}), {6}... | custom-call | flops 3000000 | bytes 3000000 | tf_op jit(solution)/shard_map/pallas_call | solution.py:476
Async XLA Ops:
  2.5 5.3 %collective-permute-start.2 = (f32[11,16,8,256]{3,2,1,0:T(8,128)S(1)}, f32[11,16,8,256]{3,2,1,0:T(8,128)S(1)}, u32[]{:S(2)}, u32[]{:S(2)}) collective-permute-start(f32[11,16,8,256]{3,2,1,0:T(8,128)S(1)} %get-tuple-element.93), channel_id=1, source_target_pairs={{0,1},{1,0},{2,3},{3,2},{4,5},{5,4},{6,7},{7,6},{8,9},{9,8},{10,11... | collective-permute-start | bytes 4325384 | tf_op jit(solution)/shard_map/ppermute | solution.py:490
  3.3 20.7 %collective-permute-start = (f32[49,16,256]{2,1,0:T(8,128)S(1)}, f32[49,16,256]{2,1,0:T(8,128)S(1)}, u32[]{:S(2)}, u32[]{:S(2)}) collective-permute-start(f32[49,16,256]{2,1,0:T(8,128)S(1)} %get-tuple-element.86), channel_id=1, source_target_pairs={{0,8},{16,24},{8,0},{24,16},{1,9},{17,25},{9,1},{25,17},{2,10},{18... | collective-permute-start | bytes 2408456 | tf_op jit(solution)/shard_map/ppermute | solution.py:490
  3.5 22.3 %collective-permute-start.1 = (f32[49,16,256]{2,1,0:T(8,128)S(1)}, f32[49,16,256]{2,1,0:T(8,128)S(1)}, u32[]{:S(2)}, u32[]{:S(2)}) collective-permute-start(f32[49,16,256]{2,1,0:T(8,128)S(1)} %get-tuple-element.87), channel_id=1, source_target_pairs={{8,16},{16,8},{9,17},{17,9},{10,18},{18,10},{11,19},{19,11},{12,20... | collective-permute-start | bytes 2408456 | tf_op jit(solution)/shard_map/ppermute | solution.py:490
  9.1 4.7 %collective-permute-start.3 = (f32[11,24,128]{2,1,0:T(8,128)S(1)}, f32[11,24,128]{2,1,0:T(8,128)S(1)}, u32[]{:S(2)}, u32[]{:S(2)}) collective-permute-start(f32[11,24,128]{2,1,0:T(8,128)S(1)} %get-tuple-element.96), channel_id=1, source_target_pairs={{0,2},{4,6},{2,0},{6,4},{1,3},{5,7},{3,1},{7,5},{8,10},{12,14},{10... | collective-permute-start | bytes 405512 | tf_op jit(solution)/shard_map/ppermute | solution.py:490
  10.4 7.0 %collective-permute-start.4 = (f32[11,24,128]{2,1,0:T(8,128)S(1)}, f32[11,24,128]{2,1,0:T(8,128)S(1)}, u32[]{:S(2)}, u32[]{:S(2)}) collective-permute-start(f32[11,24,128]{2,1,0:T(8,128)S(1)} %get-tuple-element.97), channel_id=1, source_target_pairs={{2,4},{4,2},{3,5},{5,3},{10,12},{12,10},{11,13},{13,11},{18,20},{2... | collective-permute-start | bytes 405512 | tf_op jit(solution)/shard_map/ppermute | solution.py:490
  17.5 8.3 %collective-permute-start.5 = (f32[11,24,128]{2,1,0:T(8,128)S(1)}, f32[11,24,128]{2,1,0:T(8,128)S(1)}, u32[]{:S(2)}, u32[]{:S(2)}) collective-permute-start(f32[11,24,128]{2,1,0:T(8,128)S(1)} %get-tuple-element.115), channel_id=1, source_target_pairs={{0,8},{16,24},{8,0},{24,16},{1,9},{17,25},{9,1},{25,17},{2,10},{18... | collective-permute-start | bytes 405512 | tf_op jit(solution)/shard_map/ppermute | solution.py:490
  17.6 11.1 %collective-permute-start.6 = (f32[11,24,128]{2,1,0:T(8,128)S(1)}, f32[11,24,128]{2,1,0:T(8,128)S(1)}, u32[]{:S(2)}, u32[]{:S(2)}) collective-permute-start(f32[11,24,128]{2,1,0:T(8,128)S(1)} %get-tuple-element.116), channel_id=1, source_target_pairs={{8,16},{16,8},{9,17},{17,9},{10,18},{18,10},{11,19},{19,11},{12,20... | collective-permute-start | bytes 405512 | tf_op jit(solution)/shard_map/ppermute | solution.py:490
  28.7 3.6 %collective-permute-start.7 = (f32[49,16,256]{2,1,0:T(8,128)S(1)}, f32[49,16,256]{2,1,0:T(8,128)S(1)}, u32[]{:S(2)}, u32[]{:S(2)}) collective-permute-start(f32[49,16,256]{2,1,0:T(8,128)S(1)} %collective-permute-done.first_ref), channel_id=1, source_target_pairs={{0,1},{1,0},{2,3},{3,2},{4,5},{5,4},{6,7},{7,6},{8,9},{9,8},{10,11... | collective-permute-start | bytes 2408456 | tf_op jit(solution)/shard_map/ppermute | solution.py:490
  29.5 3.1 %collective-permute-start.8 = (f32[49,16,256]{2,1,0:T(8,128)S(1)}, f32[49,16,256]{2,1,0:T(8,128)S(1)}, u32[]{:S(2)}, u32[]{:S(2)}) collective-permute-start(f32[49,16,256]{2,1,0:T(8,128)S(1)} %collective-permute-done.1.second_ref), channel_id=1, source_target_pairs={{0,1},{1,0},{2,3},{3,2},{4,5},{5,4},{6,7},{7,6},{8,9},{9,8},{10,11... | collective-permute-start | bytes 2408456 | tf_op jit(solution)/shard_map/ppermute | solution.py:490

commit v5 on v4

--- a/solution.py
+++ b/solution.py
@@ -7,7 +7,6 @@
 from jax.sharding import PartitionSpec as P
 
 STEPS = 5
-SPLIT = 3
 AHEAD = 2
 GROUP = 8
 NPML = 8
@@ -143,19 +142,31 @@
 
 
 def merge_strips(first_ref, second_ref, low_ref, high_ref, corner_first_ref, corner_second_ref):
-    _, _, left = slots()
+    _, slot, left = slots()
     up, over = even("gy"), even("gx")
-    for array in range(ARRAYS):
-        for t in range(first_ref.shape[1] // ROWS):
-            rows = slice(t * ROWS, (t + 1) * ROWS)
+    per = LANES // SLOT
+    for t in range(first_ref.shape[1] // ROWS):
+        rows = slice(t * ROWS, (t + 1) * ROWS)
+        packed = ([None] * (corner_rows() + 1), [None] * (corner_rows() + 1))
+        for array in range(ARRAYS):
             first, second = first_ref[array, rows, :], second_ref[array, rows, :]
             ahead, behind = jnp.where(up, first, second), jnp.where(up, second, first)
             low = jnp.where(left, behind, ahead)
             high = jnp.where(left, turn(behind, -SIDE), turn(ahead, SIDE))
             low_ref[array, rows, :] = low
             high_ref[array, rows, :] = high
-            corner_first_ref[array, rows, :] = jnp.where(over, high, low)
-            corner_second_ref[array, rows, :] = jnp.where(over, low, high)
+            at, place = divmod(STEPS * array, per)
+            begin, end = turn(low, SLOT * place), turn(high, SLOT * (place - per + STEPS))
+            for into, value in zip(packed, (jnp.where(over, end, begin), jnp.where(over, begin, end))):
+                into[at] = value if into[at] is None else jnp.where(slot >= place, value, into[at])
+                into[at + 1] = value if place + STEPS > per else None
+        for into, out_ref in zip(packed, (corner_first_ref, corner_second_ref)):
+            for n in range(corner_rows()):
+                out_ref[n, rows, :] = into[n]
+
+
+def corner_rows():
+    return -(-STEPS * ARRAYS // (LANES // SLOT))
 
 
 def profile(index, total):
@@ -173,7 +184,6 @@
         core = lax.axis_index("gz")
         self.own = pl.multiple_of(GUARD + core * ROWS, ROWS)
         self.halo = pl.multiple_of(GUARD + (1 - core) * self.zcount, ROWS)
-        self.near = pl.multiple_of(core * (self.zcount - ROWS), ROWS)
         self.lane = lax.broadcasted_iota(jnp.int32, (ROWS, LANES), 1)
 
     def put(self, array, plane, row, j, value):
@@ -189,9 +199,9 @@
         else:
             self.BM[plane, j, rows, :] = value
 
-    def put_ends(self, array, plane, packed, slot):
+    def put_ends(self, array, plane, packed, slot, row=None):
         for t in range(self.zsteps):
-            ends = pltpu.roll(packed[array, t * ROWS : (t + 1) * ROWS, :], LANES - SIDE - SLOT * slot, 1)
+            ends = pltpu.roll(packed[array if row is None else row, t * ROWS : (t + 1) * ROWS, :], LANES - SIDE - SLOT * slot, 1)
             self.put(array, plane, GUARD + t * ROWS, self.tiles, ends)
 
     def place(self, x, j):
@@ -216,11 +226,11 @@
             self.HC[x, j] = jnp.where(inside, (1.0 - half) * over, 0.0)
             self.HB[x, j] = jnp.where(inside, (DT / 6.0) * over, 0.0)
 
-    def electric_coefficients(self, x, columns):
+    def electric_coefficients(self, x, columns, at=None):
         for j in columns:
             half, inside = self.place(x, j)
-            for t in range(self.zsteps):
-                rows = pl.ds(GUARD + t * ROWS, ROWS)
+            for row in at or range(GUARD, GUARD + self.zsteps * ROWS, ROWS):
+                rows = pl.ds(row, ROWS)
                 eps = self.EC[x, j, rows, :]
                 over = 1.0 / jnp.where(inside, eps + half, 1.0)
                 self.EC[x, j, rows, :] = jnp.where(inside, (eps - half) * over, 0.0)
@@ -388,37 +398,49 @@
         act(*range(begin + whole * size, end))
 
 
-def inner(shape, begin, end, *states):
+def inner(shape, *states):
     block = Block(shape, states[len(states) // 2 :])
-    for step in range(begin, end):
+    for step in range(1, STEPS + 1):
         last = STEPS + block.xcount - step
         groups(STEPS + step - 1, last, block.magnetic, GROUP)
         groups(STEPS + step, last, functools.partial(block.electric, step=step), GROUP)
 
 
+def pack_near(first_ref, second_ref, near_ref):
+    begin = pl.multiple_of((1 - lax.axis_index("gz")) * (first_ref.shape[1] - ROWS), ROWS)
+    near_ref[0] = first_ref[:, pl.ds(begin, ROWS), :]
+    near_ref[1] = second_ref[:, pl.ds(begin, ROWS), :]
+
+
 def arrivals(block, first, second):
-    per = LANES // SLOT
     for above, refs in ((even("gx"), first), (jnp.logical_not(even("gx")), second)):
         at = 0
         for array, count in faces():
             for i in range(count):
                 plane = jnp.where(above, block.xcount + STEPS + i, STEPS - 1 - i)
-                yield array, plane, at + i, jnp.where(above, i, per - 1 - i), *refs
+                yield array, plane, at + i, STEPS * array + jnp.where(above, i, STEPS - 1 - i), *refs
             at += count
 
 
-def inner_end(shape, first_ref, second_ref, corner_first_ref, corner_second_ref, *states):
-    inner(shape, SPLIT, STEPS + 1, *states)
+def halo_planes(block):
+    return (*range(1, STEPS), *range(STEPS + block.xcount, block.extent - 1))
+
+
+def place_arrivals(shape, first_ref, second_ref, corner_first_ref, corner_second_ref, *states):
     block = Block(shape, states[len(states) // 2 :])
+    per = LANES // SLOT
     came = arrivals(block, (first_ref, corner_first_ref), (second_ref, corner_second_ref))
     for array, plane, at, slot, face, corner in came:
         for j in range(block.tiles):
             for z in range(0, block.zcount, ROWS):
                 block.put(array, plane, block.own + z, j, face[at, z : z + ROWS, j * LANES : (j + 1) * LANES])
-        block.put_ends(array, plane, corner, slot)
-
-
-def outer(shape, first_side_ref, second_side_ref, *rest):
+        block.put_ends(array, plane, corner, lax.rem(slot, per), lax.div(slot, per))
+    for plane in halo_planes(block):
+        block.electric_coefficients(plane, range(block.tiles), [block.own + z for z in range(0, block.zcount, ROWS)])
+        block.electric_coefficients(plane, (block.tiles,))
+
+
+def outer(shape, near_ref, *rest):
     e_stage, h_stage, sent = rest[-3:]
     count = (len(rest) - 5) // 2
     e_out, h_out = rest[count : count + 2]
@@ -446,13 +468,12 @@
     send(e_stage, e_out, *middle)
     stage(block.H, h_stage, 6.0, *middle)
     send(h_stage, h_out, *middle)
-    for array, plane, at, _, side in arrivals(block, (first_side_ref,), (second_side_ref,)):
+    for array, plane, at, _, side in arrivals(block, (near_ref.at[0],), (near_ref.at[1],)):
         for j in range(block.tiles):
-            value = side[at, pl.ds(block.near, ROWS), j * LANES : (j + 1) * LANES]
+            value = side[at, :, j * LANES : (j + 1) * LANES]
             block.put(array, plane, block.halo, j, value)
-    coefficients = functools.partial(block.electric_coefficients, columns=range(block.tiles + 1))
-    loop(1, STEPS, coefficients, STEPS - 1)
-    loop(STEPS + xcount, block.extent - 1, coefficients, STEPS - 1)
+    for plane in halo_planes(block):
+        block.electric_coefficients(plane, range(block.tiles), (block.halo,))
     for step in range(1, STEPS + 1):
         above = xcount + STEPS - step
         block.magnetic(*range(step - 1, step - 1 + STEPS), *range(above, above + STEPS))
@@ -515,6 +536,7 @@
     second, first = swap(second, "gx", 1), swap(first, "gx")
     fields = (*fields, side)
     strip = kept(ARRAYS, zcount + ROWS, LANES)
+    corner = kept(corner_rows(), zcount + ROWS, LANES)
     strips = call(pack_strips, [strip] * 2, fields, 1)
     *strips, fields = lax.optimization_barrier((*strips, fields))
     strip_second, strip_first = swap(strips[1], "gy", 1), swap(strips[0], "gy")
@@ -524,23 +546,23 @@
     count = len(states)
     state = call(prepare, states, fields, 2)
     strip_first, strip_second, state = lax.optimization_barrier((strip_first, strip_second, state))
-    low, high, corner_first, corner_second = call(merge_strips, [strip] * 4, (strip_first, strip_second), 0.2)
+    low, high, corner_first, corner_second = call(merge_strips, [strip] * 2 + [corner] * 2, (strip_first, strip_second), 0.2)
     corner_second, corner_first = swap(corner_second, "gx", 1), swap(corner_first, "gx")
     ends = functools.partial(prepare_ends, shape)
     state = call(ends, states, (low, high, *state), 0.1, {2 + i: i for i in range(count)})
     same = {i: i for i in range(count)}
-    state = call(functools.partial(inner, shape, 1, SPLIT), states, state, 0.1, same)
-    barrier = (first, second, corner_first, corner_second, state)
-    first, second, corner_first, corner_second, state = lax.optimization_barrier(barrier)
-    first_side, second_side = swap(first, "gz"), swap(second, "gz")
+    state = call(functools.partial(inner, shape), states, state, 0.1, same)
+    first, second, state = lax.optimization_barrier((first, second, state))
     came = (first, second, corner_first, corner_second)
-    given = len(came)
-    aliases = {given + i: i for i in range(count)}
-    state = call(functools.partial(inner_end, shape), states, (*came, *state), 0.1, aliases)
+    near = call(pack_near, [kept(2, planes_of(faces()), ROWS, ycount)], (first, second), 0.2)[0]
+    near, came, state = lax.optimization_barrier((near, came, state))
+    near = swap(near, "gz")
+    aliases = {len(came) + i: i for i in range(count)}
+    state = call(functools.partial(place_arrivals, shape), states, (*came, *state), 0.1, aliases)
     outs = [jax.ShapeDtypeStruct(e_field.shape, jnp.float32), jax.ShapeDtypeStruct(h_field.shape, jnp.float32)]
     scratch = [pltpu.VMEM(e_field.shape, jnp.float32)] * 2 + [pltpu.SemaphoreType.DMA((6,))]
-    aliases = {2 + i: 2 + i for i in range(count)}
-    ends = (first_side, second_side, *state)
+    aliases = {1 + i: 2 + i for i in range(count)}
+    ends = (near, *state)
     return tuple(call(functools.partial(outer, shape), outs + states, ends, 1, aliases, scratch, hbm=2)[:2])
 
 

time: 38.6 us -> 36.4 us (0.943)
  waiting for transfers between devices: 8.56 us -> 6.15 us
    ppermute x9 -> x8, waiting for transfers between devices: 8.56 us -> 6.15 us  [swap(): return lax.ppermute(value, axis, pairs + [(b, a) for a, b in pairs])]
    pallas_call x8 -> x9, Pallas kernels: 16.3 us -> 16.5 us  [call(): pl.pallas_call(kernel, out_shape=outs, in_specs=[pl.BlockSpec(memory_spac...]
    ppermute x9 -> x8, starting transfers between devices: 12.6 us -> 12.7 us  [swap(): return lax.ppermute(value, axis, pairs + [(b, a) for a, b in pairs])]
  transfers between devices with their start and end apart: 9 -> 8, of which waited for: 4 -> 3; matrix products, arithmetic and copies ran while one was open for 0% -> 0% of each run, Pallas kernels for 23% -> 25%
where the time goes in v5:
time: 36.4 us; the launch traced here: 36.1 us
  Pallas kernels  16.5 us (45%)
  starting transfers between devices  12.7 us (35%)
  waiting for transfers between devices  6.15 us (17%)
  between operations  0.76 us (2%)
    pallas_call x9, Pallas kernels, call(): pl.pallas_call(kernel, out_shape=outs, in_specs=[pl.BlockSpec(memory_spac...  16.5 us
    ppermute x8, starting transfers between devices, swap(): return lax.ppermute(value, axis, pairs + [(b, a) for a, b in pairs])  12.7 us
    ppermute x8, waiting for transfers between devices, swap(): return lax.ppermute(value, axis, pairs + [(b, a) for a, b in pairs])  6.15 us
  transfers between devices with their start and end apart: 8, of which 3 were waited for; matrix products, arithmetic and copies ran while one was open for 0% of the time, Pallas kernels for 25%

profile of v5, /device:TPU:13, one launch (start us, length us, event | category | flops | bytes accessed | tf_op | source)
XLA Modules:
  0.0 36.1 jit_solution(8578237413609638808)
XLA Ops:
  0.6 1.9 %shard_map.77 = (f32[49,16,256]{2,1,0:T(8,128)S(1)}, f32[49,16,256]{2,1,0:T(8,128)S(1)}, f32[11,16,8,256]{3,2,1,0:T(8,128)S(1)}, f32[3,16,16,256]{3,2,1,0:T(8,12...) custom-call(f32[3,16,16,256]{3,2,1,0:T(8,128)} %e_hbm.1, ...), custom_call_target="tpu_custom_call" | custom-call | flops 3000000 | bytes 3000000 | tf_op jit(solution)/shard_map/pallas_call | solution.py:497
  2.5 0.7 %collective-permute-start.2 = (f32[11,16,8,256]{3,2,1,0:T(8,128)S(1)}, f32[11,16,8,256]{3,2,1,0:T(8,128)S(1)}, u32[]{:S(2)}, u32[]{:S(2)}) collective-permute-start(f32[11,16,8,256]{3,2,1,0:T(8,128)S(1)} %get-tuple-element.105), channel_id=1, source_target_pairs={{0,1},{1,0},{2,3},{3,2},{4,5},{5,4},{6,7},{7,6},{8,9},{9,8},{10,11... | collective-permute-start | bytes 4325384 | tf_op jit(solution)/shard_map/ppermute | solution.py:511
  3.3 0.2 collective-permute-start
  3.5 4.3 %collective-permute-start.1 = (f32[49,16,256]{2,1,0:T(8,128)S(1)}, f32[49,16,256]{2,1,0:T(8,128)S(1)}, u32[]{:S(2)}, u32[]{:S(2)}) collective-permute-start(f32[49,16,256]{2,1,0:T(8,128)S(1)} %get-tuple-element.99), channel_id=1, source_target_pairs={{8,16},{16,8},{9,17},{17,9},{10,18},{18,10},{11,19},{19,11},{12,20... | collective-permute-start | bytes 2408456 | tf_op jit(solution)/shard_map/ppermute | solution.py:511
  7.8 0.0 collective-permute-done.2.side_ref
  7.8 1.3 %shard_map.78 = (f32[11,24,128]{2,1,0:T(8,128)S(1)}, f32[11,24,128]{2,1,0:T(8,128)S(1)}) custom-call(f32[3,16,16,256]{3,2,1,0:T(8,128)S(1)} %get-tuple-element.110.e_ref, f32[3,16,16,256]{3,2,1,0:T(8,128)S(1)} %get-tuple-element.111.h_ref, f32[3,16,16,256]{3,2,1,0:T(8,128)S(1)} %get-tuple-element.112.p_ref, f32[16,16,256]{2,1,0:T(8,128)S(1)} %get-tuple-element.113.eps_ref, ...), custom_call_target="tpu_custom_call" | custom-call | flops 3000000 | bytes 3000000 | tf_op jit(solution)/shard_map/pallas_call | solution.py:497
  9.1 1.3 %collective-permute-start.3 = (f32[11,24,128]{2,1,0:T(8,128)S(1)}, f32[11,24,128]{2,1,0:T(8,128)S(1)}, u32[]{:S(2)}, u32[]{:S(2)}) collective-permute-start(f32[11,24,128]{2,1,0:T(8,128)S(1)} %get-tuple-element.108), channel_id=1, source_target_pairs={{0,2},{4,6},{2,0},{6,4},{1,3},{5,7},{3,1},{7,5},{8,10},{12,14},{10... | collective-permute-start | bytes 405512 | tf_op jit(solution)/shard_map/ppermute | solution.py:511
  10.4 2.1 %collective-permute-start.4 = (f32[11,24,128]{2,1,0:T(8,128)S(1)}, f32[11,24,128]{2,1,0:T(8,128)S(1)}, u32[]{:S(2)}, u32[]{:S(2)}) collective-permute-start(f32[11,24,128]{2,1,0:T(8,128)S(1)} %get-tuple-element.109), channel_id=1, source_target_pairs={{2,4},{4,2},{3,5},{5,3},{10,12},{12,10},{11,13},{13,11},{18,20},{2... | collective-permute-start | bytes 405512 | tf_op jit(solution)/shard_map/ppermute | solution.py:511
  12.5 1.4 %shard_map.79 = (f32[3,26,3,40,128]{4,3,2,1,0:T(8,128)S(1)}, f32[3,26,3,40,128]{4,3,2,1,0:T(8,128)S(1)}, f32[3,26,3,40,128]{4,3,2,1,0:T(8,128)S(1)}, f32[3,26,3,...) custom-call(f32[3,16,16,256]{3,2,1,0:T(8,128)S(1)} %get-tuple-elemen, ...), custom_call_target="tpu_custom_call" | custom-call | flops 6000000 | bytes 6000000 | tf_op jit(solution)/shard_map/pallas_call | solution.py:497
  13.8 0.0 collective-permute-done.3.first_ref
  13.8 3.5 %collective-permute-done.4.second_ref = f32[11,24,128]{2,1,0:T(8,128)S(1)} collective-permute-done((f32[11,24,128]{2,1,0:T(8,128)S(1)}, f32[11,24,128]{2,1,0:T(8,128)S(1)}, u32[]{:S(2)}, u32[]{:S(2)}) %collective-permute-start.4) | collective-permute-done | bytes 135200 | tf_op jit(solution)/shard_map/ppermute | solution.py:511
  17.3 0.3 shard_map.80
  17.6 0.0 collective-permute-start.5
  17.6 3.1 %collective-permute-start.6 = (f32[7,24,128]{2,1,0:T(8,128)S(1)}, f32[7,24,128]{2,1,0:T(8,128)S(1)}, u32[]{:S(2)}, u32[]{:S(2)}) collective-permute-start(f32[7,24,128]{2,1,0:T(8,128)S(1)} %get-tuple-element.159), channel_id=1, source_target_pairs={{8,16},{16,8},{9,17},{17,9},{10,18},{18,10},{11,19},{19,11},{12,20... | collective-permute-start | bytes 258056 | tf_op jit(solution)/shard_map/ppermute | solution.py:511
  20.7 0.9 %shard_map.81 = (f32[3,26,3,40,128]{4,3,2,1,0:T(8,128)S(1)}, f32[3,26,3,40,128]{4,3,2,1,0:T(8,128)S(1)}, f32[3,26,3,40,128]{4,3,2,1,0:T(8,128)S(1)}, f32[3,26,3,...) custom-call(f32[11,24,128]{2,1,0:T(8,128)S(1)} %get-tuple-element.12, ...), custom_call_target="tpu_custom_call", output_to_operand_aliasing={{0}: (2, {}), {1}: (3, {}), {2}: (4, {}), {3}: (5, {}), {4}... | custom-call | flops 300000 | bytes 300000 | tf_op jit(solution)/shard_map/pallas_call | solution.py:497
  21.6 4.7 %shard_map.82 = (f32[3,26,3,40,128]{4,3,2,1,0:T(8,128)S(1)}, f32[3,26,3,40,128]{4,3,2,1,0:T(8,128)S(1)}, f32[3,26,3,40,128]{4,3,2,1,0:T(8,128)S(1)}, f32[3,26,3,...) custom-call(f32[3,26,3,40,128]{4,3,2,1,0:T(8,128)S(1)} %get-tuple-el, ...), custom_call_target="tpu_custom_call", output_to_operand_aliasing={{0}: (0, {}), {1}: (1, {}), {2}: (2, {}), {3}: (3, {}), {4}... | custom-call | flops 300000 | bytes 300000 | tf_op jit(solution)/shard_map/pallas_call | solution.py:497
  26.3 0.0 collective-permute-done.first_ref
  26.3 0.0 collective-permute-done.1.second_ref
  26.3 0.1 shard_map.83
  26.4 0.0 collective-permute-done.5.corner_first_ref
  26.4 1.2 %collective-permute-done.6.corner_second_ref = f32[7,24,128]{2,1,0:T(8,128)S(1)} collective-permute-done((f32[7,24,128]{2,1,0:T(8,128)S(1)}, f32[7,24,128]{2,1,0:T(8,128)S(1)}, u32[]{:S(2)}, u32[]{:S(2)}) %collective-permute-start.6) | collective-permute-done | bytes 86048 | tf_op jit(solution)/shard_map/ppermute | solution.py:511
  27.6 1.0 %collective-permute-start.7 = (f32[2,49,8,256]{3,2,1,0:T(8,128)S(1)}, f32[2,49,8,256]{3,2,1,0:T(8,128)S(1)}, u32[]{:S(2)}, u32[]{:S(2)}) collective-permute-start(f32[2,49,8,256]{3,2,1,0:T(8,128)S(1)} %shard_map.83), channel_id=1, source_target_pairs={{0,1},{1,0},{2,3},{3,2},{4,5},{5,4},{6,7},{7,6},{8,9},{9,8},{10,11... | collective-permute-start | bytes 2408456 | tf_op jit(solution)/shard_map/ppermute | solution.py:511
  28.6 0.5 %shard_map.84 = (f32[3,26,3,40,128]{4,3,2,1,0:T(8,128)S(1)}, f32[3,26,3,40,128]{4,3,2,1,0:T(8,128)S(1)}, f32[3,26,3,40,128]{4,3,2,1,0:T(8,128)S(1)}, f32[3,26,3,...) custom-call(f32[49,16,256]{2,1,0:T(8,128)S(1)} %collective-permute-d, ...), custom_call_target="tpu_custom_call", output_to_operand_aliasing={{0}: (4, {}), {1}: (5, {}), {2}: (6, {}), {3}: (7, {}), {4}... | custom-call | flops 300000 | bytes 300000 | tf_op jit(solution)/shard_map/pallas_call | solution.py:497
  29.1 1.4 %collective-permute-done.7.near_ref = f32[2,49,8,256]{3,2,1,0:T(8,128)S(1)} collective-permute-done((f32[2,49,8,256]{3,2,1,0:T(8,128)S(1)}, f32[2,49,8,256]{3,2,1,0:T(8,128)S(1)}, u32[]{:S(2)}, u32[]{:S(2)}) %collective-permute-start.7) | collective-permute-done | bytes 802848 | tf_op jit(solution)/shard_map/ppermute | solution.py:511
  30.5 5.6 %shard_map.85 = (f32[3,16,16,256]{3,2,1,0:T(8,128)}, f32[3,16,16,256]{3,2,1,0:T(8,128)}, f32[3,26,3,40,128]{4,3,2,1,0:T(8,128)S(1)}, f32[3,26,3,40,128]{4,3,2,1,...) custom-call(f32[2,49,8,256]{3,2,1,0:T(8,128)S(1)} %collective-permut, ...), custom_call_target="tpu_custom_call", output_to_operand_aliasing={{2}: (1, {}), {3}: (2, {}), {4}: (3, {}), {5}: (4, {}), {6}... | custom-call | flops 3000000 | bytes 3000000 | tf_op jit(solution)/shard_map/pallas_call | solution.py:497
Async XLA Ops:
  2.5 5.3 %collective-permute-start.2 = (f32[11,16,8,256]{3,2,1,0:T(8,128)S(1)}, f32[11,16,8,256]{3,2,1,0:T(8,128)S(1)}, u32[]{:S(2)}, u32[]{:S(2)}) collective-permute-start(f32[11,16,8,256]{3,2,1,0:T(8,128)S(1)} %get-tuple-element.105), channel_id=1, source_target_pairs={{0,1},{1,0},{2,3},{3,2},{4,5},{5,4},{6,7},{7,6},{8,9},{9,8},{10,11... | collective-permute-start | bytes 4325384 | tf_op jit(solution)/shard_map/ppermute | solution.py:511
  3.3 23.0 %collective-permute-start = (f32[49,16,256]{2,1,0:T(8,128)S(1)}, f32[49,16,256]{2,1,0:T(8,128)S(1)}, u32[]{:S(2)}, u32[]{:S(2)}) collective-permute-start(f32[49,16,256]{2,1,0:T(8,128)S(1)} %get-tuple-element.98), channel_id=1, source_target_pairs={{0,8},{16,24},{8,0},{24,16},{1,9},{17,25},{9,1},{25,17},{2,10},{18... | collective-permute-start | bytes 2408456 | tf_op jit(solution)/shard_map/ppermute | solution.py:511
  3.5 22.9 %collective-permute-start.1 = (f32[49,16,256]{2,1,0:T(8,128)S(1)}, f32[49,16,256]{2,1,0:T(8,128)S(1)}, u32[]{:S(2)}, u32[]{:S(2)}) collective-permute-start(f32[49,16,256]{2,1,0:T(8,128)S(1)} %get-tuple-element.99), channel_id=1, source_target_pairs={{8,16},{16,8},{9,17},{17,9},{10,18},{18,10},{11,19},{19,11},{12,20... | collective-permute-start | bytes 2408456 | tf_op jit(solution)/shard_map/ppermute | solution.py:511
  9.1 4.7 %collective-permute-start.3 = (f32[11,24,128]{2,1,0:T(8,128)S(1)}, f32[11,24,128]{2,1,0:T(8,128)S(1)}, u32[]{:S(2)}, u32[]{:S(2)}) collective-permute-start(f32[11,24,128]{2,1,0:T(8,128)S(1)} %get-tuple-element.108), channel_id=1, source_target_pairs={{0,2},{4,6},{2,0},{6,4},{1,3},{5,7},{3,1},{7,5},{8,10},{12,14},{10... | collective-permute-start | bytes 405512 | tf_op jit(solution)/shard_map/ppermute | solution.py:511
  10.4 7.0 %collective-permute-start.4 = (f32[11,24,128]{2,1,0:T(8,128)S(1)}, f32[11,24,128]{2,1,0:T(8,128)S(1)}, u32[]{:S(2)}, u32[]{:S(2)}) collective-permute-start(f32[11,24,128]{2,1,0:T(8,128)S(1)} %get-tuple-element.109), channel_id=1, source_target_pairs={{2,4},{4,2},{3,5},{5,3},{10,12},{12,10},{11,13},{13,11},{18,20},{2... | collective-permute-start | bytes 405512 | tf_op jit(solution)/shard_map/ppermute | solution.py:511
  17.6 8.8 %collective-permute-start.5 = (f32[7,24,128]{2,1,0:T(8,128)S(1)}, f32[7,24,128]{2,1,0:T(8,128)S(1)}, u32[]{:S(2)}, u32[]{:S(2)}) collective-permute-start(f32[7,24,128]{2,1,0:T(8,128)S(1)} %get-tuple-element.158), channel_id=1, source_target_pairs={{0,8},{16,24},{8,0},{24,16},{1,9},{17,25},{9,1},{25,17},{2,10},{18... | collective-permute-start | bytes 258056 | tf_op jit(solution)/shard_map/ppermute | solution.py:511
  17.6 10.0 %collective-permute-start.6 = (f32[7,24,128]{2,1,0:T(8,128)S(1)}, f32[7,24,128]{2,1,0:T(8,128)S(1)}, u32[]{:S(2)}, u32[]{:S(2)}) collective-permute-start(f32[7,24,128]{2,1,0:T(8,128)S(1)} %get-tuple-element.159), channel_id=1, source_target_pairs={{8,16},{16,8},{9,17},{17,9},{10,18},{18,10},{11,19},{19,11},{12,20... | collective-permute-start | bytes 258056 | tf_op jit(solution)/shard_map/ppermute | solution.py:511
  27.6 2.9 %collective-permute-start.7 = (f32[2,49,8,256]{3,2,1,0:T(8,128)S(1)}, f32[2,49,8,256]{3,2,1,0:T(8,128)S(1)}, u32[]{:S(2)}, u32[]{:S(2)}) collective-permute-start(f32[2,49,8,256]{3,2,1,0:T(8,128)S(1)} %shard_map.83), channel_id=1, source_target_pairs={{0,1},{1,0},{2,3},{3,2},{4,5},{5,4},{6,7},{7,6},{8,9},{9,8},{10,11... | collective-permute-start | bytes 2408456 | tf_op jit(solution)/shard_map/ppermute | solution.py:511

commit v6 on v5

--- a/solution.py
+++ b/solution.py
@@ -226,10 +226,10 @@
             self.HC[x, j] = jnp.where(inside, (1.0 - half) * over, 0.0)
             self.HB[x, j] = jnp.where(inside, (DT / 6.0) * over, 0.0)
 
-    def electric_coefficients(self, x, columns, at=None):
+    def electric_coefficients(self, x, columns):
         for j in columns:
             half, inside = self.place(x, j)
-            for row in at or range(GUARD, GUARD + self.zsteps * ROWS, ROWS):
+            for row in range(GUARD, GUARD + self.zsteps * ROWS, ROWS):
                 rows = pl.ds(row, ROWS)
                 eps = self.EC[x, j, rows, :]
                 over = 1.0 / jnp.where(inside, eps + half, 1.0)
@@ -406,10 +406,34 @@
         groups(STEPS + step, last, functools.partial(block.electric, step=step), GROUP)
 
 
+NEAR = ROWS - STEPS + 1
+
+
+def depth(array):
+    return STEPS if array < HX + 2 else STEPS - 1
+
+
+def near_places():
+    row, places = NEAR, []
+    for face in range(2):
+        at = 0
+        for array, count in faces():
+            for i in range(count):
+                places.append((face, at + i, row, depth(array)))
+                row += depth(array)
+            at += count
+    return places, -(-(row + NEAR) // ROWS) * ROWS
+
+
 def pack_near(first_ref, second_ref, near_ref):
-    begin = pl.multiple_of((1 - lax.axis_index("gz")) * (first_ref.shape[1] - ROWS), ROWS)
-    near_ref[0] = first_ref[:, pl.ds(begin, ROWS), :]
-    near_ref[1] = second_ref[:, pl.ds(begin, ROWS), :]
+    low_core = lax.axis_index("gz") == 0
+    zcount, ycount = first_ref.shape[1:]
+    places, rows = near_places()
+    near_ref[0:ROWS, :] = jnp.zeros((ROWS, ycount), jnp.float32)
+    near_ref[rows - ROWS :, :] = jnp.zeros((ROWS, ycount), jnp.float32)
+    for face, at, row, count in places:
+        ref = (first_ref, second_ref)[face]
+        near_ref[row : row + count, :] = jnp.where(low_core, ref[at, zcount - count :, :], ref[at, 0:count, :])
 
 
 def arrivals(block, first, second):
@@ -426,21 +450,7 @@
     return (*range(1, STEPS), *range(STEPS + block.xcount, block.extent - 1))
 
 
-def place_arrivals(shape, first_ref, second_ref, corner_first_ref, corner_second_ref, *states):
-    block = Block(shape, states[len(states) // 2 :])
-    per = LANES // SLOT
-    came = arrivals(block, (first_ref, corner_first_ref), (second_ref, corner_second_ref))
-    for array, plane, at, slot, face, corner in came:
-        for j in range(block.tiles):
-            for z in range(0, block.zcount, ROWS):
-                block.put(array, plane, block.own + z, j, face[at, z : z + ROWS, j * LANES : (j + 1) * LANES])
-        block.put_ends(array, plane, corner, lax.rem(slot, per), lax.div(slot, per))
-    for plane in halo_planes(block):
-        block.electric_coefficients(plane, range(block.tiles), [block.own + z for z in range(0, block.zcount, ROWS)])
-        block.electric_coefficients(plane, (block.tiles,))
-
-
-def outer(shape, near_ref, *rest):
+def outer(shape, first_ref, second_ref, corner_first_ref, corner_second_ref, near_ref, *rest):
     e_stage, h_stage, sent = rest[-3:]
     count = (len(rest) - 5) // 2
     e_out, h_out = rest[count : count + 2]
@@ -468,12 +478,22 @@
     send(e_stage, e_out, *middle)
     stage(block.H, h_stage, 6.0, *middle)
     send(h_stage, h_out, *middle)
-    for array, plane, at, _, side in arrivals(block, (near_ref.at[0],), (near_ref.at[1],)):
+    core = lax.axis_index("gz")
+    per = LANES // SLOT
+    rows_at = {(face, at): (row, count) for face, at, row, count in near_places()[0]}
+    faces_in = ((first_ref, corner_first_ref, 0), (second_ref, corner_second_ref, 1))
+    for array, plane, at, slot, face, corner, side in arrivals(block, *faces_in):
+        row, count = rows_at[side, at]
         for j in range(block.tiles):
-            value = side[at, :, j * LANES : (j + 1) * LANES]
-            block.put(array, plane, block.halo, j, value)
+            lanes = slice(j * LANES, (j + 1) * LANES)
+            for z in range(0, zcount, ROWS):
+                block.put(array, plane, block.own + z, j, face[at, z : z + ROWS, lanes])
+            begin = near_ref[1 - core, row : row + ROWS, lanes]
+            end = near_ref[1 - core, row + count - ROWS : row + count, lanes]
+            block.put(array, plane, block.halo, j, jnp.where(core == 0, begin, end))
+        block.put_ends(array, plane, corner, lax.rem(slot, per), lax.div(slot, per))
     for plane in halo_planes(block):
-        block.electric_coefficients(plane, range(block.tiles), (block.halo,))
+        block.electric_coefficients(plane, range(block.tiles + 1))
     for step in range(1, STEPS + 1):
         above = xcount + STEPS - step
         block.magnetic(*range(step - 1, step - 1 + STEPS), *range(above, above + STEPS))
@@ -553,16 +573,13 @@
     same = {i: i for i in range(count)}
     state = call(functools.partial(inner, shape), states, state, 0.1, same)
     first, second, state = lax.optimization_barrier((first, second, state))
-    came = (first, second, corner_first, corner_second)
-    near = call(pack_near, [kept(2, planes_of(faces()), ROWS, ycount)], (first, second), 0.2)[0]
-    near, came, state = lax.optimization_barrier((near, came, state))
-    near = swap(near, "gz")
-    aliases = {len(came) + i: i for i in range(count)}
-    state = call(functools.partial(place_arrivals, shape), states, (*came, *state), 0.1, aliases)
+    near = call(pack_near, [kept(near_places()[1], ycount)], (first, second), 0.2)[0]
+    near = lax.all_gather(near, "gz")
+    came = (first, second, corner_first, corner_second, near)
     outs = [jax.ShapeDtypeStruct(e_field.shape, jnp.float32), jax.ShapeDtypeStruct(h_field.shape, jnp.float32)]
     scratch = [pltpu.VMEM(e_field.shape, jnp.float32)] * 2 + [pltpu.SemaphoreType.DMA((6,))]
-    aliases = {1 + i: 2 + i for i in range(count)}
-    ends = (near, *state)
+    aliases = {len(came) + i: 2 + i for i in range(count)}
+    ends = (*came, *state)
     return tuple(call(functools.partial(outer, shape), outs + states, ends, 1, aliases, scratch, hbm=2)[:2])
 
 

time: 36.4 us -> 39 us (1.071)
  blocking collectives: 0 us -> 3.54 us
  starting transfers between devices: 12.7 us -> 11.6 us
    all_gather x0 -> x1, blocking collectives: none -> 3.54 us  [body(): near = lax.all_gather(near, 'gz')]
    ppermute x8 -> x7, starting transfers between devices: 12.7 us -> 11.6 us  [swap(): return lax.ppermute(value, axis, pairs + [(b, a) for a, b in pairs])]
    pallas_call x9 -> x8, Pallas kernels: 16.5 us -> 16.7 us  [call(): pl.pallas_call(kernel, out_shape=outs, in_specs=[pl.BlockSpec(memory_spac...]
    ppermute x8 -> x7, waiting for transfers between devices: 6.15 us -> 6.08 us  [swap(): return lax.ppermute(value, axis, pairs + [(b, a) for a, b in pairs])]
  transfers between devices with their start and end apart: 8 -> 7, of which waited for: 3 -> 2; matrix products, arithmetic and copies ran while one was open for 0% -> 0% of each run, Pallas kernels for 25% -> 22%
where the time goes in v6:
time: 39 us; the launch traced here: 38.7 us
  Pallas kernels  16.7 us (43%)
  starting transfers between devices  11.6 us (30%)
  waiting for transfers between devices  6.08 us (16%)
  blocking collectives  3.54 us (9%)
  between operations  0.73 us (2%)
    pallas_call x8, Pallas kernels, call(): pl.pallas_call(kernel, out_shape=outs, in_specs=[pl.BlockSpec(memory_spac...  16.7 us
    ppermute x7, starting transfers between devices, swap(): return lax.ppermute(value, axis, pairs + [(b, a) for a, b in pairs])  11.6 us
    ppermute x7, waiting for transfers between devices, swap(): return lax.ppermute(value, axis, pairs + [(b, a) for a, b in pairs])  6.08 us
    all_gather x1, blocking collectives, body(): near = lax.all_gather(near, 'gz')  3.54 us
  transfers between devices with their start and end apart: 7, of which 2 were waited for; matrix products, arithmetic and copies ran while one was open for 0% of the time, Pallas kernels for 22%

profile of v6, /device:TPU:13, one launch (start us, length us, event | category | flops | bytes accessed | tf_op | source)
XLA Modules:
  0.0 38.7 jit_solution(7077095167830720348)
XLA Ops:
  0.6 1.9 %shard_map.77 = (f32[49,16,256]{2,1,0:T(8,128)S(1)}, f32[49,16,256]{2,1,0:T(8,128)S(1)}, f32[11,16,8,256]{3,2,1,0:T(8,128)S(1)}, f32[3,16,16,256]{3,2,1,0:T(8,12...) custom-call(f32[3,16,16,256]{3,2,1,0:T(8,128)} %e_hbm.1, ...), custom_call_target="tpu_custom_call" | custom-call | flops 3000000 | bytes 3000000 | tf_op jit(solution)/shard_map/pallas_call | solution.py:517
  2.5 0.7 %collective-permute-start.2 = (f32[11,16,8,256]{3,2,1,0:T(8,128)S(1)}, f32[11,16,8,256]{3,2,1,0:T(8,128)S(1)}, u32[]{:S(2)}, u32[]{:S(2)}) collective-permute-start(f32[11,16,8,256]{3,2,1,0:T(8,128)S(1)} %get-tuple-element.82), channel_id=1, source_target_pairs={{0,1},{1,0},{2,3},{3,2},{4,5},{5,4},{6,7},{7,6},{8,9},{9,8},{10,11... | collective-permute-start | bytes 4325384 | tf_op jit(solution)/shard_map/ppermute | solution.py:531
  3.3 0.2 collective-permute-start
  3.5 4.3 %collective-permute-start.1 = (f32[49,16,256]{2,1,0:T(8,128)S(1)}, f32[49,16,256]{2,1,0:T(8,128)S(1)}, u32[]{:S(2)}, u32[]{:S(2)}) collective-permute-start(f32[49,16,256]{2,1,0:T(8,128)S(1)} %get-tuple-element.76), channel_id=1, source_target_pairs={{8,16},{16,8},{9,17},{17,9},{10,18},{18,10},{11,19},{19,11},{12,20... | collective-permute-start | bytes 2408456 | tf_op jit(solution)/shard_map/ppermute | solution.py:531
  7.8 0.0 collective-permute-done.2.side_ref
  7.8 1.3 %shard_map.78 = (f32[11,24,128]{2,1,0:T(8,128)S(1)}, f32[11,24,128]{2,1,0:T(8,128)S(1)}) custom-call(f32[3,16,16,256]{3,2,1,0:T(8,128)S(1)} %get-tuple-element.87.e_ref, f32[3,16,16,256]{3,2,1,0:T(8,128)S(1)} %get-tuple-element.88.h_ref, f32[3,16,16,256]{3,2,1,0:T(8,128)S(1)} %get-tuple-element.89.p_ref, f32[16,16,256]{2,1,0:T(8,128)S(1)} %get-tuple-element.90.eps_ref, ...), custom_call_target="tpu_custom_call" | custom-call | flops 3000000 | bytes 3000000 | tf_op jit(solution)/shard_map/pallas_call | solution.py:517
  9.1 1.3 %collective-permute-start.3 = (f32[11,24,128]{2,1,0:T(8,128)S(1)}, f32[11,24,128]{2,1,0:T(8,128)S(1)}, u32[]{:S(2)}, u32[]{:S(2)}) collective-permute-start(f32[11,24,128]{2,1,0:T(8,128)S(1)} %get-tuple-element.85), channel_id=1, source_target_pairs={{0,2},{4,6},{2,0},{6,4},{1,3},{5,7},{3,1},{7,5},{8,10},{12,14},{10... | collective-permute-start | bytes 405512 | tf_op jit(solution)/shard_map/ppermute | solution.py:531
  10.4 2.1 %collective-permute-start.4 = (f32[11,24,128]{2,1,0:T(8,128)S(1)}, f32[11,24,128]{2,1,0:T(8,128)S(1)}, u32[]{:S(2)}, u32[]{:S(2)}) collective-permute-start(f32[11,24,128]{2,1,0:T(8,128)S(1)} %get-tuple-element.86), channel_id=1, source_target_pairs={{2,4},{4,2},{3,5},{5,3},{10,12},{12,10},{11,13},{13,11},{18,20},{2... | collective-permute-start | bytes 405512 | tf_op jit(solution)/shard_map/ppermute | solution.py:531
  12.5 1.4 %shard_map.79 = (f32[3,26,3,40,128]{4,3,2,1,0:T(8,128)S(1)}, f32[3,26,3,40,128]{4,3,2,1,0:T(8,128)S(1)}, f32[3,26,3,40,128]{4,3,2,1,0:T(8,128)S(1)}, f32[3,26,3,...) custom-call(f32[3,16,16,256]{3,2,1,0:T(8,128)S(1)} %get-tuple-elemen, ...), custom_call_target="tpu_custom_call" | custom-call | flops 6000000 | bytes 6000000 | tf_op jit(solution)/shard_map/pallas_call | solution.py:517
  13.8 0.0 collective-permute-done.3.first_ref
  13.8 3.5 %collective-permute-done.4.second_ref = f32[11,24,128]{2,1,0:T(8,128)S(1)} collective-permute-done((f32[11,24,128]{2,1,0:T(8,128)S(1)}, f32[11,24,128]{2,1,0:T(8,128)S(1)}, u32[]{:S(2)}, u32[]{:S(2)}) %collective-permute-start.4) | collective-permute-done | bytes 135200 | tf_op jit(solution)/shard_map/ppermute | solution.py:531
  17.3 0.3 shard_map.80
  17.6 0.9 %shard_map.81 = (f32[3,26,3,40,128]{4,3,2,1,0:T(8,128)S(1)}, f32[3,26,3,40,128]{4,3,2,1,0:T(8,128)S(1)}, f32[3,26,3,40,128]{4,3,2,1,0:T(8,128)S(1)}, f32[3,26,3,...) custom-call(f32[11,24,128]{2,1,0:T(8,128)S(1)} %get-tuple-element.10, ...), custom_call_target="tpu_custom_call", output_to_operand_aliasing={{0}: (2, {}), {1}: (3, {}), {2}: (4, {}), {3}: (5, {}), {4}... | custom-call | flops 300000 | bytes 300000 | tf_op jit(solution)/shard_map/pallas_call | solution.py:517
  18.5 4.7 %shard_map.82 = (f32[3,26,3,40,128]{4,3,2,1,0:T(8,128)S(1)}, f32[3,26,3,40,128]{4,3,2,1,0:T(8,128)S(1)}, f32[3,26,3,40,128]{4,3,2,1,0:T(8,128)S(1)}, f32[3,26,3,...) custom-call(f32[3,26,3,40,128]{4,3,2,1,0:T(8,128)S(1)} %get-tuple-el, ...), custom_call_target="tpu_custom_call", output_to_operand_aliasing={{0}: (0, {}), {1}: (1, {}), {2}: (2, {}), {3}: (3, {}), {4}... | custom-call | flops 300000 | bytes 300000 | tf_op jit(solution)/shard_map/pallas_call | solution.py:517
  23.2 0.0 collective-permute-done.first_ref
  23.2 2.6 %collective-permute-done.1.second_ref = f32[49,16,256]{2,1,0:T(8,128)S(1)} collective-permute-done((f32[49,16,256]{2,1,0:T(8,128)S(1)}, f32[49,16,256]{2,1,0:T(8,128)S(1)}, u32[]{:S(2)}, u32[]{:S(2)}) %collective-permute-start.1) | collective-permute-done | bytes 802848 | tf_op jit(solution)/shard_map/ppermute | solution.py:531
  25.8 0.0 collective-permute-start.5
  25.8 3.0 %collective-permute-start.6 = (f32[7,24,128]{2,1,0:T(8,128)S(1)}, f32[7,24,128]{2,1,0:T(8,128)S(1)}, u32[]{:S(2)}, u32[]{:S(2)}) collective-permute-start(f32[7,24,128]{2,1,0:T(8,128)S(1)} %get-tuple-element.136), channel_id=1, source_target_pairs={{8,16},{16,8},{9,17},{17,9},{10,18},{18,10},{11,19},{19,11},{12,20... | collective-permute-start | bytes 258056 | tf_op jit(solution)/shard_map/ppermute | solution.py:531
  28.8 0.1 shard_map.83
  29.0 3.5 %all-gather = f32[896,256]{1,0:T(8,128)S(1)} all-gather(f32[448,256]{1,0:T(8,128)S(1)} %shard_map.83), channel_id=2, replica_groups=mesh['gx'=4,'gy'=4,'gz'=2] {'gz'}, dimensions={0}, use_global_device_ids=true | all-gather | bytes 1376256 | tf_op jit(solution)/shard_map/all_gather | solution.py:577
  32.5 0.0 collective-permute-done.5.corner_first_ref
  32.5 0.0 collective-permute-done.6.corner_second_ref
  32.5 6.2 %shard_map.84 = (f32[3,16,16,256]{3,2,1,0:T(8,128)}, f32[3,16,16,256]{3,2,1,0:T(8,128)}, f32[3,26,3,40,128]{4,3,2,1,0:T(8,128)S(1)}, f32[3,26,3,40,128]{4,3,2,1,...) custom-call(f32[49,16,256]{2,1,0:T(8,128)S(1)} %collective-permute-d, ...), custom_call_target="tpu_custom_call", output_to_operand_aliasing={{2}: (5, {}), {3}: (6, {}), {4}: (7, {}), {5}: (8, {}), {6}... | custom-call | flops 3000000 | bytes 3000000 | tf_op jit(solution)/shard_map/pallas_call | solution.py:517
Async XLA Ops:
  2.5 5.3 %collective-permute-start.2 = (f32[11,16,8,256]{3,2,1,0:T(8,128)S(1)}, f32[11,16,8,256]{3,2,1,0:T(8,128)S(1)}, u32[]{:S(2)}, u32[]{:S(2)}) collective-permute-start(f32[11,16,8,256]{3,2,1,0:T(8,128)S(1)} %get-tuple-element.82), channel_id=1, source_target_pairs={{0,1},{1,0},{2,3},{3,2},{4,5},{5,4},{6,7},{7,6},{8,9},{9,8},{10,11... | collective-permute-start | bytes 4325384 | tf_op jit(solution)/shard_map/ppermute | solution.py:531
  3.3 19.9 %collective-permute-start = (f32[49,16,256]{2,1,0:T(8,128)S(1)}, f32[49,16,256]{2,1,0:T(8,128)S(1)}, u32[]{:S(2)}, u32[]{:S(2)}) collective-permute-start(f32[49,16,256]{2,1,0:T(8,128)S(1)} %get-tuple-element.75), channel_id=1, source_target_pairs={{0,8},{16,24},{8,0},{24,16},{1,9},{17,25},{9,1},{25,17},{2,10},{18... | collective-permute-start | bytes 2408456 | tf_op jit(solution)/shard_map/ppermute | solution.py:531
  3.5 22.3 %collective-permute-start.1 = (f32[49,16,256]{2,1,0:T(8,128)S(1)}, f32[49,16,256]{2,1,0:T(8,128)S(1)}, u32[]{:S(2)}, u32[]{:S(2)}) collective-permute-start(f32[49,16,256]{2,1,0:T(8,128)S(1)} %get-tuple-element.76), channel_id=1, source_target_pairs={{8,16},{16,8},{9,17},{17,9},{10,18},{18,10},{11,19},{19,11},{12,20... | collective-permute-start | bytes 2408456 | tf_op jit(solution)/shard_map/ppermute | solution.py:531
  9.1 4.7 %collective-permute-start.3 = (f32[11,24,128]{2,1,0:T(8,128)S(1)}, f32[11,24,128]{2,1,0:T(8,128)S(1)}, u32[]{:S(2)}, u32[]{:S(2)}) collective-permute-start(f32[11,24,128]{2,1,0:T(8,128)S(1)} %get-tuple-element.85), channel_id=1, source_target_pairs={{0,2},{4,6},{2,0},{6,4},{1,3},{5,7},{3,1},{7,5},{8,10},{12,14},{10... | collective-permute-start | bytes 405512 | tf_op jit(solution)/shard_map/ppermute | solution.py:531
  10.4 7.0 %collective-permute-start.4 = (f32[11,24,128]{2,1,0:T(8,128)S(1)}, f32[11,24,128]{2,1,0:T(8,128)S(1)}, u32[]{:S(2)}, u32[]{:S(2)}) collective-permute-start(f32[11,24,128]{2,1,0:T(8,128)S(1)} %get-tuple-element.86), channel_id=1, source_target_pairs={{2,4},{4,2},{3,5},{5,3},{10,12},{12,10},{11,13},{13,11},{18,20},{2... | collective-permute-start | bytes 405512 | tf_op jit(solution)/shard_map/ppermute | solution.py:531
  25.8 6.7 %collective-permute-start.5 = (f32[7,24,128]{2,1,0:T(8,128)S(1)}, f32[7,24,128]{2,1,0:T(8,128)S(1)}, u32[]{:S(2)}, u32[]{:S(2)}) collective-permute-start(f32[7,24,128]{2,1,0:T(8,128)S(1)} %get-tuple-element.135), channel_id=1, source_target_pairs={{0,8},{16,24},{8,0},{24,16},{1,9},{17,25},{9,1},{25,17},{2,10},{18... | collective-permute-start | bytes 258056 | tf_op jit(solution)/shard_map/ppermute | solution.py:531
  25.8 6.7 %collective-permute-start.6 = (f32[7,24,128]{2,1,0:T(8,128)S(1)}, f32[7,24,128]{2,1,0:T(8,128)S(1)}, u32[]{:S(2)}, u32[]{:S(2)}) collective-permute-start(f32[7,24,128]{2,1,0:T(8,128)S(1)} %get-tuple-element.136), channel_id=1, source_target_pairs={{8,16},{16,8},{9,17},{17,9},{10,18},{18,10},{11,19},{19,11},{12,20... | collective-permute-start | bytes 258056 | tf_op jit(solution)/shard_map/ppermute | solution.py:531

commit v7 on v5

--- a/solution.py
+++ b/solution.py
@@ -21,6 +21,7 @@
 ROWS = 8
 SIDE = 8
 SLOT = 2 * SIDE
+CORNER = 2 * STEPS
 GUARD = 8
 VMEM_LIMIT = 8 * 1024 * 1024
 
@@ -142,12 +143,12 @@
 
 
 def merge_strips(first_ref, second_ref, low_ref, high_ref, corner_first_ref, corner_second_ref):
-    _, slot, left = slots()
+    lane, _, left = slots()
     up, over = even("gy"), even("gx")
     per = LANES // SLOT
     for t in range(first_ref.shape[1] // ROWS):
         rows = slice(t * ROWS, (t + 1) * ROWS)
-        packed = ([None] * (corner_rows() + 1), [None] * (corner_rows() + 1))
+        packed = ([None] * corner_rows(), [None] * corner_rows())
         for array in range(ARRAYS):
             first, second = first_ref[array, rows, :], second_ref[array, rows, :]
             ahead, behind = jnp.where(up, first, second), jnp.where(up, second, first)
@@ -155,18 +156,20 @@
             high = jnp.where(left, turn(behind, -SIDE), turn(ahead, SIDE))
             low_ref[array, rows, :] = low
             high_ref[array, rows, :] = high
-            at, place = divmod(STEPS * array, per)
-            begin, end = turn(low, SLOT * place), turn(high, SLOT * (place - per + STEPS))
-            for into, value in zip(packed, (jnp.where(over, end, begin), jnp.where(over, begin, end))):
-                into[at] = value if into[at] is None else jnp.where(slot >= place, value, into[at])
-                into[at + 1] = value if place + STEPS > per else None
+            for i in range(STEPS):
+                at, place = divmod(STEPS * array + i, LANES // CORNER)
+                here = (lane >= CORNER * place) & (lane < CORNER * (place + 1))
+                shift = CORNER * place - (SIDE - STEPS)
+                begin, end = turn(low, shift - SLOT * i), turn(high, shift - SLOT * (i + per - STEPS))
+                for into, value in zip(packed, (jnp.where(over, end, begin), jnp.where(over, begin, end))):
+                    into[at] = value if into[at] is None else jnp.where(here, value, into[at])
         for into, out_ref in zip(packed, (corner_first_ref, corner_second_ref)):
             for n in range(corner_rows()):
                 out_ref[n, rows, :] = into[n]
 
 
 def corner_rows():
-    return -(-STEPS * ARRAYS // (LANES // SLOT))
+    return -(-STEPS * ARRAYS // (LANES // CORNER))
 
 
 def profile(index, total):
@@ -199,9 +202,9 @@
         else:
             self.BM[plane, j, rows, :] = value
 
-    def put_ends(self, array, plane, packed, slot, row=None):
+    def put_ends(self, array, plane, packed, shift, row=None):
         for t in range(self.zsteps):
-            ends = pltpu.roll(packed[array if row is None else row, t * ROWS : (t + 1) * ROWS, :], LANES - SIDE - SLOT * slot, 1)
+            ends = pltpu.roll(packed[array if row is None else row, t * ROWS : (t + 1) * ROWS, :], shift, 1)
             self.put(array, plane, GUARD + t * ROWS, self.tiles, ends)
 
     def place(self, x, j):
@@ -377,7 +380,7 @@
     per = LANES // SLOT
     for array in range(ARRAYS):
         for x in range(block.xcount):
-            block.put_ends(array, x + STEPS, low_ref if x < per else high_ref, x % per)
+            block.put_ends(array, x + STEPS, low_ref if x < per else high_ref, LANES - SIDE - SLOT * (x % per))
     coefficients = functools.partial(block.electric_coefficients, columns=(block.tiles,))
     loop(STEPS, STEPS + block.xcount, coefficients, 2)
 
@@ -398,18 +401,42 @@
         act(*range(begin + whole * size, end))
 
 
-def inner(shape, *states):
+def inner(shape, begin, end, *states):
     block = Block(shape, states[len(states) // 2 :])
-    for step in range(1, STEPS + 1):
+    for step in range(begin, end):
         last = STEPS + block.xcount - step
         groups(STEPS + step - 1, last, block.magnetic, GROUP)
         groups(STEPS + step, last, functools.partial(block.electric, step=step), GROUP)
 
 
+NEAR = ROWS - STEPS + 1
+
+
+def depth(array):
+    return STEPS if array < HX + 2 else STEPS - 1
+
+
+def near_places():
+    row, places = NEAR, []
+    for face in range(2):
+        at = 0
+        for array, count in faces():
+            for i in range(count):
+                places.append((face, at + i, row, depth(array)))
+                row += depth(array)
+            at += count
+    return places, -(-(row + NEAR) // ROWS) * ROWS
+
+
 def pack_near(first_ref, second_ref, near_ref):
-    begin = pl.multiple_of((1 - lax.axis_index("gz")) * (first_ref.shape[1] - ROWS), ROWS)
-    near_ref[0] = first_ref[:, pl.ds(begin, ROWS), :]
-    near_ref[1] = second_ref[:, pl.ds(begin, ROWS), :]
+    low_core = lax.axis_index("gz") == 0
+    zcount, ycount = first_ref.shape[1:]
+    places, rows = near_places()
+    near_ref[0:ROWS, :] = jnp.zeros((ROWS, ycount), jnp.float32)
+    near_ref[rows - ROWS :, :] = jnp.zeros((ROWS, ycount), jnp.float32)
+    for face, at, row, count in places:
+        ref = (first_ref, second_ref)[face]
+        near_ref[row : row + count, :] = jnp.where(low_core, ref[at, zcount - count :, :], ref[at, 0:count, :])
 
 
 def arrivals(block, first, second):
@@ -428,13 +455,13 @@
 
 def place_arrivals(shape, first_ref, second_ref, corner_first_ref, corner_second_ref, *states):
     block = Block(shape, states[len(states) // 2 :])
-    per = LANES // SLOT
+    per = LANES // CORNER
     came = arrivals(block, (first_ref, corner_first_ref), (second_ref, corner_second_ref))
     for array, plane, at, slot, face, corner in came:
         for j in range(block.tiles):
             for z in range(0, block.zcount, ROWS):
                 block.put(array, plane, block.own + z, j, face[at, z : z + ROWS, j * LANES : (j + 1) * LANES])
-        block.put_ends(array, plane, corner, lax.rem(slot, per), lax.div(slot, per))
+        block.put_ends(array, plane, corner, LANES - STEPS - CORNER * lax.rem(slot, per), lax.div(slot, per))
     for plane in halo_planes(block):
         block.electric_coefficients(plane, range(block.tiles), [block.own + z for z in range(0, block.zcount, ROWS)])
         block.electric_coefficients(plane, (block.tiles,))
@@ -468,10 +495,14 @@
     send(e_stage, e_out, *middle)
     stage(block.H, h_stage, 6.0, *middle)
     send(h_stage, h_out, *middle)
-    for array, plane, at, _, side in arrivals(block, (near_ref.at[0],), (near_ref.at[1],)):
+    low_core = lax.axis_index("gz") == 0
+    rows_at = {(face, at): (row, count) for face, at, row, count in near_places()[0]}
+    for array, plane, at, _, face in arrivals(block, (0,), (1,)):
+        row, count = rows_at[face, at]
         for j in range(block.tiles):
-            value = side[at, :, j * LANES : (j + 1) * LANES]
-            block.put(array, plane, block.halo, j, value)
+            lanes = slice(j * LANES, (j + 1) * LANES)
+            begin, end = near_ref[row : row + ROWS, lanes], near_ref[row + count - ROWS : row + count, lanes]
+            block.put(array, plane, block.halo, j, jnp.where(low_core, begin, end))
     for plane in halo_planes(block):
         block.electric_coefficients(plane, range(block.tiles), (block.halo,))
     for step in range(1, STEPS + 1):
@@ -551,14 +582,15 @@
     ends = functools.partial(prepare_ends, shape)
     state = call(ends, states, (low, high, *state), 0.1, {2 + i: i for i in range(count)})
     same = {i: i for i in range(count)}
-    state = call(functools.partial(inner, shape), states, state, 0.1, same)
+    state = call(functools.partial(inner, shape, 1, STEPS), states, state, 0.1, same)
     first, second, state = lax.optimization_barrier((first, second, state))
     came = (first, second, corner_first, corner_second)
-    near = call(pack_near, [kept(2, planes_of(faces()), ROWS, ycount)], (first, second), 0.2)[0]
+    near = call(pack_near, [kept(near_places()[1], ycount)], (first, second), 0.2)[0]
     near, came, state = lax.optimization_barrier((near, came, state))
     near = swap(near, "gz")
     aliases = {len(came) + i: i for i in range(count)}
     state = call(functools.partial(place_arrivals, shape), states, (*came, *state), 0.1, aliases)
+    state = call(functools.partial(inner, shape, STEPS, STEPS + 1), states, state, 0.1, same)
     outs = [jax.ShapeDtypeStruct(e_field.shape, jnp.float32), jax.ShapeDtypeStruct(h_field.shape, jnp.float32)]
     scratch = [pltpu.VMEM(e_field.shape, jnp.float32)] * 2 + [pltpu.SemaphoreType.DMA((6,))]
     aliases = {1 + i: 2 + i for i in range(count)}

time: 36.4 us -> 37.3 us (1.025)
  waiting for transfers between devices: 6.15 us -> 3.92 us
  Pallas kernels: 16.5 us -> 18.4 us
  starting transfers between devices: 12.7 us -> 13.9 us
    ppermute x8, waiting for transfers between devices: 6.15 us -> 3.92 us  [swap(): return lax.ppermute(value, axis, pairs + [(b, a) for a, b in pairs])]
    pallas_call x9 -> x10, Pallas kernels: 16.5 us -> 18.4 us  [call(): pl.pallas_call(kernel, out_shape=outs, in_specs=[pl.BlockSpec(memory_spac...]
    ppermute x8, starting transfers between devices: 12.7 us -> 13.9 us  [swap(): return lax.ppermute(value, axis, pairs + [(b, a) for a, b in pairs])]
  transfers between devices with their start and end apart: 8 -> 8, of which waited for: 3 -> 2; matrix products, arithmetic and copies ran while one was open for 0% -> 0% of each run, Pallas kernels for 25% -> 29%
where the time goes in v7:
time: 37.3 us; the launch traced here: 37.1 us
  Pallas kernels  18.4 us (49%)
  starting transfers between devices  13.9 us (37%)
  waiting for transfers between devices  3.92 us (11%)
  between operations  0.78 us (2%)
    pallas_call x10, Pallas kernels, call(): pl.pallas_call(kernel, out_shape=outs, in_specs=[pl.BlockSpec(memory_spac...  18.4 us
    ppermute x8, starting transfers between devices, swap(): return lax.ppermute(value, axis, pairs + [(b, a) for a, b in pairs])  13.9 us
    ppermute x8, waiting for transfers between devices, swap(): return lax.ppermute(value, axis, pairs + [(b, a) for a, b in pairs])  3.92 us
  transfers between devices with their start and end apart: 8, of which 2 were waited for; matrix products, arithmetic and copies ran while one was open for 0% of the time, Pallas kernels for 29%

profile of v7, /device:TPU:13, one launch (start us, length us, event | category | flops | bytes accessed | tf_op | source)
XLA Modules:
  0.0 37.1 jit_solution(16802150834907467896)
XLA Ops:
  0.6 1.9 %shard_map.77 = (f32[49,16,256]{2,1,0:T(8,128)S(1)}, f32[49,16,256]{2,1,0:T(8,128)S(1)}, f32[11,16,8,256]{3,2,1,0:T(8,128)S(1)}, f32[3,16,16,256]{3,2,1,0:T(8,12...) custom-call(f32[3,16,16,256]{3,2,1,0:T(8,128)} %e_hbm.1, ...), custom_call_target="tpu_custom_call" | custom-call | flops 3000000 | bytes 3000000 | tf_op jit(solution)/shard_map/pallas_call | solution.py:528
  2.5 0.7 %collective-permute-start.2 = (f32[11,16,8,256]{3,2,1,0:T(8,128)S(1)}, f32[11,16,8,256]{3,2,1,0:T(8,128)S(1)}, u32[]{:S(2)}, u32[]{:S(2)}) collective-permute-start(f32[11,16,8,256]{3,2,1,0:T(8,128)S(1)} %get-tuple-element.114), channel_id=1, source_target_pairs={{0,1},{1,0},{2,3},{3,2},{4,5},{5,4},{6,7},{7,6},{8,9},{9,8},{10,11... | collective-permute-start | bytes 4325384 | tf_op jit(solution)/shard_map/ppermute | solution.py:542
  3.3 0.2 collective-permute-start
  3.5 4.3 %collective-permute-start.1 = (f32[49,16,256]{2,1,0:T(8,128)S(1)}, f32[49,16,256]{2,1,0:T(8,128)S(1)}, u32[]{:S(2)}, u32[]{:S(2)}) collective-permute-start(f32[49,16,256]{2,1,0:T(8,128)S(1)} %get-tuple-element.108), channel_id=1, source_target_pairs={{8,16},{16,8},{9,17},{17,9},{10,18},{18,10},{11,19},{19,11},{12,20... | collective-permute-start | bytes 2408456 | tf_op jit(solution)/shard_map/ppermute | solution.py:542
  7.8 0.0 collective-permute-done.2.side_ref
  7.8 1.3 %shard_map.78 = (f32[11,24,128]{2,1,0:T(8,128)S(1)}, f32[11,24,128]{2,1,0:T(8,128)S(1)}) custom-call(f32[3,16,16,256]{3,2,1,0:T(8,128)S(1)} %get-tuple-element.119.e_ref, f32[3,16,16,256]{3,2,1,0:T(8,128)S(1)} %get-tuple-element.120.h_ref, f32[3,16,16,256]{3,2,1,0:T(8,128)S(1)} %get-tuple-element.121.p_ref, f32[16,16,256]{2,1,0:T(8,128)S(1)} %get-tuple-element.122.eps_ref, ...), custom_call_target="tpu_custom_call" | custom-call | flops 3000000 | bytes 3000000 | tf_op jit(solution)/shard_map/pallas_call | solution.py:528
  9.1 1.3 %collective-permute-start.3 = (f32[11,24,128]{2,1,0:T(8,128)S(1)}, f32[11,24,128]{2,1,0:T(8,128)S(1)}, u32[]{:S(2)}, u32[]{:S(2)}) collective-permute-start(f32[11,24,128]{2,1,0:T(8,128)S(1)} %get-tuple-element.117), channel_id=1, source_target_pairs={{0,2},{4,6},{2,0},{6,4},{1,3},{5,7},{3,1},{7,5},{8,10},{12,14},{10... | collective-permute-start | bytes 405512 | tf_op jit(solution)/shard_map/ppermute | solution.py:542
  10.4 2.1 %collective-permute-start.4 = (f32[11,24,128]{2,1,0:T(8,128)S(1)}, f32[11,24,128]{2,1,0:T(8,128)S(1)}, u32[]{:S(2)}, u32[]{:S(2)}) collective-permute-start(f32[11,24,128]{2,1,0:T(8,128)S(1)} %get-tuple-element.118), channel_id=1, source_target_pairs={{2,4},{4,2},{3,5},{5,3},{10,12},{12,10},{11,13},{13,11},{18,20},{2... | collective-permute-start | bytes 405512 | tf_op jit(solution)/shard_map/ppermute | solution.py:542
  12.5 1.4 %shard_map.79 = (f32[3,26,3,40,128]{4,3,2,1,0:T(8,128)S(1)}, f32[3,26,3,40,128]{4,3,2,1,0:T(8,128)S(1)}, f32[3,26,3,40,128]{4,3,2,1,0:T(8,128)S(1)}, f32[3,26,3,...) custom-call(f32[3,16,16,256]{3,2,1,0:T(8,128)S(1)} %get-tuple-elemen, ...), custom_call_target="tpu_custom_call" | custom-call | flops 6000000 | bytes 6000000 | tf_op jit(solution)/shard_map/pallas_call | solution.py:528
  13.8 0.0 collective-permute-done.3.first_ref
  13.8 3.5 %collective-permute-done.4.second_ref = f32[11,24,128]{2,1,0:T(8,128)S(1)} collective-permute-done((f32[11,24,128]{2,1,0:T(8,128)S(1)}, f32[11,24,128]{2,1,0:T(8,128)S(1)}, u32[]{:S(2)}, u32[]{:S(2)}) %collective-permute-start.4) | collective-permute-done | bytes 135200 | tf_op jit(solution)/shard_map/ppermute | solution.py:542
  17.3 1.9 %shard_map.80 = (f32[11,24,128]{2,1,0:T(8,128)S(1)}, f32[11,24,128]{2,1,0:T(8,128)S(1)}, f32[5,24,128]{2,1,0:T(8,128)S(1)}, f32[5,24,128]{2,1,0:T(8,128)S(1)}) custom-call(f32[11,24,128]{2,1,0:T(8,128)S(1)} %collective-permute-done.3.first_ref, f32[11,24,128]{2,1,0:T(8,128)S(1)} %collective-permute-done.4.second_ref), custom_call_target="tpu_custom_call" | custom-call | flops 600000 | bytes 600000 | tf_op jit(solution)/shard_map/pallas_call | solution.py:528
  19.3 0.1 collective-permute-start.5
  19.3 3.1 %collective-permute-start.6 = (f32[5,24,128]{2,1,0:T(8,128)S(1)}, f32[5,24,128]{2,1,0:T(8,128)S(1)}, u32[]{:S(2)}, u32[]{:S(2)}) collective-permute-start(f32[5,24,128]{2,1,0:T(8,128)S(1)} %get-tuple-element.168), channel_id=1, source_target_pairs={{8,16},{16,8},{9,17},{17,9},{10,18},{18,10},{11,19},{19,11},{12,20... | collective-permute-start | bytes 184328 | tf_op jit(solution)/shard_map/ppermute | solution.py:542
  22.4 0.9 %shard_map.81 = (f32[3,26,3,40,128]{4,3,2,1,0:T(8,128)S(1)}, f32[3,26,3,40,128]{4,3,2,1,0:T(8,128)S(1)}, f32[3,26,3,40,128]{4,3,2,1,0:T(8,128)S(1)}, f32[3,26,3,...) custom-call(f32[11,24,128]{2,1,0:T(8,128)S(1)} %get-tuple-element.13, ...), custom_call_target="tpu_custom_call", output_to_operand_aliasing={{0}: (2, {}), {1}: (3, {}), {2}: (4, {}), {3}: (5, {}), {4}... | custom-call | flops 300000 | bytes 300000 | tf_op jit(solution)/shard_map/pallas_call | solution.py:528
  23.3 4.2 %shard_map.82 = (f32[3,26,3,40,128]{4,3,2,1,0:T(8,128)S(1)}, f32[3,26,3,40,128]{4,3,2,1,0:T(8,128)S(1)}, f32[3,26,3,40,128]{4,3,2,1,0:T(8,128)S(1)}, f32[3,26,3,...) custom-call(f32[3,26,3,40,128]{4,3,2,1,0:T(8,128)S(1)} %get-tuple-el, ...), custom_call_target="tpu_custom_call", output_to_operand_aliasing={{0}: (0, {}), {1}: (1, {}), {2}: (2, {}), {3}: (3, {}), {4}... | custom-call | flops 300000 | bytes 300000 | tf_op jit(solution)/shard_map/pallas_call | solution.py:528
  27.6 0.0 collective-permute-done.first_ref
  27.6 0.0 collective-permute-done.1.second_ref
  27.6 0.1 shard_map.83
  27.7 0.0 collective-permute-done.5.corner_first_ref
  27.7 0.0 collective-permute-done.6.corner_second_ref
  27.8 2.1 %collective-permute-start.7 = (f32[448,256]{1,0:T(8,128)S(1)}, f32[448,256]{1,0:T(8,128)S(1)}, u32[]{:S(2)}, u32[]{:S(2)}) collective-permute-start(f32[448,256]{1,0:T(8,128)S(1)} %shard_map.83), channel_id=1, source_target_pairs={{0,1},{1,0},{2,3},{3,2},{4,5},{5,4},{6,7},{7,6},{8,9},{9,8},{10,11... | collective-permute-start | bytes 1376264 | tf_op jit(solution)/shard_map/ppermute | solution.py:542
  29.9 0.5 %shard_map.84 = (f32[3,26,3,40,128]{4,3,2,1,0:T(8,128)S(1)}, f32[3,26,3,40,128]{4,3,2,1,0:T(8,128)S(1)}, f32[3,26,3,40,128]{4,3,2,1,0:T(8,128)S(1)}, f32[3,26,3,...) custom-call(f32[49,16,256]{2,1,0:T(8,128)S(1)} %collective-permute-d, ...), custom_call_target="tpu_custom_call", output_to_operand_aliasing={{0}: (4, {}), {1}: (5, {}), {2}: (6, {}), {3}: (7, {}), {4}... | custom-call | flops 300000 | bytes 300000 | tf_op jit(solution)/shard_map/pallas_call | solution.py:528
  30.4 0.5 %shard_map.85 = (f32[3,26,3,40,128]{4,3,2,1,0:T(8,128)S(1)}, f32[3,26,3,40,128]{4,3,2,1,0:T(8,128)S(1)}, f32[3,26,3,40,128]{4,3,2,1,0:T(8,128)S(1)}, f32[3,26,3,...) custom-call(f32[3,26,3,40,128]{4,3,2,1,0:T(8,128)S(1)} %get-tuple-el, ...), custom_call_target="tpu_custom_call", output_to_operand_aliasing={{0}: (0, {}), {1}: (1, {}), {2}: (2, {}), {3}: (3, {}), {4}... | custom-call | flops 300000 | bytes 300000 | tf_op jit(solution)/shard_map/pallas_call | solution.py:528
  30.9 0.4 %collective-permute-done.7.near_ref = f32[448,256]{1,0:T(8,128)S(1)} collective-permute-done((f32[448,256]{1,0:T(8,128)S(1)}, f32[448,256]{1,0:T(8,128)S(1)}, u32[]{:S(2)}, u32[]{:S(2)}) %collective-permute-start.7) | collective-permute-done | bytes 458784 | tf_op jit(solution)/shard_map/ppermute | solution.py:542
  31.4 5.7 %shard_map.86 = (f32[3,16,16,256]{3,2,1,0:T(8,128)}, f32[3,16,16,256]{3,2,1,0:T(8,128)}, f32[3,26,3,40,128]{4,3,2,1,0:T(8,128)S(1)}, f32[3,26,3,40,128]{4,3,2,1,...) custom-call(f32[448,256]{1,0:T(8,128)S(1)} %collective-permute-done., ...), custom_call_target="tpu_custom_call", output_to_operand_aliasing={{2}: (1, {}), {3}: (2, {}), {4}: (3, {}), {5}: (4, {}), {6}... | custom-call | flops 3000000 | bytes 3000000 | tf_op jit(solution)/shard_map/pallas_call | solution.py:528
Async XLA Ops:
  2.5 5.3 %collective-permute-start.2 = (f32[11,16,8,256]{3,2,1,0:T(8,128)S(1)}, f32[11,16,8,256]{3,2,1,0:T(8,128)S(1)}, u32[]{:S(2)}, u32[]{:S(2)}) collective-permute-start(f32[11,16,8,256]{3,2,1,0:T(8,128)S(1)} %get-tuple-element.114), channel_id=1, source_target_pairs={{0,1},{1,0},{2,3},{3,2},{4,5},{5,4},{6,7},{7,6},{8,9},{9,8},{10,11... | collective-permute-start | bytes 4325384 | tf_op jit(solution)/shard_map/ppermute | solution.py:542
  3.3 24.3 %collective-permute-start = (f32[49,16,256]{2,1,0:T(8,128)S(1)}, f32[49,16,256]{2,1,0:T(8,128)S(1)}, u32[]{:S(2)}, u32[]{:S(2)}) collective-permute-start(f32[49,16,256]{2,1,0:T(8,128)S(1)} %get-tuple-element.107), channel_id=1, source_target_pairs={{0,8},{16,24},{8,0},{24,16},{1,9},{17,25},{9,1},{25,17},{2,10},{18... | collective-permute-start | bytes 2408456 | tf_op jit(solution)/shard_map/ppermute | solution.py:542
  3.5 24.1 %collective-permute-start.1 = (f32[49,16,256]{2,1,0:T(8,128)S(1)}, f32[49,16,256]{2,1,0:T(8,128)S(1)}, u32[]{:S(2)}, u32[]{:S(2)}) collective-permute-start(f32[49,16,256]{2,1,0:T(8,128)S(1)} %get-tuple-element.108), channel_id=1, source_target_pairs={{8,16},{16,8},{9,17},{17,9},{10,18},{18,10},{11,19},{19,11},{12,20... | collective-permute-start | bytes 2408456 | tf_op jit(solution)/shard_map/ppermute | solution.py:542
  9.1 4.7 %collective-permute-start.3 = (f32[11,24,128]{2,1,0:T(8,128)S(1)}, f32[11,24,128]{2,1,0:T(8,128)S(1)}, u32[]{:S(2)}, u32[]{:S(2)}) collective-permute-start(f32[11,24,128]{2,1,0:T(8,128)S(1)} %get-tuple-element.117), channel_id=1, source_target_pairs={{0,2},{4,6},{2,0},{6,4},{1,3},{5,7},{3,1},{7,5},{8,10},{12,14},{10... | collective-permute-start | bytes 405512 | tf_op jit(solution)/shard_map/ppermute | solution.py:542
  10.4 7.0 %collective-permute-start.4 = (f32[11,24,128]{2,1,0:T(8,128)S(1)}, f32[11,24,128]{2,1,0:T(8,128)S(1)}, u32[]{:S(2)}, u32[]{:S(2)}) collective-permute-start(f32[11,24,128]{2,1,0:T(8,128)S(1)} %get-tuple-element.118), channel_id=1, source_target_pairs={{2,4},{4,2},{3,5},{5,3},{10,12},{12,10},{11,13},{13,11},{18,20},{2... | collective-permute-start | bytes 405512 | tf_op jit(solution)/shard_map/ppermute | solution.py:542
  19.3 8.5 %collective-permute-start.5 = (f32[5,24,128]{2,1,0:T(8,128)S(1)}, f32[5,24,128]{2,1,0:T(8,128)S(1)}, u32[]{:S(2)}, u32[]{:S(2)}) collective-permute-start(f32[5,24,128]{2,1,0:T(8,128)S(1)} %get-tuple-element.167), channel_id=1, source_target_pairs={{0,8},{16,24},{8,0},{24,16},{1,9},{17,25},{9,1},{25,17},{2,10},{18... | collective-permute-start | bytes 184328 | tf_op jit(solution)/shard_map/ppermute | solution.py:542
  19.3 8.4 %collective-permute-start.6 = (f32[5,24,128]{2,1,0:T(8,128)S(1)}, f32[5,24,128]{2,1,0:T(8,128)S(1)}, u32[]{:S(2)}, u32[]{:S(2)}) collective-permute-start(f32[5,24,128]{2,1,0:T(8,128)S(1)} %get-tuple-element.168), channel_id=1, source_target_pairs={{8,16},{16,8},{9,17},{17,9},{10,18},{18,10},{11,19},{19,11},{12,20... | collective-permute-start | bytes 184328 | tf_op jit(solution)/shard_map/ppermute | solution.py:542
  27.8 3.6 %collective-permute-start.7 = (f32[448,256]{1,0:T(8,128)S(1)}, f32[448,256]{1,0:T(8,128)S(1)}, u32[]{:S(2)}, u32[]{:S(2)}) collective-permute-start(f32[448,256]{1,0:T(8,128)S(1)} %shard_map.83), channel_id=1, source_target_pairs={{0,1},{1,0},{2,3},{3,2},{4,5},{5,4},{6,7},{7,6},{8,9},{9,8},{10,11... | collective-permute-start | bytes 1376264 | tf_op jit(solution)/shard_map/ppermute | solution.py:542
